TPU v7x, 1024 devices: a whole 4x4x32 slice. The times are simulated.
1024 devices in a mesh: leaf: 4 (over x), row: 8 (over y, core), col: 32 (over z).
Axes of the slice: x: 4, y: 4, z: 32, core: 2. Of those that a mesh axis runs over, the one named last changes fastest.
Arguments:
- child_inv: bfloat16 [4, 4096, 4096], P('leaf', 'col', 'row'), as said below
- child_panel: bfloat16 [4, 2048, 4096], P('leaf', 'row', 'col'), may hold values from -0.09375 to 0.09375
- child_rhs: bfloat16 [4, 4096, 512], P('leaf', 'row'), may hold values from -6 to 6
- anc_tiles: int32 [4, 16], P('leaf', 'row'), may hold values from 0 to 63, as said below
- root_inv: bfloat16 [8192, 8192], P('col', 'row'), as said below
- root_rhs: bfloat16 [8192, 512], P('row'), may hold values from -6 to 6
Outputs:
- child_sol: bfloat16 [4, 4096, 512], P('leaf', ('row', 'col'))
- root_sol: bfloat16 [8192, 512], P(('row', 'col'))
Inputs may be any that keep to these rules, and one draw needn't show every extreme that they name: anc_tiles[k, j] names the root tile that update tile j of child k belongs to; it lies in block row j // 2 of the root, that is among the root tiles (j // 2) * 8 to (j // 2) * 8 + 7, and the entries of one child are distinct. child_inv[k] is lower triangular with a diagonal between 0.5 and 1.5. root_inv is lower triangular with a diagonal between 0.5 and 1.5.
All inputs are finite; a program needn't handle non-finite values.
Results may differ from a plain program's by a relative error of at most 0.035.
Values may be sent and summed in bfloat16 or wider, within the bound.
No kernel may reach another device: no remote copies, remote signals or barrier semaphores. Data moves between devices by JAX's collectives and lax.ppermute only.
A program may use at most 32 MiB of HBM per device.

v0:
```python
import jax
import jax.numpy as jnp
from jax import lax
from jax.sharding import PartitionSpec as P


def row_total(partial_term):
    return lax.psum(partial_term.astype(jnp.bfloat16), "row").astype(jnp.float32)


def column_share(matrix, vector):
    return lax.psum_scatter(
        lax.dot_general(
            matrix, vector, (((0,), (0,)), ((), ())), preferred_element_type=jnp.float32
        ).astype(jnp.bfloat16),
        "col",
        scatter_dimension=0,
        tiled=True,
    ).astype(jnp.float32)


def body(child_inv, child_panel, child_rhs, anc_tiles, root_inv, root_rhs):
    inv_local = child_inv[0]
    panel_rows = child_panel[0]
    right_side = child_rhs[0]
    ancestor = anc_tiles[0]
    slot_rows = panel_rows.shape[0]
    slot_tiles = ancestor.shape[0]
    tile_rows = slot_rows // slot_tiles
    columns = right_side.shape[1]
    root_rows = root_rhs.shape[0]
    blocks = root_rows // tile_rows
    local_tiles = ancestor - lax.axis_index("row") * blocks
    selector = (local_tiles[None, :] == jnp.arange(blocks, dtype=jnp.int32)[:, None]).astype(
        jnp.float32
    )
    forward = row_total(jnp.dot(inv_local, right_side, preferred_element_type=jnp.float32)).astype(
        jnp.bfloat16
    )
    update = jnp.dot(panel_rows, forward, preferred_element_type=jnp.float32)
    shaped = update.reshape(slot_tiles, tile_rows, columns)
    placed = jnp.einsum("tu,uqn->tqn", selector, shaped, precision=lax.Precision.HIGHEST)
    landed = lax.psum(placed.reshape(root_rows, columns), ("leaf", "col"))
    root_side = (root_rhs.astype(jnp.float32) - landed).astype(jnp.bfloat16)
    root_forward = row_total(
        jnp.dot(root_inv, root_side, preferred_element_type=jnp.float32)
    ).astype(jnp.bfloat16)
    root_sol = column_share(root_inv, root_forward).astype(jnp.bfloat16)
    root_block = lax.all_gather(root_sol, "col", axis=0, tiled=True)
    picked = (
        jnp.einsum(
            "tu,tqn->uqn",
            selector.astype(jnp.bfloat16),
            root_block.reshape(blocks, tile_rows, columns),
            preferred_element_type=jnp.float32,
        )
        .astype(jnp.bfloat16)
        .reshape(slot_rows, columns)
    )
    correction_part = lax.dot_general(
        panel_rows, picked, (((0,), (0,)), ((), ())), preferred_element_type=jnp.float32
    )
    correction = row_total(correction_part).astype(jnp.bfloat16)
    residue = (forward.astype(jnp.float32) - correction.astype(jnp.float32)).astype(jnp.bfloat16)
    child_sol = column_share(inv_local, residue).astype(jnp.bfloat16)
    return (child_sol[None], root_sol)


def solution(mesh):
    in_specs = (
        P("leaf", "col", "row"),
        P("leaf", "row", "col"),
        P("leaf", "row", None),
        P("leaf", "row"),
        P("col", "row"),
        P("row", None),
    )
    out_specs = (P("leaf", ("row", "col"), None), P(("row", "col"), None))
    return jax.shard_map(body, mesh=mesh, in_specs=in_specs, out_specs=out_specs, check_vma=False)
```

profile of v0, /device:TPU:1, one launch (start us, length us, event | category | flops | bytes accessed | tf_op | source)
XLA Modules:
  0.0 1209.6 jit_solution(326246553575548778)
XLA Ops:
  7.2 2.0 convolution_convert_fusion.4
  9.3 0.0 all-reduce.7.cloned.1.call-start
  9.3 0.7 subtract_bitcast_fusion
  10.0 104.1 %all-reduce.5.cloned.1.call-done = bf16[128,512]{1,0:T(8,128)(2,1)} async-done(((bf16[128,512]{1,0:T(8,128)(2,1)}), bf16[128,512]{1,0:T(8,128)(2,1)}) %all-reduce.5.cloned.1.call-update) | async-done | bytes 131088 | tf_op jit(solution)/shard_map/psum | solution.py:8
  114.1 1.1 fusion.11
  115.2 1.6 fusion.6
  116.8 2.5 copy.26
  119.4 497.9 %all-reduce.7.cloned.1.call-done = f32[1024,512]{1,0:T(8,128)} async-done(((f32[1024,512]{1,0:T(8,128)}), f32[1024,512]{1,0:T(8,128)}) %all-reduce.7.cloned.1.call-update) | async-done | bytes 2097168 | tf_op jit(solution)/shard_map/psum | solution.py:43
  617.3 2.9 fusion.2
  620.2 0.0 reduce-scatter.7.cloned.1.call-start
  620.2 105.8 %all-reduce.9.cloned.1.call-done = bf16[256,512]{0,1:T(8,128)(2,1)} async-done(((bf16[256,512]{0,1:T(8,128)(2,1)}), bf16[256,512]{0,1:T(8,128)(2,1)}) %all-reduce.9.cloned.1.call-update) | async-done | bytes 262160 | tf_op jit(solution)/shard_map/psum | solution.py:8
  726.0 1.4 fusion
  727.5 1.3 copy.34
  728.9 111.6 %reduce-scatter.7.cloned.1.call-done = bf16[32,512]{1,0:T(8,128)(2,1)} async-done(((bf16[1024,512]{1,0:T(8,128)(2,1)}), bf16[32,512]{1,0:T(8,128)(2,1)}) %reduce-scatter.7.cloned.1.call-update) | async-done | bytes 32784 | tf_op jit(solution)/shard_map/reduce_scatter | solution.py:12
  840.5 137.8 %all-gather.2.cloned.1.call-done = bf16[1024,512]{1,0:T(8,128)(2,1)} async-done(((bf16[32,512]{1,0:T(8,128)(2,1)}), bf16[1024,512]{1,0:T(8,128)(2,1)}) %all-gather.2.cloned.1.call-update) | async-done | bytes 1048592 | tf_op jit(solution)/shard_map/all_gather | solution.py:49
  978.3 2.0 convolution_convert_fusion.2
  980.4 0.9 fusion.3
  981.3 0.0 reduce-scatter.9.cloned.1.call-start
  981.4 107.5 %all-reduce.11.cloned.1.call-done = bf16[128,512]{1,0:T(8,128)(2,1)} async-done(((bf16[128,512]{1,0:T(8,128)(2,1)}), bf16[128,512]{1,0:T(8,128)(2,1)}) %all-reduce.11.cloned.1.call-update) | async-done | bytes 131088 | tf_op jit(solution)/shard_map/psum | solution.py:8
  1088.8 1.2 fusion.1
  1090.1 1.0 copy.36
  1091.1 110.1 %reduce-scatter.9.cloned.1.call-done = bf16[16,512]{1,0:T(8,128)(2,1)} async-done(((bf16[512,512]{1,0:T(8,128)(2,1)}), bf16[16,512]{1,0:T(8,128)(2,1)}) %reduce-scatter.9.cloned.1.call-update) | async-done | bytes 16400
  1201.2 0.8 copy.37
  1202.0 0.7 copy.31
  (22 shorter events, 0.3 us)
Async XLA Ops:
  7.2 610.1 %copy-start = (bf16[256,1024]{1,0:T(8,128)(2,1)S(1)}, bf16[256,1024]{1,0:T(8,128)(2,1)}, u32[]{:S(2)}) copy-start(bf16[256,1024]{1,0:T(8,128)(2,1)} %param.10) | copy-start | bytes 1572868
  7.2 106.9 %all-reduce.5.cloned.1.call-start = ((), (), s32[]{:S(2)}) async-start(), calls=%async_computation.2 | async-start | bytes 262144 | tf_op jit(solution)/shard_map/psum | solution.py:8
  9.3 608.0 %all-reduce.7.cloned.1.call-start = ((), (), s32[]{:S(2)}) async-start(), calls=%async_computation.3 | async-start | bytes 4194304 | tf_op jit(solution)/shard_map/psum | solution.py:43
  119.3 498.0 %copy-start.1 = (bf16[1024,512]{1,0:T(8,128)(2,1)S(1)}, bf16[1024,512]{1,0:T(8,128)(2,1)}, u32[]{:S(2)}) copy-start(bf16[1024,512]{1,0:T(8,128)(2,1)} %param.11) | copy-start | bytes 3145732
  119.3 606.7 %all-reduce.9.cloned.1.call-start = ((), (), s32[]{:S(2)}) async-start(), calls=%async_computation.4 | async-start | bytes 524288 | tf_op jit(solution)/shard_map/psum | solution.py:8
  620.2 220.3 %reduce-scatter.7.cloned.1.call-start = ((), (), s32[]{:S(2)}) async-start(), calls=%async_computation.7 | async-start | bytes 1081344 | tf_op jit(solution)/shard_map/reduce_scatter | solution.py:12
  727.4 252.9 %copy-start.4 = (bf16[1,256,128]{2,1,0:T(8,128)(2,1)S(1)}, bf16[1,256,128]{2,1,0:T(8,128)(2,1)}, u32[]{:S(2)}) copy-start(bf16[1,256,128]{2,1,0:T(8,128)(2,1)} %param.7) | copy-start | bytes 196612
  728.8 360.0 %copy-start.2 = (bf16[1,128,512]{2,1,0:T(8,128)(2,1)S(1)}, bf16[1,128,512]{2,1,0:T(8,128)(2,1)}, u32[]{:S(2)}) copy-start(bf16[1,128,512]{2,1,0:T(8,128)(2,1)} %param.6) | copy-start | bytes 393220
  728.8 360.0 %copy-start.3 = (bf16[128,512]{1,0:T(8,128)(2,1)S(1)}, bf16[128,512]{1,0:T(8,128)(2,1)}, u32[]{:S(2)}) copy-start(bf16[128,512]{1,0:T(8,128)(2,1)} %all-reduce.5.cloned.1.call-done) | copy-start | bytes 393220
  728.8 249.5 %all-gather.2.cloned.1.call-start = ((), (), s32[]{:S(2)}) async-start(), calls=%async_computation.5 | async-start | bytes 1081344 | tf_op jit(solution)/shard_map/all_gather | solution.py:49
  840.5 248.3 %all-reduce.11.cloned.1.call-start = ((), (), s32[]{:S(2)}) async-start(), calls=%async_computation.6 | async-start | bytes 262144 | tf_op jit(solution)/shard_map/psum | solution.py:8
  981.3 219.9 %reduce-scatter.9.cloned.1.call-start = ((), (), s32[]{:S(2)}) async-start(), calls=%async_computation.8 | async-start | bytes 540672
Sparse Core Ops, SparseCore 0:
  10.3 103.6 all-reduce.4
  119.4 497.7 all-reduce.6
  620.3 105.6 all-reduce.8
  729.8 110.5 reduce-scatter.6
  843.9 134.3 all-gather.1
  981.4 107.3 all-reduce.10
  1092.2 108.9 reduce-scatter.8
where the time goes:
time: 1230 us; the launch traced here: 1210 us
  waiting for transfers between devices  1170 us (95%)
  between operations  14.2 us (1%)
  matrix products  13.1 us (1%)
    psum x1, waiting for transfers between devices, body(): landed = lax.psum(placed.reshape(root_rows, columns), ('leaf', 'col'))  498 us
    psum x3, waiting for transfers between devices, row_total(): lax.psum(partial_term.astype(jnp.bfloat16), 'row').astype(jnp.float32)  317 us
    all_gather x1, waiting for transfers between devices, body(): root_block = lax.all_gather(root_sol, 'col', axis=0, tiled=True)  138 us
    reduce_scatter x1, waiting for transfers between devices, column_share(): lax.psum_scatter(lax.dot_general(matrix, vector, (((0,), (0,)), ((), ()))...  112 us
    unnamed x8, waiting for transfers between devices  110 us
  transfers between devices with their start and end apart: 7, of which 7 were waited for; matrix products, arithmetic and copies ran while one was open for 0% of the time, Pallas kernels for 0%

commit v1 on v0

v1 whole, which is shorter than its diff:
```python
import jax
import jax.numpy as jnp
from jax import lax
from jax.experimental import pallas as pl
from jax.experimental.pallas import tpu as pltpu
from jax.sharding import Mesh, PartitionSpec as P

BF = jnp.bfloat16
F32 = jnp.float32
TILE = 128
LEAF, Y, CORE, ZHI, ZLO = 4, 4, 2, 8, 4
Z = ("zhi", "zlo")


def exchange(x, axis):
    return lax.all_to_all(x, axis, 0, 0, tiled=True)


def share(x, axis, n):
    return exchange(jnp.broadcast_to(x[None], (n,) + x.shape), axis)


def total(parts):
    return jnp.sum(parts.astype(F32), axis=0)


def dot(a, b, contract):
    return lax.dot_general(a, b, (contract, ((), ())), preferred_element_type=F32)


def place_kernel(slot_ref, upd_ref, rhs_own, rhs_oth, root_own, root_oth, out_ref, side_ref):
    half = rhs_own.shape[1]
    side_ref[:, :half] = rhs_own[...].astype(F32)
    side_ref[:, half:] = rhs_oth[...].astype(F32)
    width = side_ref.shape[0]
    for k in range(LEAF):
        for u in range(4):
            at = pl.ds(pl.multiple_of(slot_ref[k * 4 + u] * TILE, TILE), TILE)
            side_ref[:, at] = side_ref[:, at] - upd_ref[k, :width, u * TILE:(u + 1) * TILE].astype(F32)
    out = dot(side_ref[:, :half].astype(BF), root_own[...], ((1,), (1,)))
    out = out + dot(side_ref[:, half:].astype(BF), root_oth[...], ((1,), (1,)))
    out_ref[...] = out.astype(BF)


def pick_kernel(slot_ref, parts_ref, sol_ref, pick_ref, sum_ref):
    acc = parts_ref[0].astype(F32)
    for k in range(1, LEAF):
        acc = acc + parts_ref[k].astype(F32)
    sum_ref[...] = acc
    sol_ref[...] = acc.astype(BF)
    for u in range(4):
        at = pl.ds(pl.multiple_of(slot_ref[u] * TILE, TILE), TILE)
        pick_ref[:, u * TILE:(u + 1) * TILE] = sum_ref[:, at].astype(BF)


def call(kernel, out_shape, scratch, n_in):
    return pl.pallas_call(
        kernel,
        out_shape=out_shape,
        in_specs=[pl.BlockSpec(memory_space=pltpu.SMEM)]
        + [pl.BlockSpec(memory_space=pltpu.VMEM)] * n_in,
        out_specs=jax.tree.map(lambda _: pl.BlockSpec(memory_space=pltpu.VMEM), out_shape),
        scratch_shapes=scratch,
        compiler_params=pltpu.CompilerParams(vmem_limit_bytes=32 * 1024 * 1024),
    )


def body(child_inv, child_panel, child_rhs, anc_tiles, root_inv, root_rhs):
    inv, panel, rhs, anc = child_inv[0], child_panel[0], child_rhs[0], anc_tiles[0]
    y, core, zlo = lax.axis_index("y"), lax.axis_index("core"), lax.axis_index("zlo")
    rows = root_rhs.shape[0]
    width = rhs.shape[1] // (CORE * ZLO)

    swap = [(s * ZLO + t, t * ZLO + s) for s in range(LEAF) for t in range(ZLO)]
    root_own = lax.ppermute(root_inv, ("leaf", "zlo"), swap)
    n = inv.shape[0]
    packed = jnp.concatenate([inv[:, i:i + n] for i in range(0, inv.shape[1], n)] + [panel], axis=0)
    packed = lax.all_gather(packed, ("core", "zlo"), axis=0, tiled=False)

    part = dot(rhs, inv, ((0,), (1,))).astype(BF)
    part = total(exchange(part.reshape(CORE, -1, part.shape[1]), "core")).astype(BF)
    forward = total(share(part, "y", Y)).astype(BF)

    panel_y = lax.all_gather(panel, "core", axis=0, tiled=True)
    anc_y = lax.all_gather(anc, "core", axis=0, tiled=True)

    chunk = lax.dynamic_slice_in_dim(
        root_rhs.reshape(rows, CORE, ZLO, width), zlo, 1, axis=2
    )[:, :, 0]
    chunk = jnp.transpose(chunk, (1, 2, 0))
    side_own = lax.dynamic_index_in_dim(chunk, core, 0, keepdims=False)
    side_oth = lax.ppermute(
        lax.dynamic_index_in_dim(chunk, 1 - core, 0, keepdims=False), "core", [(0, 1), (1, 0)]
    )

    update = dot(forward, panel_y, ((1,), (1,))).astype(BF)
    both = jnp.concatenate([update, forward], axis=1).reshape(ZLO, width, -1)
    both = exchange(both, "zlo")
    forward_all = jnp.transpose(both[:, :, update.shape[1]:], (1, 0, 2)).reshape(width, -1)
    update = total(both[:, :, :update.shape[1]]).astype(BF)
    root_own, side_oth, update = lax.optimization_barrier((root_own, side_oth, update))
    update = total(exchange(update.reshape(ZHI, width // ZHI, -1), "zhi")).astype(BF)
    root_oth = lax.ppermute(root_own, "core", [(0, 1), (1, 0)])
    update = share(update, "zhi", ZHI).reshape(width, -1)
    names = jnp.zeros((8, update.shape[1]), BF).at[:, :4].set(anc_y.astype(BF)[None])
    root_oth, update = lax.optimization_barrier((root_oth, update))
    update = share(jnp.concatenate([update, names], axis=0), "leaf", LEAF)
    slots = update[:, width, :4].reshape(-1).astype(jnp.int32)

    def local(t):
        return lax.rem(t - y * 16 + core * 8, 16)

    root_part = call(
        place_kernel,
        jax.ShapeDtypeStruct((width, root_inv.shape[0]), BF),
        [pltpu.VMEM((width, 2 * rows), F32)],
        5,
    )(local(slots), update, side_own, side_oth, root_own, root_oth)
    packed, root_part = lax.optimization_barrier((packed, root_part))
    inv_all = packed[:, :inv.size // n].reshape(CORE, ZLO, -1, n, n)
    inv_all = jnp.transpose(inv_all, (0, 1, 3, 2, 4))
    panel_all = packed[:, inv.size // n:].reshape(CORE, ZLO, -1, n)
    panel_all = jnp.transpose(panel_all, (1, 0, 2, 3)).reshape(ZLO, -1, n)
    root_forward = total(share(root_part, "y", Y)).astype(BF)
    sol = jnp.concatenate(
        [dot(root_forward, root_own, ((1,), (0,))), dot(root_forward, root_oth, ((1,), (0,)))], axis=1
    ).astype(BF)
    sol = total(exchange(sol.reshape(ZHI, width // ZHI, -1), "zhi")).astype(BF)
    sol = share(sol, "leaf", LEAF)
    root_sol, picked = call(
        pick_kernel,
        (
            jax.ShapeDtypeStruct((width // ZHI, 2 * rows), BF),
            jax.ShapeDtypeStruct((width // ZHI, 4 * TILE), BF),
        ),
        [pltpu.VMEM((width // ZHI, 2 * rows), F32)],
        1,
    )(local(anc_y), sol)
    picked = share(picked, "zhi", ZHI).reshape(width, -1)

    correction = jnp.concatenate(
        [dot(picked, panel_all[z], ((1,), (0,))) for z in range(ZLO)], axis=1
    ).astype(BF)
    correction = total(share(correction, "y", Y)).astype(BF)
    residue = (forward_all.astype(F32) - correction.astype(F32)).astype(BF)
    inv_all = inv_all.reshape(CORE, -1, inv.shape[1])
    child = jnp.stack([dot(inv_all[c], residue, ((0,), (1,))) for c in range(CORE)]).astype(BF)

    cols = ZHI * ZLO
    child = jnp.transpose(child.reshape(CORE, cols, -1, width), (1, 0, 2, 3)).reshape(cols, -1)
    n_child = child.shape[1]
    own, oth = root_sol[:, :rows], root_sol[:, rows:]
    root = jnp.stack([jnp.where(core == 0, own, oth), jnp.where(core == 0, oth, own)])
    few = width // ZHI
    root = jnp.transpose(root.reshape(CORE, few, cols, -1), (2, 0, 1, 3)).reshape(cols, -1)
    out = exchange(jnp.concatenate([child, root], axis=1).reshape(cols, -1, TILE), Z)
    out = out.reshape(ZHI, ZLO, -1)
    child = total(out[:, :, :n_child]).astype(BF)
    child = jnp.transpose(child.reshape(ZLO, CORE, -1), (1, 0, 2)).reshape(CORE, -1)
    n_child = child.shape[1]
    root = out[:, :, CORE * n_child // ZLO:]
    root = jnp.transpose(root.reshape(ZHI, ZLO, CORE, -1), (2, 1, 0, 3)).reshape(CORE, -1)
    out = exchange(jnp.concatenate([child, root], axis=1).reshape(CORE, -1, TILE), "core")
    out = out.reshape(CORE, -1)
    child = out[:, :n_child].reshape(CORE, ZLO, -1, width)
    child = jnp.transpose(child, (2, 0, 1, 3)).reshape(child.shape[2], -1)
    root = out[:, n_child:].reshape(CORE * ZLO * ZHI * few, -1)
    return child[None], jnp.transpose(root)


def solution(mesh):
    split = Mesh(
        mesh.devices.reshape(LEAF, Y, CORE, ZHI, ZLO), ("leaf", "y", "core", "zhi", "zlo")
    )
    row, col = ("y", "core"), ("zhi", "zlo")
    in_specs = (
        P("leaf", col, row),
        P("leaf", row, col),
        P("leaf", row, None),
        P("leaf", row),
        P(col, row),
        P(row, None),
    )
    out_specs = (P("leaf", row + col, None), P(row + col, None))
    return jax.shard_map(body, mesh=split, in_specs=in_specs, out_specs=out_specs, check_vma=False)
```

time: 1230 us -> 345 us (0.28); the launches traced: 1210 us -> 343 us
  waiting for transfers between devices: 1170 us -> 89.7 us
  starting transfers between devices: 0.29 us -> 134 us
  blocking collectives: 0 us -> 80.6 us
    psum x4 -> x0, waiting for transfers between devices: 815 us -> none  [the longest x1 498 us: body(): landed = lax.psum(placed.reshape(root_rows, columns), ('leaf', 'col'))]
    all_gather x1, waiting for transfers between devices: 138 us -> 0.02 us  [body(): packed = lax.all_gather(packed, ('core', 'zlo'), axis=0, tiled=False)]
    all_to_all x0 -> x9, starting transfers between devices: none -> 112 us  [exchange(): return lax.all_to_all(x, axis, 0, 0, tiled=True)]
    reduce_scatter x1 -> x0, waiting for transfers between devices: 112 us -> none  [column_share(): lax.psum_scatter(lax.dot_general(matrix, vector, (((0,), (0,)), ((), ()))...]
    unnamed x8 -> x1, waiting for transfers between devices: 110 us -> 0.02 us
    all_to_all x0 -> x9, waiting for transfers between devices: none -> 89.6 us  [exchange(): return lax.all_to_all(x, axis, 0, 0, tiled=True)]
    all_to_all x0 -> x4, blocking collectives: none -> 74 us  [exchange(): return lax.all_to_all(x, axis, 0, 0, tiled=True)]
    ppermute x0 -> x3, starting transfers between devices: none -> 21.5 us  [the longest x1 17.4 us: body(): root_oth = lax.ppermute(root_own, 'core', [(0, 1), (1, 0)])]
  transfers between devices with their start and end apart: 7 -> 13, of which waited for: 7 -> 9; matrix products, arithmetic and copies ran while one was open for 0% -> 3% of each run, Pallas kernels for 0% -> 0%
where the time goes in v1:
time: 345 us; the launch traced here: 343 us
  starting transfers between devices  134 us (39%)
  waiting for transfers between devices  89.7 us (26%)
  blocking collectives  80.6 us (23%)
  local copies, waits for them, and re-layouts  15.3 us (4%)
  between operations  15.2 us (4%)
  other arithmetic  3.99 us (1%)
    all_to_all x9, starting transfers between devices, exchange(): return lax.all_to_all(x, axis, 0, 0, tiled=True)  112 us
    all_to_all x9, waiting for transfers between devices, exchange(): return lax.all_to_all(x, axis, 0, 0, tiled=True)  89.6 us
    all_to_all x4, blocking collectives, exchange(): return lax.all_to_all(x, axis, 0, 0, tiled=True)  74 us
    ppermute x1, starting transfers between devices, body(): root_oth = lax.ppermute(root_own, 'core', [(0, 1), (1, 0)])  17.4 us
  transfers between devices with their start and end apart: 13, of which 9 were waited for; matrix products, arithmetic and copies ran while one was open for 3% of the time, Pallas kernels for 0%

profile of v1, /device:TPU:1, one launch (start us, length us, event | category | flops | bytes accessed | tf_op | source)
XLA Modules:
  0.0 343.2 jit_solution(15003298913832144427)
XLA Ops:
  9.5 17.6 %all_to_all.65 = bf16[2,256,128]{2,1,0:T(8,128)(2,1)S(1)} all-to-all(bf16[2,256,128]{2,1,0:T(8,128)(2,1)S(1)} %bitcast.145), channel_id=1, replica_groups=mesh['leaf'=4,'y'=4,'core'=2,'zhi'=8,'zlo'=4] {'core'}, dimensions={0} | all-to-all | bytes 262144 | tf_op jit(solution)/shard_map/all_to_all | solution.py:16
  27.9 3.4 all-to-all-start.1
  33.3 4.1 %all-to-all-done.1 = bf16[4,256,128]{2,1,0:T(8,128)(2,1)S(1)} async-done(((bf16[4,256,128]{2,1,0:T(8,128)(2,1)}), bf16[4,256,128]{2,1,0:T(8,128)(2,1)S(1)}, u32[]{:S(2)}, u32[]{:S(2)}) %all-to-all-start.1) | async-done | bytes 262176 | tf_op jit(solution)/shard_map/all_to_all | solution.py:16
  38.4 3.5 %all-to-all-start.2 = ((bf16[4,64,640]{2,1,0:T(8,128)(2,1)}), bf16[4,64,640]{2,1,0:T(8,128)(2,1)S(1)}, u32[]{:S(2)}, u32[]{:S(2)}) async-start(bf16[4,64,640]{2,1,0:T(8,128)(2,1)} %bitcast.10), calls=%async_computation.2 | async-start | bytes 655360 | tf_op jit(solution)/shard_map/all_to_all | solution.py:16
  45.0 3.4 collective-permute-start.1
  48.4 2.8 all-to-all-done.2
  51.8 14.8 %all-to-all-start.3 = ((bf16[8,8,512]{2,1,0:T(8,128)(2,1)}), bf16[8,8,512]{2,1,0:T(8,128)(2,1)S(1)}, u32[]{:S(2)}, u32[]{:S(2)}) async-start(bf16[8,8,512]{2,1,0:T(8,128)(2,1)} %bitcast.11), calls=%async_computation.3 | async-start | bytes 131072 | tf_op jit(solution)/shard_map/all_to_all | solution.py:16
  66.7 17.4 %collective-permute-start.2 = (bf16[256,1024]{1,0:T(8,128)(2,1)S(1)}, bf16[256,1024]{1,0:T(8,128)(2,1)S(1)}, u32[]{:S(2)}, u32[]{:S(2)}) collective-permute-start(bf16[256,1024]{1,0:T(8,128)(2,1)S(1)} %collective-permute-done.root_own), channel_id=1, source_target_pairs={{0,32},{32,0},{1,33},{33,1},{2,34},{34,2},{3,35},{35,3},{4,36},{36... | collective-permute-start | bytes 1572872 | tf_op jit(solution)/shard_map/ppermute | solution.py:103
  84.1 4.3 %all-to-all-done.3 = bf16[8,8,512]{2,1,0:T(8,128)(2,1)S(1)} async-done(((bf16[8,8,512]{2,1,0:T(8,128)(2,1)}), bf16[8,8,512]{2,1,0:T(8,128)(2,1)S(1)}, u32[]{:S(2)}, u32[]{:S(2)}) %all-to-all-start.3) | async-done | bytes 65568 | tf_op jit(solution)/shard_map/all_to_all | solution.py:16
  89.0 17.1 %all-to-all-start.4 = ((bf16[8,8,512]{2,1,0:T(8,128)(2,1)}), bf16[8,8,512]{2,1,0:T(8,128)(2,1)S(1)}, u32[]{:S(2)}, u32[]{:S(2)}) async-start(bf16[8,8,512]{2,1,0:T(8,128)(2,1)} %broadcast_in_dim.15), calls=%async_computation.4 | async-start | bytes 131072 | tf_op jit(solution)/shard_map/all_to_all | solution.py:16
  108.1 4.6 %all-reduce.1 = s32[4]{0:T(128)S(1)} all-reduce(s32[4]{0:T(128)S(1)} %bitcast_dynamic-update-slice_fusion.1), channel_id=4, replica_groups=mesh['leaf'=4,'y'=4,'core'=2,'zhi'=8,'zlo'=4] {'core'}, use_global_device_ids=true, to_apply=%add.1 | all-reduce | flops 4 | bytes 32
  114.0 15.2 %all-to-all-done.4 = bf16[8,8,512]{2,1,0:T(8,128)(2,1)S(1)} async-done(((bf16[8,8,512]{2,1,0:T(8,128)(2,1)}), bf16[8,8,512]{2,1,0:T(8,128)(2,1)S(1)}, u32[]{:S(2)}, u32[]{:S(2)}) %all-to-all-start.4) | async-done | bytes 65568 | tf_op jit(solution)/shard_map/all_to_all | solution.py:16
  129.9 45.7 %all-to-all-start.5 = ((bf16[4,72,512]{2,1,0:T(8,128)(2,1)}), bf16[4,72,512]{2,1,0:T(8,128)(2,1)S(1)}, u32[]{:S(2)}, u32[]{:S(2)}) async-start(bf16[4,72,512]{2,1,0:T(8,128)(2,1)} %broadcast_in_dim.16), calls=%async_computation.5 | async-start | bytes 589824 | tf_op jit(solution)/shard_map/all_to_all | solution.py:16
  175.7 5.7 %all-to-all-done.5.upd_ref = bf16[4,72,512]{2,1,0:T(8,128)(2,1)S(1)} async-done(((bf16[4,72,512]{2,1,0:T(8,128)(2,1)}), bf16[4,72,512]{2,1,0:T(8,128)(2,1)S(1)}, u32[]{:S(2)}, u32[]{:S(2)}) %all-to-all-start.5) | async-done | bytes 294944 | tf_op jit(solution)/shard_map/all_to_all | solution.py:16
  182.6 7.2 %all_to_all.66 = bf16[4,64,256]{2,1,0:T(8,128)(2,1)S(1)} all-to-all(bf16[4,64,256]{2,1,0:T(8,128)(2,1)S(1)} %broadcast_in_dim.17), channel_id=1, replica_groups=mesh['leaf'=4,'y'=4,'core'=2,'zhi'=8,'zlo'=4] {'y'}, dimensions={0} | all-to-all | bytes 262144 | tf_op jit(solution)/shard_map/all_to_all | solution.py:16
  191.0 7.7 %all-to-all-start.7 = ((bf16[8,8,2048]{2,1,0:T(8,128)(2,1)}), bf16[8,8,2048]{2,1,0:T(8,128)(2,1)S(1)}, u32[]{:S(2)}, u32[]{:S(2)}) async-start(bf16[8,8,2048]{2,1,0:T(8,128)(2,1)} %pad_maximum_fusion.1), calls=%async_computation.7 | async-start | bytes 524288 | tf_op jit(solution)/shard_map/all_to_all | solution.py:16
  198.7 29.8 %all-to-all-done.7 = bf16[8,8,2048]{2,1,0:T(8,128)(2,1)S(1)} async-done(((bf16[8,8,2048]{2,1,0:T(8,128)(2,1)}), bf16[8,8,2048]{2,1,0:T(8,128)(2,1)S(1)}, u32[]{:S(2)}, u32[]{:S(2)}) %all-to-all-start.7) | async-done | bytes 262176 | tf_op jit(solution)/shard_map/all_to_all | solution.py:16
  229.2 5.7 %all-to-all-start.8 = ((bf16[4,8,2048]{2,1,0:T(8,128)(2,1)}), bf16[4,8,2048]{2,1,0:T(8,128)(2,1)S(1)}, u32[]{:S(2)}, u32[]{:S(2)}) async-start(bf16[4,8,2048]{2,1,0:T(8,128)(2,1)} %broadcast_in_dim.18), calls=%async_computation.8 | async-start | bytes 262144 | tf_op jit(solution)/shard_map/all_to_all | solution.py:16
  240.9 10.9 %all-to-all-start.9 = ((bf16[8,8,512]{2,1,0:T(8,128)(2,1)}), bf16[8,8,512]{2,1,0:T(8,128)(2,1)S(1)}, u32[]{:S(2)}, u32[]{:S(2)}) async-start(bf16[8,8,512]{2,1,0:T(8,128)(2,1)} %broadcast_in_dim.19), calls=%async_computation.9 | async-start | bytes 131072 | tf_op jit(solution)/shard_map/all_to_all | solution.py:16
  252.4 21.1 %all-to-all-done.9 = bf16[8,8,512]{2,1,0:T(8,128)(2,1)S(1)} async-done(((bf16[8,8,512]{2,1,0:T(8,128)(2,1)}), bf16[8,8,512]{2,1,0:T(8,128)(2,1)S(1)}, u32[]{:S(2)}, u32[]{:S(2)}) %all-to-all-start.9) | async-done | bytes 65568 | tf_op jit(solution)/shard_map/all_to_all | solution.py:16
  274.9 3.4 all-to-all-start.10
  278.8 5.0 %all-to-all-done.10 = bf16[4,64,512]{2,1,0:T(8,128)(2,1)S(1)} async-done(((bf16[4,64,512]{2,1,0:T(8,128)(2,1)}), bf16[4,64,512]{2,1,0:T(8,128)(2,1)S(1)}, u32[]{:S(2)}, u32[]{:S(2)}) %all-to-all-start.10) | async-done | bytes 262176 | tf_op jit(solution)/shard_map/all_to_all | solution.py:16
  285.1 39.9 %all_to_all.67 = bf16[32,20,128]{2,1,0:T(8,128)(2,1)S(1)} all-to-all(bf16[32,20,128]{2,1,0:T(8,128)(2,1)S(1)} %reshape.199), channel_id=1, replica_groups=mesh['leaf'=4,'y'=4,'core'=2,'zhi'=8,'zlo'=4] {'zhi','zlo'}, dimensions={0} | all-to-all | bytes 327680 | tf_op jit(solution)/shard_map/all_to_all | solution.py:16
  325.4 9.2 %all_to_all.68 = bf16[2,96,128]{2,1,0:T(8,128)(2,1)S(1)} all-to-all(bf16[2,96,128]{2,1,0:T(8,128)(2,1)S(1)} %bitcast.153), channel_id=1, replica_groups=mesh['leaf'=4,'y'=4,'core'=2,'zhi'=8,'zlo'=4] {'core'}, dimensions={0} | all-to-all | bytes 98304 | tf_op jit(solution)/shard_map/all_to_all | solution.py:16
  (109 shorter events, 28.5 us)
Async XLA Ops:
  7.2 1.0 copy-start
  7.2 24.1 %copy-start.3 = (bf16[1,256,128]{2,1,0:T(8,128)(2,1)S(1)}, bf16[1,256,128]{2,1,0:T(8,128)(2,1)}, u32[]{:S(2)}) copy-start(bf16[1,256,128]{2,1,0:T(8,128)(2,1)} %param.9) | copy-start | bytes 196612
  27.1 14.8 %copy-start.1 = (bf16[1,128,512]{2,1,0:T(8,128)(2,1)S(1)}, bf16[1,128,512]{2,1,0:T(8,128)(2,1)}, u32[]{:S(2)}) copy-start(bf16[1,128,512]{2,1,0:T(8,128)(2,1)} %param.8) | copy-start | bytes 393220
  27.9 9.5 %all-to-all-start.1 = ((bf16[4,256,128]{2,1,0:T(8,128)(2,1)}), bf16[4,256,128]{2,1,0:T(8,128)(2,1)S(1)}, u32[]{:S(2)}, u32[]{:S(2)}) async-start(bf16[4,256,128]{2,1,0:T(8,128)(2,1)} %broadcast_in_dim.14), calls=%async_computation.1 | async-start | bytes 524288 | tf_op jit(solution)/shard_map/all_to_all | solution.py:16
  31.3 11.4 %copy-start.4 = (bf16[256,1024]{1,0:T(8,128)(2,1)S(1)}, bf16[256,1024]{1,0:T(8,128)(2,1)}, u32[]{:S(2)}) copy-start(bf16[256,1024]{1,0:T(8,128)(2,1)} %param.12) | copy-start | bytes 1572868
  38.4 12.8 %all-to-all-start.2 = ((bf16[4,64,640]{2,1,0:T(8,128)(2,1)}), bf16[4,64,640]{2,1,0:T(8,128)(2,1)S(1)}, u32[]{:S(2)}, u32[]{:S(2)}) async-start(bf16[4,64,640]{2,1,0:T(8,128)(2,1)} %bitcast.10), calls=%async_computation.2 | async-start | bytes 655360 | tf_op jit(solution)/shard_map/all_to_all | solution.py:16
  41.9 140.7 %all-gather.5.cloned.1.call-start = ((), (), s32[]{:S(2)}) async-start(), calls=%async_computation.13 | async-start | bytes 1769472 | tf_op jit(solution)/shard_map/all_gather | solution.py:78
  42.0 0.7 copy-start.2
  42.7 9.1 %collective-permute-start = (bf16[256,1024]{1,0:T(8,128)(2,1)S(1)}, bf16[256,1024]{1,0:T(8,128)(2,1)S(1)}, u32[]{:S(2)}, u32[]{:S(2)}) collective-permute-start(bf16[256,1024]{1,0:T(8,128)(2,1)S(1)} %copy-done.4), channel_id=1, source_target_pairs={{0,0},{1,256},{2,512},{3,768},{256,1},{257,257},{258,513},{259,769... | collective-permute-start | bytes 1572872 | tf_op jit(solution)/shard_map/ppermute | solution.py:75
  43.4 64.6 %copy-start.5 = (s32[1,2]{1,0:T(1,128)S(1)}, s32[1,2]{1,0:T(1,128)}, u32[]{:S(2)}) copy-start(s32[1,2]{1,0:T(1,128)} %param.11) | copy-start | bytes 28
  45.0 6.9 %collective-permute-start.1 = (bf16[64,1024]{1,0:T(8,128)(2,1)S(1)}, bf16[64,1024]{1,0:T(8,128)(2,1)S(1)}, u32[]{:S(2)}, u32[]{:S(2)}) collective-permute-start(bf16[64,1024]{1,0:T(8,128)(2,1)S(1)} %get-tuple-element.43), channel_id=1, source_target_pairs={{0,32},{32,0},{1,33},{33,1},{2,34},{34,2},{3,35},{35,3},{4,36},{36... | collective-permute-start | bytes 393224 | tf_op jit(solution)/shard_map/ppermute | solution.py:92
  51.8 36.5 %all-to-all-start.3 = ((bf16[8,8,512]{2,1,0:T(8,128)(2,1)}), bf16[8,8,512]{2,1,0:T(8,128)(2,1)S(1)}, u32[]{:S(2)}, u32[]{:S(2)}) async-start(bf16[8,8,512]{2,1,0:T(8,128)(2,1)} %bitcast.11), calls=%async_computation.3 | async-start | bytes 131072 | tf_op jit(solution)/shard_map/all_to_all | solution.py:16
  66.7 47.3 %collective-permute-start.2 = (bf16[256,1024]{1,0:T(8,128)(2,1)S(1)}, bf16[256,1024]{1,0:T(8,128)(2,1)S(1)}, u32[]{:S(2)}, u32[]{:S(2)}) collective-permute-start(bf16[256,1024]{1,0:T(8,128)(2,1)S(1)} %collective-permute-done.root_own), channel_id=1, source_target_pairs={{0,32},{32,0},{1,33},{33,1},{2,34},{34,2},{3,35},{35,3},{4,36},{36... | collective-permute-start | bytes 1572872 | tf_op jit(solution)/shard_map/ppermute | solution.py:103
  89.0 40.2 %all-to-all-start.4 = ((bf16[8,8,512]{2,1,0:T(8,128)(2,1)}), bf16[8,8,512]{2,1,0:T(8,128)(2,1)S(1)}, u32[]{:S(2)}, u32[]{:S(2)}) async-start(bf16[8,8,512]{2,1,0:T(8,128)(2,1)} %broadcast_in_dim.15), calls=%async_computation.4 | async-start | bytes 131072 | tf_op jit(solution)/shard_map/all_to_all | solution.py:16
  129.9 51.4 %all-to-all-start.5 = ((bf16[4,72,512]{2,1,0:T(8,128)(2,1)}), bf16[4,72,512]{2,1,0:T(8,128)(2,1)S(1)}, u32[]{:S(2)}, u32[]{:S(2)}) async-start(bf16[4,72,512]{2,1,0:T(8,128)(2,1)} %broadcast_in_dim.16), calls=%async_computation.5 | async-start | bytes 589824 | tf_op jit(solution)/shard_map/all_to_all | solution.py:16
  191.0 37.5 %all-to-all-start.7 = ((bf16[8,8,2048]{2,1,0:T(8,128)(2,1)}), bf16[8,8,2048]{2,1,0:T(8,128)(2,1)S(1)}, u32[]{:S(2)}, u32[]{:S(2)}) async-start(bf16[8,8,2048]{2,1,0:T(8,128)(2,1)} %pad_maximum_fusion.1), calls=%async_computation.7 | async-start | bytes 524288 | tf_op jit(solution)/shard_map/all_to_all | solution.py:16
  229.2 10.5 %all-to-all-start.8 = ((bf16[4,8,2048]{2,1,0:T(8,128)(2,1)}), bf16[4,8,2048]{2,1,0:T(8,128)(2,1)S(1)}, u32[]{:S(2)}, u32[]{:S(2)}) async-start(bf16[4,8,2048]{2,1,0:T(8,128)(2,1)} %broadcast_in_dim.18), calls=%async_computation.8 | async-start | bytes 262144 | tf_op jit(solution)/shard_map/all_to_all | solution.py:16
  240.9 32.6 %all-to-all-start.9 = ((bf16[8,8,512]{2,1,0:T(8,128)(2,1)}), bf16[8,8,512]{2,1,0:T(8,128)(2,1)S(1)}, u32[]{:S(2)}, u32[]{:S(2)}) async-start(bf16[8,8,512]{2,1,0:T(8,128)(2,1)} %broadcast_in_dim.19), calls=%async_computation.9 | async-start | bytes 131072 | tf_op jit(solution)/shard_map/all_to_all | solution.py:16
  274.9 8.9 %all-to-all-start.10 = ((bf16[4,64,512]{2,1,0:T(8,128)(2,1)}), bf16[4,64,512]{2,1,0:T(8,128)(2,1)S(1)}, u32[]{:S(2)}, u32[]{:S(2)}) async-start(bf16[4,64,512]{2,1,0:T(8,128)(2,1)} %broadcast_in_dim.20), calls=%async_computation.10 | async-start | bytes 524288 | tf_op jit(solution)/shard_map/all_to_all | solution.py:16
Sparse Core Ops, SparseCore 0:
  45.4 75.2 all-gather.4

commit v2 on v1

v2 whole, which is shorter than its diff:
```python
import jax
import jax.numpy as jnp
from jax import lax
from jax.experimental import pallas as pl
from jax.experimental.pallas import tpu as pltpu
from jax.sharding import Mesh, PartitionSpec as P

BF = jnp.bfloat16
F32 = jnp.float32
TILE = 128
LEAF, Y, CORE, ZHI, ZLO = 4, 4, 2, 4, 8
Z = ("zhi", "zlo")


def exchange(x, axis):
    return lax.all_to_all(x, axis, 0, 0, tiled=True)


def share(x, axis, n):
    return exchange(jnp.broadcast_to(x[None], (n,) + x.shape), axis)


def total(parts):
    return jnp.sum(parts.astype(F32), axis=0)


def dot(a, b, contract):
    return lax.dot_general(a, b, (contract, ((), ())), preferred_element_type=F32)


def place_kernel(slot_ref, upd_ref, rhs_own, rhs_oth, root_own, root_oth, out_ref, side_ref):
    half = rhs_own.shape[1]
    side_ref[:, :half] = rhs_own[...].astype(F32)
    side_ref[:, half:] = rhs_oth[...].astype(F32)
    width = side_ref.shape[0]
    for k in range(LEAF):
        for u in range(4):
            at = pl.ds(pl.multiple_of(slot_ref[k * 4 + u] * TILE, TILE), TILE)
            side_ref[:, at] = side_ref[:, at] - upd_ref[k, :width, u * TILE:(u + 1) * TILE].astype(F32)
    out = dot(side_ref[:, :half].astype(BF), root_own[...], ((1,), (1,)))
    out = out + dot(side_ref[:, half:].astype(BF), root_oth[...], ((1,), (1,)))
    out_ref[...] = out.astype(BF)


def spread_kernel(slot_ref, parts_ref, root_own, root_oth, out_ref, sol_ref):
    half = root_own.shape[1]
    forward = parts_ref[0].astype(F32)
    for k in range(1, Y):
        forward = forward + parts_ref[k].astype(F32)
    forward = forward.astype(BF)
    sol_ref[:, :half] = dot(forward, root_own[...], ((1,), (0,)))
    sol_ref[:, half:] = dot(forward, root_oth[...], ((1,), (0,)))
    width, span = forward.shape[0], 4 * TILE
    few = width // LEAF
    for k in range(LEAF):
        for u in range(4):
            at = pl.ds(pl.multiple_of(slot_ref[k * 4 + u] * TILE, TILE), TILE)
            out_ref[k, :width, u * TILE:(u + 1) * TILE] = sol_ref[:, at].astype(BF)
        mine = sol_ref[k * few:(k + 1) * few, :]
        mine = jnp.concatenate([mine[:, j * span:(j + 1) * span] for j in range(4)], axis=0)
        out_ref[k, width:, :] = mine.astype(BF)


def call(kernel, out_shape, scratch, n_in):
    return pl.pallas_call(
        kernel,
        out_shape=out_shape,
        in_specs=[pl.BlockSpec(memory_space=pltpu.SMEM)]
        + [pl.BlockSpec(memory_space=pltpu.VMEM)] * n_in,
        out_specs=jax.tree.map(lambda _: pl.BlockSpec(memory_space=pltpu.VMEM), out_shape),
        scratch_shapes=scratch,
        compiler_params=pltpu.CompilerParams(vmem_limit_bytes=32 * 1024 * 1024),
    )


def body(child_inv, child_panel, child_rhs, anc_tiles, root_inv, root_rhs):
    inv, panel, rhs, anc = child_inv[0], child_panel[0], child_rhs[0], anc_tiles[0]
    y, core = lax.axis_index("y"), lax.axis_index("core")
    leaf, zlo = lax.axis_index("leaf"), lax.axis_index("zlo")
    rows = root_rhs.shape[0]
    half = rhs.shape[1] // CORE
    width = half // ZLO
    few = width // LEAF

    def source(to_leaf, to_zlo, j):
        return (to_zlo % LEAF) * ZLO + 2 * to_leaf + (j if to_zlo < LEAF else 1 - j)

    root_own = [
        lax.ppermute(
            root_inv,
            ("leaf", "zlo"),
            [(source(t, s, j), t * ZLO + s) for t in range(LEAF) for s in range(ZLO)],
        )
        for j in range(2)
    ]
    n = inv.shape[0]
    packed = jnp.concatenate([inv[:, i:i + n] for i in range(0, inv.shape[1], n)] + [panel], axis=0)
    packed = lax.all_gather(packed, ("core", "zlo"), axis=0, tiled=False)

    part = dot(rhs, inv, ((0,), (1,))).astype(BF).reshape(CORE, half, n)
    chunk = lax.dynamic_slice_in_dim(
        root_rhs.reshape(rows, CORE, ZLO, width), zlo, 1, axis=2
    )[:, :, 0]
    chunk = jnp.transpose(chunk, (1, 2, 0)).reshape(CORE, width * rows // n, n)
    names = jnp.zeros((16, n), BF).at[:, :2].set(anc.astype(BF)[None])
    local_part = jnp.concatenate([panel, names], axis=0)
    local_part = jnp.broadcast_to(local_part[None], (CORE,) + local_part.shape)
    first = exchange(jnp.concatenate([part, chunk, local_part], axis=1), "core")
    at = [half, half + chunk.shape[1], half + chunk.shape[1] + panel.shape[0]]
    forward = total(share(total(first[:, :at[0]]).astype(BF), "y", Y)).astype(BF)
    side = first[:, at[0]:at[1]].reshape(CORE, width, rows)
    side_own = jnp.where(core == 0, side[0], side[1])
    side_oth = jnp.where(core == 0, side[1], side[0])
    panel_y = first[:, at[1]:at[2]].reshape(-1, n)
    anc_y = first[:, at[2], :2].reshape(-1)

    update = dot(forward, panel_y, ((1,), (1,))).astype(BF)
    span = update.shape[1]
    both = jnp.concatenate([update, forward], axis=1).reshape(ZLO, width, -1)
    both = exchange(both, "zlo")
    forward_all = jnp.transpose(both[:, :, span:], (1, 0, 2)).reshape(width, -1)
    update = total(both[:, :, :span]).astype(BF)
    update = total(share(update, "zhi", ZHI)).astype(BF)
    root_own, update = lax.optimization_barrier((root_own, update))
    root_own = jnp.concatenate(root_own, axis=0)
    root_oth = lax.ppermute(root_own, "core", [(0, 1), (1, 0)])
    names = jnp.zeros((16, span), BF).at[:, :4].set(anc_y[None])
    update = share(jnp.concatenate([update, names], axis=0), "leaf", LEAF)
    slots = update[:, width, :4].reshape(-1).astype(jnp.int32)
    slots = lax.rem(slots - y * 16 + core * 8, 16)

    root_part = call(
        place_kernel,
        jax.ShapeDtypeStruct((width, root_own.shape[0]), BF),
        [pltpu.VMEM((width, 2 * rows), F32)],
        5,
    )(slots, update, side_own, side_oth, root_own, root_oth)
    sol = call(
        spread_kernel,
        jax.ShapeDtypeStruct((LEAF, 2 * width, span), BF),
        [pltpu.VMEM((width, 2 * rows), F32)],
        3,
    )(slots, share(root_part, "y", Y), root_own, root_oth)
    sol = total(exchange(sol, "leaf")).astype(BF)
    picked, root = sol[:width], sol[width:]
    packed, picked = lax.optimization_barrier((packed, picked))
    inv_all = packed[:, :inv.size // n].reshape(CORE, ZLO, -1, n, n)
    inv_all = jnp.transpose(inv_all, (0, 1, 3, 2, 4)).reshape(CORE, ZLO * n, inv.shape[1])
    panel_all = packed[:, inv.size // n:].reshape(CORE, ZLO, -1, n)
    panel_all = jnp.transpose(panel_all, (1, 0, 2, 3)).reshape(ZLO, -1, n)
    picked = total(share(picked, "zhi", ZHI)).astype(BF)

    correction = jnp.concatenate(
        [dot(picked, panel_all[z], ((1,), (0,))) for z in range(ZLO)], axis=1
    ).astype(BF)
    correction = total(share(correction, "y", Y)).astype(BF)
    residue = (forward_all.astype(F32) - correction.astype(F32)).astype(BF)
    child = jnp.stack([dot(inv_all[c], residue, ((0,), (1,))) for c in range(CORE)]).astype(BF)

    cols = ZHI * ZLO
    child = jnp.transpose(child.reshape(CORE, cols, -1, width), (1, 0, 2, 3)).reshape(cols, -1)
    n_child = child.shape[1]
    root = jnp.transpose(root.reshape(CORE, 2, few, span), (0, 2, 1, 3)).reshape(CORE, few, rows)
    root = jnp.stack([jnp.where(core == 0, root[0], root[1]), jnp.where(core == 0, root[1], root[0])])
    root = jnp.transpose(root.reshape(CORE, few, cols, -1), (2, 0, 1, 3)).reshape(cols, -1)
    out = exchange(jnp.concatenate([child, root], axis=1).reshape(cols, -1, TILE), Z)
    out = total(out.reshape(ZHI, ZLO, -1)).astype(BF)
    child = jnp.transpose(out[:, :n_child].reshape(ZLO, CORE, -1), (1, 0, 2)).reshape(CORE, -1)
    root = jnp.transpose(out[:, n_child:].reshape(ZLO, CORE, -1), (1, 0, 2)).reshape(CORE, -1)
    n_child = child.shape[1]
    out = jnp.concatenate([child, root], axis=1)
    out = jnp.broadcast_to(out[None], (LEAF,) + out.shape).reshape(LEAF * CORE, -1, TILE)
    out = exchange(out, ("leaf", "core")).reshape(LEAF, CORE, -1)
    child = lax.dynamic_index_in_dim(out, leaf, 0, keepdims=False)[:, :n_child]
    child = jnp.transpose(child.reshape(CORE * ZLO, -1, width), (1, 0, 2)).reshape(-1, CORE * half)
    root = out[:, :, n_child:].reshape(LEAF, CORE, ZLO, few, -1)
    root = jnp.transpose(root, (4, 1, 2, 0, 3)).reshape(-1, CORE * half)
    return child[None], root


def solution(mesh):
    split = Mesh(
        mesh.devices.reshape(LEAF, Y, CORE, ZHI, ZLO), ("leaf", "y", "core", "zhi", "zlo")
    )
    row, col = ("y", "core"), ("zhi", "zlo")
    in_specs = (
        P("leaf", col, row),
        P("leaf", row, col),
        P("leaf", row, None),
        P("leaf", row),
        P(col, row),
        P(row, None),
    )
    out_specs = (P("leaf", row + col, None), P(row + col, None))
    return jax.shard_map(body, mesh=split, in_specs=in_specs, out_specs=out_specs, check_vma=False)
```

time: 345 us -> 366 us (1.061)
  starting transfers between devices: 134 us -> 77.4 us
  waiting for transfers between devices: 89.7 us -> 131 us
  blocking collectives: 80.6 us -> 104 us
  local copies, waits for them, and re-layouts: 15.3 us -> 26 us
    ppermute x2, waiting for transfers between devices: 0.01 us -> 93.5 us  [body(): lax.ppermute(root_inv, ('leaf', 'zlo'), [(source(t, s, j), t * ZLO + s) f...]
    all_to_all x9 -> x5, waiting for transfers between devices: 89.6 us -> 37 us  [exchange(): return lax.all_to_all(x, axis, 0, 0, tiled=True)]
    all_to_all x9 -> x5, starting transfers between devices: 112 us -> 63.4 us  [exchange(): return lax.all_to_all(x, axis, 0, 0, tiled=True)]
    all_to_all x4 -> x6, blocking collectives: 74 us -> 104 us  [exchange(): return lax.all_to_all(x, axis, 0, 0, tiled=True)]
    ppermute x1, starting transfers between devices: 17.4 us -> 2.29 us  [body(): root_oth = lax.ppermute(root_own, 'core', [(0, 1), (1, 0)])]
    ppermute x2, starting transfers between devices: 4.07 us -> 11.7 us  [body(): lax.ppermute(root_inv, ('leaf', 'zlo'), [(source(t, s, j), t * ZLO + s) f...]
    unnamed x1 -> x0, blocking collectives: 4.57 us -> none
  transfers between devices with their start and end apart: 13 -> 9, of which waited for: 9 -> 6; matrix products, arithmetic and copies ran while one was open for 3% -> 6% of each run, Pallas kernels for 0% -> 1%
where the time goes in v2:
time: 366 us; the launch traced here: 364 us
  waiting for transfers between devices  131 us (36%)
  blocking collectives  104 us (28%)
  starting transfers between devices  77.4 us (21%)
  local copies, waits for them, and re-layouts  26 us (7%)
  between operations  14.7 us (4%)
  other arithmetic  4.68 us (1%)
  matrix products  4.36 us (1%)
    all_to_all x6, blocking collectives, exchange(): return lax.all_to_all(x, axis, 0, 0, tiled=True)  104 us
    ppermute x2, waiting for transfers between devices, body(): lax.ppermute(root_inv, ('leaf', 'zlo'), [(source(t, s, j), t * ZLO + s) f...  93.5 us
    all_to_all x5, starting transfers between devices, exchange(): return lax.all_to_all(x, axis, 0, 0, tiled=True)  63.4 us
    all_to_all x5, waiting for transfers between devices, exchange(): return lax.all_to_all(x, axis, 0, 0, tiled=True)  37 us
    ppermute x2, starting transfers between devices, body(): lax.ppermute(root_inv, ('leaf', 'zlo'), [(source(t, s, j), t * ZLO + s) f...  11.7 us
  transfers between devices with their start and end apart: 9, of which 6 were waited for; matrix products, arithmetic and copies ran while one was open for 6% of the time, Pallas kernels for 1%

profile of v2, /device:TPU:1, one launch (start us, length us, event | category | flops | bytes accessed | tf_op | source)
XLA Modules:
  0.0 364.3 jit_solution(6110579891539309832)
XLA Ops:
  12.6 1.5 copy.38
  15.3 17.8 %all_to_all.55 = bf16[2,784,128]{2,1,0:T(8,128)(2,1)S(1)} all-to-all(bf16[2,784,128]{2,1,0:T(8,128)(2,1)S(1)} %pad_maximum_fusion), channel_id=1, replica_groups=mesh['leaf'=4,'y'=4,'core'=2,'zhi'=4,'zlo'=8] {'core'}, dimensions={0} | all-to-all | bytes 802816 | tf_op jit(solution)/shard_map/all_to_all | solution.py:16
  33.2 8.9 %all_to_all.56 = bf16[4,256,128]{2,1,0:T(8,128)(2,1)S(1)} all-to-all(bf16[4,256,128]{2,1,0:T(8,128)(2,1)S(1)} %broadcast_in_dim.17), channel_id=1, replica_groups=mesh['leaf'=4,'y'=4,'core'=2,'zhi'=4,'zlo'=8] {'y'}, dimensions={0} | all-to-all | bytes 524288 | tf_op jit(solution)/shard_map/all_to_all | solution.py:16
  42.4 25.7 %all_to_all.57 = bf16[8,32,640]{2,1,0:T(8,128)(2,1)S(1)} all-to-all(bf16[8,32,640]{2,1,0:T(8,128)(2,1)S(1)} %bitcast.122), channel_id=1, replica_groups=mesh['leaf'=4,'y'=4,'core'=2,'zhi'=4,'zlo'=8] {'zlo'}, dimensions={0} | all-to-all | bytes 655360 | tf_op jit(solution)/shard_map/all_to_all | solution.py:16
  68.9 25.3 %all-to-all-start.3 = ((bf16[4,32,512]{2,1,0:T(8,128)(2,1)}), bf16[4,32,512]{2,1,0:T(8,128)(2,1)S(1)}, u32[]{:S(2)}, u32[]{:S(2)}) async-start(bf16[4,32,512]{2,1,0:T(8,128)(2,1)} %broadcast_in_dim.18), calls=%async_computation.3 | async-start | bytes 262144 | tf_op jit(solution)/shard_map/all_to_all | solution.py:16
  95.0 11.0 %collective-permute-start.1 = (bf16[256,1024]{1,0:T(8,128)(2,1)S(1)}, bf16[256,1024]{1,0:T(8,128)(2,1)S(1)}, u32[]{:S(2)}, u32[]{:S(2)}) collective-permute-start(bf16[256,1024]{1,0:T(8,128)(2,1)S(1)} %copy-done.5), channel_id=1, source_target_pairs={{1,0},{257,1},{513,2},{769,3},{0,4},{256,5},{512,6},{768,7},{3,256... | collective-permute-start | bytes 1572872 | tf_op jit(solution)/shard_map/ppermute | solution.py:89
  106.0 13.4 %all-to-all-done.3 = bf16[4,32,512]{2,1,0:T(8,128)(2,1)S(1)} async-done(((bf16[4,32,512]{2,1,0:T(8,128)(2,1)}), bf16[4,32,512]{2,1,0:T(8,128)(2,1)S(1)}, u32[]{:S(2)}, u32[]{:S(2)}) %all-to-all-start.3) | async-done | bytes 131104 | tf_op jit(solution)/shard_map/all_to_all | solution.py:16
  119.4 93.5 %collective-permute-done.1 = bf16[256,1024]{1,0:T(8,128)(2,1)S(1)} collective-permute-done((bf16[256,1024]{1,0:T(8,128)(2,1)S(1)}, bf16[256,1024]{1,0:T(8,128)(2,1)S(1)}, u32[]{:S(2)}, u32[]{:S(2)}) %collective-permute-start.1) | collective-permute-done | bytes 524320 | tf_op jit(solution)/shard_map/ppermute | solution.py:89
  213.0 2.3 collective-permute-start.2
  217.4 3.4 all-to-all-start.4
  223.2 3.2 all-to-all-done.4.upd_ref
  227.8 7.2 %all_to_all.58.parts_ref = bf16[4,32,512]{2,1,0:T(8,128)(2,1)S(1)} all-to-all(bf16[4,32,512]{2,1,0:T(8,128)(2,1)S(1)} %broadcast_in_dim.20), channel_id=1, replica_groups=mesh['leaf'=4,'y'=4,'core'=2,'zhi'=4,'zlo'=8] {'y'}, dimensions={0} | all-to-all | bytes 262144 | tf_op jit(solution)/shard_map/all_to_all | solution.py:16
  236.1 7.9 %all_to_all.59 = bf16[4,64,512]{2,1,0:T(8,128)(2,1)S(1)} all-to-all(bf16[4,64,512]{2,1,0:T(8,128)(2,1)S(1)} %shard_map.78), channel_id=1, replica_groups=mesh['leaf'=4,'y'=4,'core'=2,'zhi'=4,'zlo'=8] {'leaf'}, dimensions={0} | all-to-all | bytes 524288 | tf_op jit(solution)/shard_map/all_to_all | solution.py:16
  244.8 21.8 %all-to-all-start.7 = ((bf16[4,32,512]{2,1,0:T(8,128)(2,1)}), bf16[4,32,512]{2,1,0:T(8,128)(2,1)}, u32[]{:S(2)}, u32[]{:S(2)}) async-start(bf16[4,32,512]{2,1,0:T(8,128)(2,1)} %broadcast_in_dim.21), calls=%async_computation.7 | async-start | bytes 262144 | tf_op jit(solution)/shard_map/all_to_all | solution.py:16
  267.1 2.3 slice.164
  269.4 3.2 slice.161
  272.6 3.1 copy.39
  275.7 2.1 fusion.20
  277.8 10.6 %all-to-all-done.7 = bf16[4,32,512]{2,1,0:T(8,128)(2,1)} async-done(((bf16[4,32,512]{2,1,0:T(8,128)(2,1)}), bf16[4,32,512]{2,1,0:T(8,128)(2,1)}, u32[]{:S(2)}, u32[]{:S(2)}) %all-to-all-start.7) | async-done | bytes 131104 | tf_op jit(solution)/shard_map/all_to_all | solution.py:16
  293.0 3.4 all-to-all-start.8
  297.1 4.8 %all-to-all-done.8 = bf16[4,32,1024]{2,1,0:T(8,128)(2,1)S(1)} async-done(((bf16[4,32,1024]{2,1,0:T(8,128)(2,1)}), bf16[4,32,1024]{2,1,0:T(8,128)(2,1)S(1)}, u32[]{:S(2)}, u32[]{:S(2)}) %all-to-all-start.8) | async-done | bytes 262176 | tf_op jit(solution)/shard_map/all_to_all | solution.py:16
  303.4 36.8 %all_to_all.60 = bf16[32,12,128]{2,1,0:T(8,128)(2,1)S(1)} all-to-all(bf16[32,12,128]{2,1,0:T(8,128)(2,1)S(1)} %reshape.313), channel_id=1, replica_groups=mesh['leaf'=4,'y'=4,'core'=2,'zhi'=4,'zlo'=8] {'zhi','zlo'}, dimensions={0} | all-to-all | bytes 196608 | tf_op jit(solution)/shard_map/all_to_all | solution.py:16
  341.1 9.5 %all-to-all-start.10 = ((bf16[8,48,128]{2,1,0:T(8,128)(2,1)}), bf16[8,48,128]{2,1,0:T(8,128)(2,1)S(1)}, u32[]{:S(2)}, u32[]{:S(2)}) async-start(bf16[8,48,128]{2,1,0:T(8,128)(2,1)} %reshape.319), calls=%async_computation.10 | async-start | bytes 196608 | tf_op jit(solution)/shard_map/all_to_all | solution.py:16
  350.6 5.0 %all-to-all-done.10 = bf16[8,48,128]{2,1,0:T(8,128)(2,1)S(1)} async-done(((bf16[8,48,128]{2,1,0:T(8,128)(2,1)}), bf16[8,48,128]{2,1,0:T(8,128)(2,1)S(1)}, u32[]{:S(2)}, u32[]{:S(2)}) %all-to-all-start.10) | async-done | bytes 98336 | tf_op jit(solution)/shard_map/all_to_all | solution.py:16
  (118 shorter events, 26.0 us)
Async XLA Ops:
  7.2 7.0 %copy-start = (bf16[1,512,512]{2,1,0:T(8,128)(2,1)S(1)}, bf16[1,512,512]{2,1,0:T(8,128)(2,1)}, u32[]{:S(2)}) copy-start(bf16[1,512,512]{2,1,0:T(8,128)(2,1)} %param.12) | copy-start | bytes 1572868
  7.2 7.0 %copy-start.2 = (bf16[1,128,512]{2,1,0:T(8,128)(2,1)S(1)}, bf16[1,128,512]{2,1,0:T(8,128)(2,1)}, u32[]{:S(2)}) copy-start(bf16[1,128,512]{2,1,0:T(8,128)(2,1)} %param.10) | copy-start | bytes 393220
  7.2 8.0 %copy-start.4 = (bf16[1,256,128]{2,1,0:T(8,128)(2,1)S(1)}, bf16[1,256,128]{2,1,0:T(8,128)(2,1)}, u32[]{:S(2)}) copy-start(bf16[1,256,128]{2,1,0:T(8,128)(2,1)} %param.11) | copy-start | bytes 196612
  7.2 7.3 %copy-start.6 = (s32[1,2]{1,0:T(1,128)S(1)}, s32[1,2]{1,0:T(1,128)}, u32[]{:S(2)}) copy-start(s32[1,2]{1,0:T(1,128)} %param.13) | copy-start | bytes 28
  7.2 236.9 %all-gather.3.cloned.1.call-start = ((), (), s32[]{:S(2)}) async-start(), calls=%async_computation.11 | async-start | bytes 3342336 | tf_op jit(solution)/shard_map/all_gather | solution.py:98
  11.2 0.7 copy-start.3
  33.1 61.1 %copy-start.5 = (bf16[256,1024]{1,0:T(8,128)(2,1)S(1)}, bf16[256,1024]{1,0:T(8,128)(2,1)}, u32[]{:S(2)}) copy-start(bf16[256,1024]{1,0:T(8,128)(2,1)} %param.14) | copy-start | bytes 1572868
  68.2 198.4 %copy-start.1 = (bf16[8,32,640]{2,1,0:T(8,128)(2,1)}, bf16[8,32,640]{2,1,0:T(8,128)(2,1)S(1)}, u32[]{:S(2)}) copy-start(bf16[8,32,640]{2,1,0:T(8,128)(2,1)S(1)} %all_to_all.57) | copy-start | bytes 983044
  68.9 50.4 %all-to-all-start.3 = ((bf16[4,32,512]{2,1,0:T(8,128)(2,1)}), bf16[4,32,512]{2,1,0:T(8,128)(2,1)S(1)}, u32[]{:S(2)}, u32[]{:S(2)}) async-start(bf16[4,32,512]{2,1,0:T(8,128)(2,1)} %broadcast_in_dim.18), calls=%async_computation.3 | async-start | bytes 262144 | tf_op jit(solution)/shard_map/all_to_all | solution.py:16
  94.3 25.1 %collective-permute-start = (bf16[256,1024]{1,0:T(8,128)(2,1)S(1)}, bf16[256,1024]{1,0:T(8,128)(2,1)S(1)}, u32[]{:S(2)}, u32[]{:S(2)}) collective-permute-start(bf16[256,1024]{1,0:T(8,128)(2,1)S(1)} %copy-done.5), channel_id=1, source_target_pairs={{0,0},{256,1},{512,2},{768,3},{1,4},{257,5},{513,6},{769,7},{2,256... | collective-permute-start | bytes 1572872 | tf_op jit(solution)/shard_map/ppermute | solution.py:89
  95.0 117.9 %collective-permute-start.1 = (bf16[256,1024]{1,0:T(8,128)(2,1)S(1)}, bf16[256,1024]{1,0:T(8,128)(2,1)S(1)}, u32[]{:S(2)}, u32[]{:S(2)}) collective-permute-start(bf16[256,1024]{1,0:T(8,128)(2,1)S(1)} %copy-done.5), channel_id=1, source_target_pairs={{1,0},{257,1},{513,2},{769,3},{0,4},{256,5},{512,6},{768,7},{3,256... | collective-permute-start | bytes 1572872 | tf_op jit(solution)/shard_map/ppermute | solution.py:89
  213.0 13.5 %collective-permute-start.2 = (bf16[512,1024]{1,0:T(8,128)(2,1)S(1)}, bf16[512,1024]{1,0:T(8,128)(2,1)S(1)}, u32[]{:S(2)}, u32[]{:S(2)}) collective-permute-start(bf16[512,1024]{1,0:T(8,128)(2,1)S(1)} %constant_dynamic-update-slice_fusion.1.root_own), channel_id=1, source_target_pairs={{0,32},{32,0},{1,33},{33,1},{2,34},{34,2},{3,35},{35,3},{4,36},{36... | collective-permute-start | bytes 3145736 | tf_op jit(solution)/shard_map/ppermute | solution.py:126
  217.4 9.0 %all-to-all-start.4 = ((bf16[4,48,512]{2,1,0:T(8,128)(2,1)}), bf16[4,48,512]{2,1,0:T(8,128)(2,1)S(1)}, u32[]{:S(2)}, u32[]{:S(2)}) async-start(bf16[4,48,512]{2,1,0:T(8,128)(2,1)} %broadcast_in_dim.19), calls=%async_computation.4 | async-start | bytes 393216 | tf_op jit(solution)/shard_map/all_to_all | solution.py:16
  244.8 43.6 %all-to-all-start.7 = ((bf16[4,32,512]{2,1,0:T(8,128)(2,1)}), bf16[4,32,512]{2,1,0:T(8,128)(2,1)}, u32[]{:S(2)}, u32[]{:S(2)}) async-start(bf16[4,32,512]{2,1,0:T(8,128)(2,1)} %broadcast_in_dim.21), calls=%async_computation.7 | async-start | bytes 262144 | tf_op jit(solution)/shard_map/all_to_all | solution.py:16
  293.0 8.9 %all-to-all-start.8 = ((bf16[4,32,1024]{2,1,0:T(8,128)(2,1)}), bf16[4,32,1024]{2,1,0:T(8,128)(2,1)S(1)}, u32[]{:S(2)}, u32[]{:S(2)}) async-start(bf16[4,32,1024]{2,1,0:T(8,128)(2,1)} %broadcast_in_dim.22), calls=%async_computation.8 | async-start | bytes 524288 | tf_op jit(solution)/shard_map/all_to_all | solution.py:16
  296.6 5.4 %slice-start = ((bf16[8,32,640]{2,1,0:T(8,128)(2,1)}), bf16[8,32,128]{2,1,0:T(8,128)(2,1)S(1)}, s32[]{:S(2)}) async-start(bf16[8,32,640]{2,1,0:T(8,128)(2,1)} %copy-done.1), calls=%async_computation.12 | async-start | bytes 131072 | tf_op jit(solution)/shard_map/slice | solution.py:121
  341.1 14.5 %all-to-all-start.10 = ((bf16[8,48,128]{2,1,0:T(8,128)(2,1)}), bf16[8,48,128]{2,1,0:T(8,128)(2,1)S(1)}, u32[]{:S(2)}, u32[]{:S(2)}) async-start(bf16[8,48,128]{2,1,0:T(8,128)(2,1)} %reshape.319), calls=%async_computation.10 | async-start | bytes 196608 | tf_op jit(solution)/shard_map/all_to_all | solution.py:16
Sparse Core Ops, SparseCore 0:
  12.1 210.6 all-gather.2

commit v3 on v2

--- a/solution.py
+++ b/solution.py
@@ -78,24 +78,24 @@
     y, core = lax.axis_index("y"), lax.axis_index("core")
     leaf, zlo = lax.axis_index("leaf"), lax.axis_index("zlo")
     rows = root_rhs.shape[0]
+    other = [(0, 1), (1, 0)]
     half = rhs.shape[1] // CORE
     width = half // ZLO
     few = width // LEAF
 
-    def source(to_leaf, to_zlo, j):
-        return (to_zlo % LEAF) * ZLO + 2 * to_leaf + (j if to_zlo < LEAF else 1 - j)
-
-    root_own = [
-        lax.ppermute(
-            root_inv,
-            ("leaf", "zlo"),
-            [(source(t, s, j), t * ZLO + s) for t in range(LEAF) for s in range(ZLO)],
-        )
-        for j in range(2)
-    ]
     n = inv.shape[0]
-    packed = jnp.concatenate([inv[:, i:i + n] for i in range(0, inv.shape[1], n)] + [panel], axis=0)
-    packed = lax.all_gather(packed, ("core", "zlo"), axis=0, tiled=False)
+    part_rows = root_inv.shape[0] // LEAF
+    quarter = lax.dynamic_slice_in_dim(root_inv, leaf * part_rows, part_rows, axis=0)
+    fold = rows // n
+    packed = jnp.concatenate(
+        [
+            quarter,
+            jnp.concatenate([inv[:n // 2], inv[n // 2:]], axis=1),
+            jnp.concatenate(jnp.split(panel, fold, axis=0), axis=1),
+        ],
+        axis=0,
+    )
+    packed = lax.all_gather(packed, "zlo", axis=0, tiled=False)
 
     part = dot(rhs, inv, ((0,), (1,))).astype(BF).reshape(CORE, half, n)
     chunk = lax.dynamic_slice_in_dim(
@@ -121,9 +121,9 @@
     forward_all = jnp.transpose(both[:, :, span:], (1, 0, 2)).reshape(width, -1)
     update = total(both[:, :, :span]).astype(BF)
     update = total(share(update, "zhi", ZHI)).astype(BF)
-    root_own, update = lax.optimization_barrier((root_own, update))
-    root_own = jnp.concatenate(root_own, axis=0)
-    root_oth = lax.ppermute(root_own, "core", [(0, 1), (1, 0)])
+    packed, update = lax.optimization_barrier((packed, update))
+    root_own = packed[:, :part_rows].reshape(-1, rows)
+    root_oth = lax.ppermute(root_own, "core", other)
     names = jnp.zeros((16, span), BF).at[:, :4].set(anc_y[None])
     update = share(jnp.concatenate([update, names], axis=0), "leaf", LEAF)
     slots = update[:, width, :4].reshape(-1).astype(jnp.int32)
@@ -135,27 +135,44 @@
         [pltpu.VMEM((width, 2 * rows), F32)],
         5,
     )(slots, update, side_own, side_oth, root_own, root_oth)
+    pairs = slots.reshape(LEAF, CORE, 2)
+    pairs = jnp.where(core == 0, pairs, pairs[:, ::-1]).reshape(-1)
     sol = call(
         spread_kernel,
         jax.ShapeDtypeStruct((LEAF, 2 * width, span), BF),
         [pltpu.VMEM((width, 2 * rows), F32)],
         3,
-    )(slots, share(root_part, "y", Y), root_own, root_oth)
+    )(pairs, share(root_part, "y", Y), root_own, root_oth)
     sol = total(exchange(sol, "leaf")).astype(BF)
     picked, root = sol[:width], sol[width:]
-    packed, picked = lax.optimization_barrier((packed, picked))
-    inv_all = packed[:, :inv.size // n].reshape(CORE, ZLO, -1, n, n)
-    inv_all = jnp.transpose(inv_all, (0, 1, 3, 2, 4)).reshape(CORE, ZLO * n, inv.shape[1])
-    panel_all = packed[:, inv.size // n:].reshape(CORE, ZLO, -1, n)
-    panel_all = jnp.transpose(panel_all, (1, 0, 2, 3)).reshape(ZLO, -1, n)
+    mine = packed[:, part_rows:]
+    packed = (mine, lax.ppermute(mine, "core", other))
+
+    def unpack(x):
+        x_inv = jnp.concatenate([x[:, :n // 2, :rows // 2], x[:, :n // 2, rows // 2:]], axis=1)
+        x_panel = jnp.transpose(x[:, n // 2:].reshape(ZLO, -1, fold, n), (0, 2, 1, 3))
+        return x_inv.reshape(ZLO * n, -1), x_panel.reshape(ZLO, -1, n)
+
+    (inv_own, panel_own), (inv_oth, panel_oth) = unpack(packed[0]), unpack(packed[1])
+    inv_own, panel_own, inv_oth, panel_oth, picked = lax.optimization_barrier(
+        (inv_own, panel_own, inv_oth, panel_oth, picked)
+    )
     picked = total(share(picked, "zhi", ZHI)).astype(BF)
 
+    first, second = picked[:, :span // 2], picked[:, span // 2:]
     correction = jnp.concatenate(
-        [dot(picked, panel_all[z], ((1,), (0,))) for z in range(ZLO)], axis=1
+        [
+            dot(first, panel_own[z], ((1,), (0,))) + dot(second, panel_oth[z], ((1,), (0,)))
+            for z in range(ZLO)
+        ],
+        axis=1,
     ).astype(BF)
     correction = total(share(correction, "y", Y)).astype(BF)
     residue = (forward_all.astype(F32) - correction.astype(F32)).astype(BF)
-    child = jnp.stack([dot(inv_all[c], residue, ((0,), (1,))) for c in range(CORE)]).astype(BF)
+    child = [dot(m, residue, ((0,), (1,))).astype(BF) for m in (inv_own, inv_oth)]
+    child = jnp.stack(
+        [jnp.where(core == 0, child[0], child[1]), jnp.where(core == 0, child[1], child[0])]
+    )
 
     cols = ZHI * ZLO
     child = jnp.transpose(child.reshape(CORE, cols, -1, width), (1, 0, 2, 3)).reshape(cols, -1)

time: 366 us -> 295 us (0.81)
  waiting for transfers between devices: 131 us -> 44.2 us
  blocking collectives: 104 us -> 128 us
  starting transfers between devices: 77.4 us -> 61 us
  matrix products: 4.36 us -> 11.7 us
    ppermute x3 -> x2, waiting for transfers between devices: 93.5 us -> 0.01 us  [the longest x1 0.01 us: body(): packed = (mine, lax.ppermute(mine, 'core', other))]
    all_to_all x6 -> x5, blocking collectives: 104 us -> 128 us  [exchange(): return lax.all_to_all(x, axis, 0, 0, tiled=True)]
    all_to_all x5 -> x6, starting transfers between devices: 63.4 us -> 51.9 us  [exchange(): return lax.all_to_all(x, axis, 0, 0, tiled=True)]
    dot_general x12 -> x20, matrix products: 4.36 us -> 11.7 us  [dot(): lax.dot_general(a, b, (contract, ((), ())), preferred_element_type=F32)]
    all_to_all x5 -> x6, waiting for transfers between devices: 37 us -> 44.2 us  [exchange(): return lax.all_to_all(x, axis, 0, 0, tiled=True)]
    ppermute x3 -> x2, starting transfers between devices: 14 us -> 9.09 us  [the longest x1 6.9 us: body(): root_oth = lax.ppermute(root_own, 'core', other)]
    slice x6 -> x7, local copies, waits for them, and re-layouts: 7.73 us -> 10.7 us  [the longest x2 3.58 us: unpack(): x[:, :n // 2, :rows // 2]]
  transfers between devices with their start and end apart: 9 -> 9, of which waited for: 6 -> 5; matrix products, arithmetic and copies ran while one was open for 6% -> 4% of each run, Pallas kernels for 1% -> 1%
where the time goes in v3:
time: 295 us; the launch traced here: 293 us
  blocking collectives  128 us (43%)
  starting transfers between devices  61 us (21%)
  waiting for transfers between devices  44.2 us (15%)
  local copies, waits for them, and re-layouts  26.7 us (9%)
  between operations  14.7 us (5%)
  matrix products  11.7 us (4%)
  other arithmetic  4.63 us (2%)
  Pallas kernels  3.01 us (1%)
    all_to_all x5, blocking collectives, exchange(): return lax.all_to_all(x, axis, 0, 0, tiled=True)  128 us
    all_to_all x6, starting transfers between devices, exchange(): return lax.all_to_all(x, axis, 0, 0, tiled=True)  51.9 us
    all_to_all x6, waiting for transfers between devices, exchange(): return lax.all_to_all(x, axis, 0, 0, tiled=True)  44.2 us
    dot_general x20, matrix products, dot(): lax.dot_general(a, b, (contract, ((), ())), preferred_element_type=F32)  11.7 us
    unnamed x31, local copies, waits for them, and re-layouts  7.23 us
    ppermute x1, starting transfers between devices, body(): root_oth = lax.ppermute(root_own, 'core', other)  6.9 us
  transfers between devices with their start and end apart: 9, of which 5 were waited for; matrix products, arithmetic and copies ran while one was open for 4% of the time, Pallas kernels for 1%

profile of v3, /device:TPU:1, one launch (start us, length us, event | category | flops | bytes accessed | tf_op | source)
XLA Modules:
  0.0 293.5 jit_solution(4450687721010568073)
XLA Ops:
  17.2 17.8 %all_to_all.55 = bf16[2,784,128]{2,1,0:T(8,128)(2,1)S(1)} all-to-all(bf16[2,784,128]{2,1,0:T(8,128)(2,1)S(1)} %pad_maximum_fusion.2), channel_id=1, replica_groups=mesh['leaf'=4,'y'=4,'core'=2,'zhi'=4,'zlo'=8] {'core'}, dimensions={0} | all-to-all | bytes 802816 | tf_op jit(solution)/shard_map/all_to_all | solution.py:16
  35.1 8.8 %all_to_all.56 = bf16[4,256,128]{2,1,0:T(8,128)(2,1)S(1)} all-to-all(bf16[4,256,128]{2,1,0:T(8,128)(2,1)S(1)} %broadcast_in_dim.17), channel_id=1, replica_groups=mesh['leaf'=4,'y'=4,'core'=2,'zhi'=4,'zlo'=8] {'y'}, dimensions={0} | all-to-all | bytes 524288 | tf_op jit(solution)/shard_map/all_to_all | solution.py:16
  44.3 26.2 %all_to_all.57 = bf16[8,32,640]{2,1,0:T(8,128)(2,1)S(1)} all-to-all(bf16[8,32,640]{2,1,0:T(8,128)(2,1)S(1)} %bitcast.185), channel_id=1, replica_groups=mesh['leaf'=4,'y'=4,'core'=2,'zhi'=4,'zlo'=8] {'zlo'}, dimensions={0} | all-to-all | bytes 655360 | tf_op jit(solution)/shard_map/all_to_all | solution.py:16
  71.9 26.7 %all-to-all-start.3 = ((bf16[4,32,512]{2,1,0:T(8,128)(2,1)}), bf16[4,32,512]{2,1,0:T(8,128)(2,1)S(1)}, u32[]{:S(2)}, u32[]{:S(2)}) async-start(bf16[4,32,512]{2,1,0:T(8,128)(2,1)} %broadcast_in_dim.18), calls=%async_computation.3 | async-start | bytes 262144 | tf_op jit(solution)/shard_map/all_to_all | solution.py:16
  100.1 24.3 %all-to-all-done.3 = bf16[4,32,512]{2,1,0:T(8,128)(2,1)S(1)} async-done(((bf16[4,32,512]{2,1,0:T(8,128)(2,1)}), bf16[4,32,512]{2,1,0:T(8,128)(2,1)S(1)}, u32[]{:S(2)}, u32[]{:S(2)}) %all-to-all-start.3) | async-done | bytes 131104 | tf_op jit(solution)/shard_map/all_to_all | solution.py:16
  124.5 1.3 slice.210
  125.8 2.7 slice.202
  128.5 6.9 %collective-permute-start.1 = (bf16[512,1024]{1,0:T(8,128)(2,1)S(1)}, bf16[512,1024]{1,0:T(8,128)(2,1)S(1)}, u32[]{:S(2)}, u32[]{:S(2)}) collective-permute-start(bf16[512,1024]{1,0:T(8,128)(2,1)S(1)} %bitcast.155), channel_id=1, source_target_pairs={{0,32},{32,0},{1,33},{33,1},{2,34},{34,2},{3,35},{35,3},{4,36},{36... | collective-permute-start | bytes 3145736 | tf_op jit(solution)/shard_map/ppermute | solution.py:126
  136.1 4.2 %all-to-all-start.4 = ((bf16[4,48,512]{2,1,0:T(8,128)(2,1)}), bf16[4,48,512]{2,1,0:T(8,128)(2,1)S(1)}, u32[]{:S(2)}, u32[]{:S(2)}) async-start(bf16[4,48,512]{2,1,0:T(8,128)(2,1)} %broadcast_in_dim.19), calls=%async_computation.4 | async-start | bytes 393216 | tf_op jit(solution)/shard_map/all_to_all | solution.py:16
  140.4 2.2 collective-permute-start
  142.6 2.3 fusion.85
  147.4 1.3 shard_map.77
  149.4 3.3 %all-to-all-start.5 = ((bf16[4,32,512]{2,1,0:T(8,128)(2,1)}), bf16[4,32,512]{2,1,0:T(8,128)(2,1)S(1)}, u32[]{:S(2)}, u32[]{:S(2)}) async-start(bf16[4,32,512]{2,1,0:T(8,128)(2,1)} %broadcast_in_dim.20), calls=%async_computation.5 | async-start | bytes 262144 | tf_op jit(solution)/shard_map/all_to_all | solution.py:16
  152.9 4.6 %all-to-all-done.5.parts_ref = bf16[4,32,512]{2,1,0:T(8,128)(2,1)S(1)} async-done(((bf16[4,32,512]{2,1,0:T(8,128)(2,1)}), bf16[4,32,512]{2,1,0:T(8,128)(2,1)S(1)}, u32[]{:S(2)}, u32[]{:S(2)}) %all-to-all-start.5) | async-done | bytes 131104 | tf_op jit(solution)/shard_map/all_to_all | solution.py:16
  157.5 1.7 shard_map.78
  159.3 4.9 %all-to-all-start.6 = ((bf16[4,64,512]{2,1,0:T(8,128)(2,1)}), bf16[4,64,512]{2,1,0:T(8,128)(2,1)S(1)}, u32[]{:S(2)}, u32[]{:S(2)}) async-start(bf16[4,64,512]{2,1,0:T(8,128)(2,1)} %shard_map.78), calls=%async_computation.6 | async-start | bytes 524288 | tf_op jit(solution)/shard_map/all_to_all | solution.py:16
  164.5 5.3 %all-to-all-done.6 = bf16[4,64,512]{2,1,0:T(8,128)(2,1)S(1)} async-done(((bf16[4,64,512]{2,1,0:T(8,128)(2,1)}), bf16[4,64,512]{2,1,0:T(8,128)(2,1)S(1)}, u32[]{:S(2)}, u32[]{:S(2)}) %all-to-all-start.6) | async-done | bytes 262176 | tf_op jit(solution)/shard_map/all_to_all | solution.py:16
  172.0 1.3 fusion.86
  173.3 37.3 %all_to_all.58 = bf16[4,32,512]{2,1,0:T(8,128)(2,1)S(1)} all-to-all(bf16[4,32,512]{2,1,0:T(8,128)(2,1)S(1)} %broadcast_in_dim.21), channel_id=1, replica_groups=mesh['leaf'=4,'y'=4,'core'=2,'zhi'=4,'zlo'=8] {'zhi'}, dimensions={0} | all-to-all | bytes 262144 | tf_op jit(solution)/shard_map/all_to_all | solution.py:16
  220.3 3.4 %all-to-all-start.8 = ((bf16[4,32,1024]{2,1,0:T(8,128)(2,1)}), bf16[4,32,1024]{2,1,0:T(8,128)(2,1)S(1)}, u32[]{:S(2)}, u32[]{:S(2)}) async-start(bf16[4,32,1024]{2,1,0:T(8,128)(2,1)} %broadcast_in_dim.22), calls=%async_computation.8 | async-start | bytes 524288 | tf_op jit(solution)/shard_map/all_to_all | solution.py:16
  224.3 5.0 %all-to-all-done.8 = bf16[4,32,1024]{2,1,0:T(8,128)(2,1)S(1)} async-done(((bf16[4,32,1024]{2,1,0:T(8,128)(2,1)}), bf16[4,32,1024]{2,1,0:T(8,128)(2,1)S(1)}, u32[]{:S(2)}, u32[]{:S(2)}) %all-to-all-start.8) | async-done | bytes 262176 | tf_op jit(solution)/shard_map/all_to_all | solution.py:16
  232.2 37.3 %all_to_all.59 = bf16[32,12,128]{2,1,0:T(8,128)(2,1)S(1)} all-to-all(bf16[32,12,128]{2,1,0:T(8,128)(2,1)S(1)} %reshape.312), channel_id=1, replica_groups=mesh['leaf'=4,'y'=4,'core'=2,'zhi'=4,'zlo'=8] {'zhi','zlo'}, dimensions={0} | all-to-all | bytes 196608 | tf_op jit(solution)/shard_map/all_to_all | solution.py:16
  270.5 9.3 %all-to-all-start.10 = ((bf16[8,48,128]{2,1,0:T(8,128)(2,1)}), bf16[8,48,128]{2,1,0:T(8,128)(2,1)S(1)}, u32[]{:S(2)}, u32[]{:S(2)}) async-start(bf16[8,48,128]{2,1,0:T(8,128)(2,1)} %reshape.318), calls=%async_computation.10 | async-start | bytes 196608 | tf_op jit(solution)/shard_map/all_to_all | solution.py:16
  279.8 5.0 %all-to-all-done.10 = bf16[8,48,128]{2,1,0:T(8,128)(2,1)S(1)} async-done(((bf16[8,48,128]{2,1,0:T(8,128)(2,1)}), bf16[8,48,128]{2,1,0:T(8,128)(2,1)S(1)}, u32[]{:S(2)}, u32[]{:S(2)}) %all-to-all-start.10) | async-done | bytes 98336 | tf_op jit(solution)/shard_map/all_to_all | solution.py:16
  (142 shorter events, 35.6 us)
Async XLA Ops:
  7.2 6.8 %copy-start = (bf16[256,1024]{1,0:T(8,128)(2,1)S(1)}, bf16[256,1024]{1,0:T(8,128)(2,1)}, u32[]{:S(2)}) copy-start(bf16[256,1024]{1,0:T(8,128)(2,1)} %param.14) | copy-start | bytes 1572868
  7.2 8.3 %copy-start.4 = (bf16[1024,512]{1,0:T(8,128)(2,1)S(1)}, bf16[1024,512]{1,0:T(8,128)(2,1)}, u32[]{:S(2)}) copy-start(bf16[1024,512]{1,0:T(8,128)(2,1)} %param.15) | copy-start | bytes 3145732
  7.2 117.3 %all-gather.3.cloned.1.call-start = ((), (), s32[]{:S(2)}) async-start(), calls=%async_computation.11 | async-start | bytes 2949120 | tf_op jit(solution)/shard_map/all_gather | solution.py:98
  11.5 4.5 %copy-start.8 = (s32[1,2]{1,0:T(1,128)S(1)}, s32[1,2]{1,0:T(1,128)}, u32[]{:S(2)}) copy-start(s32[1,2]{1,0:T(1,128)} %param.13) | copy-start | bytes 28
  12.3 4.5 %copy-start.7 = (bf16[1,256,128]{2,1,0:T(8,128)(2,1)S(1)}, bf16[1,256,128]{2,1,0:T(8,128)(2,1)}, u32[]{:S(2)}) copy-start(bf16[1,256,128]{2,1,0:T(8,128)(2,1)} %param.11) | copy-start | bytes 196612
  13.0 3.8 %copy-start.5 = (bf16[1,512,512]{2,1,0:T(8,128)(2,1)S(1)}, bf16[1,512,512]{2,1,0:T(8,128)(2,1)}, u32[]{:S(2)}) copy-start(bf16[1,512,512]{2,1,0:T(8,128)(2,1)} %param.12) | copy-start | bytes 1572868
  13.0 3.8 %copy-start.6 = (bf16[1,128,512]{2,1,0:T(8,128)(2,1)S(1)}, bf16[1,128,512]{2,1,0:T(8,128)(2,1)}, u32[]{:S(2)}) copy-start(bf16[1,128,512]{2,1,0:T(8,128)(2,1)} %param.10) | copy-start | bytes 393220
  70.5 0.7 copy-start.3
  71.9 52.5 %all-to-all-start.3 = ((bf16[4,32,512]{2,1,0:T(8,128)(2,1)}), bf16[4,32,512]{2,1,0:T(8,128)(2,1)S(1)}, u32[]{:S(2)}, u32[]{:S(2)}) async-start(bf16[4,32,512]{2,1,0:T(8,128)(2,1)} %broadcast_in_dim.18), calls=%async_computation.3 | async-start | bytes 262144 | tf_op jit(solution)/shard_map/all_to_all | solution.py:16
  128.5 18.9 %collective-permute-start.1 = (bf16[512,1024]{1,0:T(8,128)(2,1)S(1)}, bf16[512,1024]{1,0:T(8,128)(2,1)S(1)}, u32[]{:S(2)}, u32[]{:S(2)}) collective-permute-start(bf16[512,1024]{1,0:T(8,128)(2,1)S(1)} %bitcast.155), channel_id=1, source_target_pairs={{0,32},{32,0},{1,33},{33,1},{2,34},{34,2},{3,35},{35,3},{4,36},{36... | collective-permute-start | bytes 3145736 | tf_op jit(solution)/shard_map/ppermute | solution.py:126
  136.1 9.9 %all-to-all-start.4 = ((bf16[4,48,512]{2,1,0:T(8,128)(2,1)}), bf16[4,48,512]{2,1,0:T(8,128)(2,1)S(1)}, u32[]{:S(2)}, u32[]{:S(2)}) async-start(bf16[4,48,512]{2,1,0:T(8,128)(2,1)} %broadcast_in_dim.19), calls=%async_computation.4 | async-start | bytes 393216 | tf_op jit(solution)/shard_map/all_to_all | solution.py:16
  140.4 29.5 %collective-permute-start = (bf16[8,96,1024]{2,1,0:T(8,128)(2,1)}, bf16[8,96,1024]{2,1,0:T(8,128)(2,1)}, u32[]{:S(2)}, u32[]{:S(2)}) collective-permute-start(bf16[8,96,1024]{2,1,0:T(8,128)(2,1)} %slice.202), channel_id=1, source_target_pairs={{0,32},{32,0},{1,33},{33,1},{2,34},{34,2},{3,35},{35,3},{4,36},{36... | collective-permute-start | bytes 4718600 | tf_op jit(solution)/shard_map/ppermute | solution.py:149
  149.4 8.1 %all-to-all-start.5 = ((bf16[4,32,512]{2,1,0:T(8,128)(2,1)}), bf16[4,32,512]{2,1,0:T(8,128)(2,1)S(1)}, u32[]{:S(2)}, u32[]{:S(2)}) async-start(bf16[4,32,512]{2,1,0:T(8,128)(2,1)} %broadcast_in_dim.20), calls=%async_computation.5 | async-start | bytes 262144 | tf_op jit(solution)/shard_map/all_to_all | solution.py:16
  159.3 5.1 %copy-start.1 = (bf16[8,64,512]{2,1,0:T(8,128)(2,1)S(1)}, bf16[8,64,512]{2,1,0:T(8,128)(2,1)}, u32[]{:S(2)}) copy-start(bf16[8,64,512]{2,1,0:T(8,128)(2,1)} %get-tuple-element.50) | copy-start | bytes 1572868
  159.3 5.1 %copy-start.2 = (bf16[8,64,512]{2,1,0:T(8,128)(2,1)S(1)}, bf16[8,64,512]{2,1,0:T(8,128)(2,1)}, u32[]{:S(2)}) copy-start(bf16[8,64,512]{2,1,0:T(8,128)(2,1)} %get-tuple-element.51) | copy-start | bytes 1572868
  159.3 10.5 %all-to-all-start.6 = ((bf16[4,64,512]{2,1,0:T(8,128)(2,1)}), bf16[4,64,512]{2,1,0:T(8,128)(2,1)S(1)}, u32[]{:S(2)}, u32[]{:S(2)}) async-start(bf16[4,64,512]{2,1,0:T(8,128)(2,1)} %shard_map.78), calls=%async_computation.6 | async-start | bytes 524288 | tf_op jit(solution)/shard_map/all_to_all | solution.py:16
  220.3 8.9 %all-to-all-start.8 = ((bf16[4,32,1024]{2,1,0:T(8,128)(2,1)}), bf16[4,32,1024]{2,1,0:T(8,128)(2,1)S(1)}, u32[]{:S(2)}, u32[]{:S(2)}) async-start(bf16[4,32,1024]{2,1,0:T(8,128)(2,1)} %broadcast_in_dim.22), calls=%async_computation.8 | async-start | bytes 524288 | tf_op jit(solution)/shard_map/all_to_all | solution.py:16
  270.5 14.3 %all-to-all-start.10 = ((bf16[8,48,128]{2,1,0:T(8,128)(2,1)}), bf16[8,48,128]{2,1,0:T(8,128)(2,1)S(1)}, u32[]{:S(2)}, u32[]{:S(2)}) async-start(bf16[8,48,128]{2,1,0:T(8,128)(2,1)} %reshape.318), calls=%async_computation.10 | async-start | bytes 196608 | tf_op jit(solution)/shard_map/all_to_all | solution.py:16
Sparse Core Ops, SparseCore 0:
  14.9 108.5 all-gather.2

commit v4 on v2

--- a/solution.py
+++ b/solution.py
@@ -39,7 +39,8 @@
             side_ref[:, at] = side_ref[:, at] - upd_ref[k, :width, u * TILE:(u + 1) * TILE].astype(F32)
     out = dot(side_ref[:, :half].astype(BF), root_own[...], ((1,), (1,)))
     out = out + dot(side_ref[:, half:].astype(BF), root_oth[...], ((1,), (1,)))
-    out_ref[...] = out.astype(BF)
+    for k in range(Y):
+        out_ref[k] = out.astype(BF)
 
 
 def spread_kernel(slot_ref, parts_ref, root_own, root_oth, out_ref, sol_ref):
@@ -61,11 +62,49 @@
         out_ref[k, width:, :] = mine.astype(BF)
 
 
-def call(kernel, out_shape, scratch, n_in):
+def pack_kernel(inv_ref, panel_ref, out_ref):
+    n, lanes = inv_ref.shape
+    out_ref[:n] = inv_ref[...]
+    fold = lanes // TILE
+    few = panel_ref.shape[0] // fold
+    for f in range(fold):
+        out_ref[n:, f * TILE:(f + 1) * TILE] = panel_ref[f * few:(f + 1) * few]
+
+
+def correct_kernel(parts_ref, own_ref, oth_ref, out_ref):
+    picked = parts_ref[0].astype(F32)
+    for k in range(1, ZHI):
+        picked = picked + parts_ref[k].astype(F32)
+    picked = picked.astype(BF)
+    half = picked.shape[1] // 2
+    n, lanes = TILE, own_ref.shape[2]
+    for z in range(ZLO):
+        out = 0.0
+        for i, ref in enumerate((own_ref, oth_ref)):
+            panel = jnp.concatenate([ref[z, n:, f:f + TILE] for f in range(0, lanes, TILE)], axis=0)
+            out = out + dot(picked[:, i * half:(i + 1) * half], panel, ((1,), (0,)))
+        for k in range(Y):
+            out_ref[k, :, z * n:(z + 1) * n] = out.astype(BF)
+
+
+def solve_kernel(core_ref, forward_ref, parts_ref, own_ref, oth_ref, out_ref):
+    correction = parts_ref[0].astype(F32)
+    for k in range(1, Y):
+        correction = correction + parts_ref[k].astype(F32)
+    residue = forward_ref[...].astype(F32) - correction.astype(BF).astype(F32)
+    residue = residue.astype(BF)
+    n = TILE
+    core = core_ref[0]
+    for i, ref in enumerate((own_ref, oth_ref)):
+        inv = ref[:, :n, :].reshape(ZLO * n, ref.shape[2])
+        out_ref[(core + i) % CORE] = dot(inv, residue, ((0,), (1,))).astype(BF)
+
+
+def call(kernel, out_shape, scratch, n_in, n_scalar=1):
     return pl.pallas_call(
         kernel,
         out_shape=out_shape,
-        in_specs=[pl.BlockSpec(memory_space=pltpu.SMEM)]
+        in_specs=[pl.BlockSpec(memory_space=pltpu.SMEM)] * n_scalar
         + [pl.BlockSpec(memory_space=pltpu.VMEM)] * n_in,
         out_specs=jax.tree.map(lambda _: pl.BlockSpec(memory_space=pltpu.VMEM), out_shape),
         scratch_shapes=scratch,
@@ -78,24 +117,19 @@
     y, core = lax.axis_index("y"), lax.axis_index("core")
     leaf, zlo = lax.axis_index("leaf"), lax.axis_index("zlo")
     rows = root_rhs.shape[0]
+    other = [(0, 1), (1, 0)]
     half = rhs.shape[1] // CORE
     width = half // ZLO
     few = width // LEAF
 
-    def source(to_leaf, to_zlo, j):
-        return (to_zlo % LEAF) * ZLO + 2 * to_leaf + (j if to_zlo < LEAF else 1 - j)
-
-    root_own = [
-        lax.ppermute(
-            root_inv,
-            ("leaf", "zlo"),
-            [(source(t, s, j), t * ZLO + s) for t in range(LEAF) for s in range(ZLO)],
-        )
-        for j in range(2)
-    ]
     n = inv.shape[0]
-    packed = jnp.concatenate([inv[:, i:i + n] for i in range(0, inv.shape[1], n)] + [panel], axis=0)
-    packed = lax.all_gather(packed, ("core", "zlo"), axis=0, tiled=False)
+    part_rows = root_inv.shape[0] // LEAF
+    quarter = lax.dynamic_slice_in_dim(root_inv, leaf * part_rows, part_rows, axis=0)
+    root_own = lax.all_gather(quarter, "zlo", axis=0, tiled=True)
+    packed = call(
+        pack_kernel, jax.ShapeDtypeStruct((n + panel.size // inv.shape[1], inv.shape[1]), BF), [], 2, 0
+    )(inv, panel)
+    packed = lax.all_gather(packed, "zlo", axis=0, tiled=False)
 
     part = dot(rhs, inv, ((0,), (1,))).astype(BF).reshape(CORE, half, n)
     chunk = lax.dynamic_slice_in_dim(
@@ -122,8 +156,7 @@
     update = total(both[:, :, :span]).astype(BF)
     update = total(share(update, "zhi", ZHI)).astype(BF)
     root_own, update = lax.optimization_barrier((root_own, update))
-    root_own = jnp.concatenate(root_own, axis=0)
-    root_oth = lax.ppermute(root_own, "core", [(0, 1), (1, 0)])
+    root_oth = lax.ppermute(root_own, "core", other)
     names = jnp.zeros((16, span), BF).at[:, :4].set(anc_y[None])
     update = share(jnp.concatenate([update, names], axis=0), "leaf", LEAF)
     slots = update[:, width, :4].reshape(-1).astype(jnp.int32)
@@ -131,31 +164,28 @@
 
     root_part = call(
         place_kernel,
-        jax.ShapeDtypeStruct((width, root_own.shape[0]), BF),
+        jax.ShapeDtypeStruct((Y, width, root_own.shape[0]), BF),
         [pltpu.VMEM((width, 2 * rows), F32)],
         5,
     )(slots, update, side_own, side_oth, root_own, root_oth)
+    packed, root_part = lax.optimization_barrier((packed, root_part))
+    packed_oth = lax.ppermute(packed, "core", other)
+    pairs = slots.reshape(LEAF, CORE, 2)
+    pairs = jnp.where(core == 0, pairs, pairs[:, ::-1]).reshape(-1)
     sol = call(
         spread_kernel,
         jax.ShapeDtypeStruct((LEAF, 2 * width, span), BF),
         [pltpu.VMEM((width, 2 * rows), F32)],
         3,
-    )(slots, share(root_part, "y", Y), root_own, root_oth)
+    )(pairs, exchange(root_part, "y"), root_own, root_oth)
     sol = total(exchange(sol, "leaf")).astype(BF)
     picked, root = sol[:width], sol[width:]
-    packed, picked = lax.optimization_barrier((packed, picked))
-    inv_all = packed[:, :inv.size // n].reshape(CORE, ZLO, -1, n, n)
-    inv_all = jnp.transpose(inv_all, (0, 1, 3, 2, 4)).reshape(CORE, ZLO * n, inv.shape[1])
-    panel_all = packed[:, inv.size // n:].reshape(CORE, ZLO, -1, n)
-    panel_all = jnp.transpose(panel_all, (1, 0, 2, 3)).reshape(ZLO, -1, n)
-    picked = total(share(picked, "zhi", ZHI)).astype(BF)
-
-    correction = jnp.concatenate(
-        [dot(picked, panel_all[z], ((1,), (0,))) for z in range(ZLO)], axis=1
-    ).astype(BF)
-    correction = total(share(correction, "y", Y)).astype(BF)
-    residue = (forward_all.astype(F32) - correction.astype(F32)).astype(BF)
-    child = jnp.stack([dot(inv_all[c], residue, ((0,), (1,))) for c in range(CORE)]).astype(BF)
+    correction = call(
+        correct_kernel, jax.ShapeDtypeStruct((Y, width, ZLO * n), BF), [], 3, 0
+    )(share(picked, "zhi", ZHI), packed, packed_oth)
+    child = call(
+        solve_kernel, jax.ShapeDtypeStruct((CORE, inv.shape[1], width), BF), [], 4
+    )(jnp.array([core], jnp.int32), forward_all, exchange(correction, "y"), packed, packed_oth)
 
     cols = ZHI * ZLO
     child = jnp.transpose(child.reshape(CORE, cols, -1, width), (1, 0, 2, 3)).reshape(cols, -1)

time: 366 us -> 330 us (0.902)
  starting transfers between devices: 77.4 us -> 59.5 us
  local copies, waits for them, and re-layouts: 26 us -> 11.9 us
  waiting for transfers between devices: 131 us -> 123 us
  Pallas kernels: 2.31 us -> 8.25 us
  matrix products: 4.36 us -> 0.58 us
    ppermute x3 -> x2, waiting for transfers between devices: 93.5 us -> 0.01 us  [the longest x1 0.01 us: body(): root_oth = lax.ppermute(root_own, 'core', other)]
    all_gather x1 -> x2, waiting for transfers between devices: 0.02 us -> 62.9 us  [the longest x1 60.1 us: body(): packed = lax.all_gather(packed, 'zlo', axis=0, tiled=False)]
    all_to_all x5 -> x7, waiting for transfers between devices: 37 us -> 60.2 us  [exchange(): return lax.all_to_all(x, axis, 0, 0, tiled=True)]
    all_to_all x5 -> x7, starting transfers between devices: 63.4 us -> 43.7 us  [exchange(): return lax.all_to_all(x, axis, 0, 0, tiled=True)]
    slice x6 -> x0, local copies, waits for them, and re-layouts: 7.73 us -> none  [the longest x1 3.16 us: body(): inv_all = packed[:, :inv.size // n].reshape(CORE, ZLO, -1, n, n)]
    pallas_call x1 -> x4, Pallas kernels: 1.27 us -> 7.21 us  [the longest x1 2.38 us: body(): call(correct_kernel, jax.ShapeDtypeStruct((Y, width, ZLO * n), BF), [], 3...]
    dot_general x12 -> x2, matrix products: 4.36 us -> 0.58 us  [dot(): lax.dot_general(a, b, (contract, ((), ())), preferred_element_type=F32)]
    all_to_all x6 -> x4, blocking collectives: 104 us -> 107 us  [exchange(): return lax.all_to_all(x, axis, 0, 0, tiled=True)]
  transfers between devices with their start and end apart: 9 -> 11, of which waited for: 6 -> 9; matrix products, arithmetic and copies ran while one was open for 6% -> 3% of each run, Pallas kernels for 1% -> 1%
where the time goes in v4:
time: 330 us; the launch traced here: 329 us
  waiting for transfers between devices  123 us (37%)
  blocking collectives  107 us (32%)
  starting transfers between devices  59.5 us (18%)
  between operations  14.5 us (4%)
  local copies, waits for them, and re-layouts  11.9 us (4%)
  Pallas kernels  8.25 us (2%)
  other arithmetic  4.35 us (1%)
    all_to_all x4, blocking collectives, exchange(): return lax.all_to_all(x, axis, 0, 0, tiled=True)  107 us
    all_to_all x7, waiting for transfers between devices, exchange(): return lax.all_to_all(x, axis, 0, 0, tiled=True)  60.2 us
    all_gather x1, waiting for transfers between devices, body(): packed = lax.all_gather(packed, 'zlo', axis=0, tiled=False)  60.1 us
    all_to_all x7, starting transfers between devices, exchange(): return lax.all_to_all(x, axis, 0, 0, tiled=True)  43.7 us
    ppermute x1, starting transfers between devices, body(): packed_oth = lax.ppermute(packed, 'core', other)  9.13 us
    ppermute x1, starting transfers between devices, body(): root_oth = lax.ppermute(root_own, 'core', other)  6.66 us
  transfers between devices with their start and end apart: 11, of which 9 were waited for; matrix products, arithmetic and copies ran while one was open for 3% of the time, Pallas kernels for 1%

profile of v4, /device:TPU:1, one launch (start us, length us, event | category | flops | bytes accessed | tf_op | source)
XLA Modules:
  0.0 329.2 jit_solution(11609559243460397016)
XLA Ops:
  10.6 17.8 %all_to_all.55 = bf16[2,784,128]{2,1,0:T(8,128)(2,1)S(1)} all-to-all(bf16[2,784,128]{2,1,0:T(8,128)(2,1)S(1)} %pad_maximum_fusion), channel_id=1, replica_groups=mesh['leaf'=4,'y'=4,'core'=2,'zhi'=4,'zlo'=8] {'core'}, dimensions={0} | all-to-all | bytes 802816 | tf_op jit(solution)/shard_map/all_to_all | solution.py:16
  29.1 3.4 %all-to-all-start.1 = ((bf16[4,256,128]{2,1,0:T(8,128)(2,1)}), bf16[4,256,128]{2,1,0:T(8,128)(2,1)S(1)}, u32[]{:S(2)}, u32[]{:S(2)}) async-start(bf16[4,256,128]{2,1,0:T(8,128)(2,1)} %broadcast_in_dim.16), calls=%async_computation.1 | async-start | bytes 524288 | tf_op jit(solution)/shard_map/all_to_all | solution.py:16
  34.2 4.5 %all-to-all-done.1 = bf16[4,256,128]{2,1,0:T(8,128)(2,1)S(1)} async-done(((bf16[4,256,128]{2,1,0:T(8,128)(2,1)}), bf16[4,256,128]{2,1,0:T(8,128)(2,1)S(1)}, u32[]{:S(2)}, u32[]{:S(2)}) %all-to-all-start.1) | async-done | bytes 262176 | tf_op jit(solution)/shard_map/all_to_all | solution.py:16
  39.7 3.4 %all-to-all-start.2 = ((bf16[8,32,640]{2,1,0:T(8,128)(2,1)}), bf16[8,32,640]{2,1,0:T(8,128)(2,1)S(1)}, u32[]{:S(2)}, u32[]{:S(2)}) async-start(bf16[8,32,640]{2,1,0:T(8,128)(2,1)} %bitcast.10), calls=%async_computation.2 | async-start | bytes 655360 | tf_op jit(solution)/shard_map/all_to_all | solution.py:16
  43.9 14.8 %all-to-all-done.2 = bf16[8,32,640]{2,1,0:T(8,128)(2,1)S(1)} async-done(((bf16[8,32,640]{2,1,0:T(8,128)(2,1)}), bf16[8,32,640]{2,1,0:T(8,128)(2,1)S(1)}, u32[]{:S(2)}, u32[]{:S(2)}) %all-to-all-start.2) | async-done | bytes 327712 | tf_op jit(solution)/shard_map/all_to_all | solution.py:16
  58.8 45.3 %all_to_all.56 = bf16[4,32,512]{2,1,0:T(8,128)(2,1)S(1)} all-to-all(bf16[4,32,512]{2,1,0:T(8,128)(2,1)S(1)} %broadcast_in_dim.17), channel_id=1, replica_groups=mesh['leaf'=4,'y'=4,'core'=2,'zhi'=4,'zlo'=8] {'zhi'}, dimensions={0} | all-to-all | bytes 262144 | tf_op jit(solution)/shard_map/all_to_all | solution.py:16
  104.2 2.8 all-gather.4.cloned.1.call-done.root_own
  107.0 6.7 %collective-permute-start = (bf16[512,1024]{1,0:T(8,128)(2,1)}, bf16[512,1024]{1,0:T(8,128)(2,1)S(1)}, u32[]{:S(2)}, u32[]{:S(2)}) collective-permute-start(bf16[512,1024]{1,0:T(8,128)(2,1)} %all-gather.4.cloned.1.call-done.root_own), channel_id=1, source_target_pairs={{0,32},{32,0},{1,33},{33,1},{2,34},{34,2},{3,35},{35,3},{4,36},{36... | collective-permute-start | bytes 3145736 | tf_op jit(solution)/shard_map/ppermute | solution.py:159
  115.8 4.0 %all-to-all-start.4 = ((bf16[4,48,512]{2,1,0:T(8,128)(2,1)}), bf16[4,48,512]{2,1,0:T(8,128)(2,1)S(1)}, u32[]{:S(2)}, u32[]{:S(2)}) async-start(bf16[4,48,512]{2,1,0:T(8,128)(2,1)} %broadcast_in_dim.18), calls=%async_computation.4 | async-start | bytes 393216 | tf_op jit(solution)/shard_map/all_to_all | solution.py:16
  119.8 5.4 %all-to-all-done.4.upd_ref = bf16[4,48,512]{2,1,0:T(8,128)(2,1)S(1)} async-done(((bf16[4,48,512]{2,1,0:T(8,128)(2,1)}), bf16[4,48,512]{2,1,0:T(8,128)(2,1)S(1)}, u32[]{:S(2)}, u32[]{:S(2)}) %all-to-all-start.4) | async-done | bytes 196640 | tf_op jit(solution)/shard_map/all_to_all | solution.py:16
  128.6 60.1 %all-gather.6.cloned.1.call-done = bf16[1536,512]{1,0:T(8,128)(2,1)} async-done(((bf16[192,512]{1,0:T(8,128)(2,1)}), bf16[1536,512]{1,0:T(8,128)(2,1)}) %all-gather.6.cloned.1.call-update) | async-done | bytes 1572880 | tf_op jit(solution)/shard_map/all_gather | solution.py:132
  188.7 9.1 %collective-permute-start.1 = (bf16[8,192,512]{2,1,0:T(8,128)(2,1)}, bf16[8,192,512]{2,1,0:T(8,128)(2,1)}, u32[]{:S(2)}, u32[]{:S(2)}) collective-permute-start(bf16[8,192,512]{2,1,0:T(8,128)(2,1)} %bitcast.56), channel_id=1, source_target_pairs={{0,32},{32,0},{1,33},{33,1},{2,34},{34,2},{3,35},{35,3},{4,36},{36... | collective-permute-start | bytes 4718600 | tf_op jit(solution)/shard_map/ppermute | solution.py:172
  197.8 3.5 %all-to-all-start.5 = ((bf16[4,32,512]{2,1,0:T(8,128)(2,1)}), bf16[4,32,512]{2,1,0:T(8,128)(2,1)S(1)}, u32[]{:S(2)}, u32[]{:S(2)}) async-start(bf16[4,32,512]{2,1,0:T(8,128)(2,1)} %shard_map.78), calls=%async_computation.5 | async-start | bytes 262144 | tf_op jit(solution)/shard_map/all_to_all | solution.py:16
  201.6 4.7 %all-to-all-done.5.parts_ref = bf16[4,32,512]{2,1,0:T(8,128)(2,1)S(1)} async-done(((bf16[4,32,512]{2,1,0:T(8,128)(2,1)}), bf16[4,32,512]{2,1,0:T(8,128)(2,1)S(1)}, u32[]{:S(2)}, u32[]{:S(2)}) %all-to-all-start.5) | async-done | bytes 131104 | tf_op jit(solution)/shard_map/all_to_all | solution.py:16
  208.5 9.4 %all_to_all.57 = bf16[4,64,512]{2,1,0:T(8,128)(2,1)S(1)} all-to-all(bf16[4,64,512]{2,1,0:T(8,128)(2,1)S(1)} %shard_map.79), channel_id=1, replica_groups=mesh['leaf'=4,'y'=4,'core'=2,'zhi'=4,'zlo'=8] {'leaf'}, dimensions={0} | all-to-all | bytes 524288 | tf_op jit(solution)/shard_map/all_to_all | solution.py:16
  218.6 16.0 %all-to-all-start.7 = ((bf16[4,32,512]{2,1,0:T(8,128)(2,1)}), bf16[4,32,512]{2,1,0:T(8,128)(2,1)S(1)}, u32[]{:S(2)}, u32[]{:S(2)}) async-start(bf16[4,32,512]{2,1,0:T(8,128)(2,1)} %broadcast_in_dim.19), calls=%async_computation.7 | async-start | bytes 262144 | tf_op jit(solution)/shard_map/all_to_all | solution.py:16
  235.5 20.9 %all-to-all-done.7.parts_ref = bf16[4,32,512]{2,1,0:T(8,128)(2,1)S(1)} async-done(((bf16[4,32,512]{2,1,0:T(8,128)(2,1)}), bf16[4,32,512]{2,1,0:T(8,128)(2,1)S(1)}, u32[]{:S(2)}, u32[]{:S(2)}) %all-to-all-start.7) | async-done | bytes 131104 | tf_op jit(solution)/shard_map/all_to_all | solution.py:16
  256.4 2.4 shard_map.80
  258.8 3.4 %all-to-all-start.8 = ((bf16[4,32,1024]{2,1,0:T(8,128)(2,1)}), bf16[4,32,1024]{2,1,0:T(8,128)(2,1)S(1)}, u32[]{:S(2)}, u32[]{:S(2)}) async-start(bf16[4,32,1024]{2,1,0:T(8,128)(2,1)} %shard_map.80), calls=%async_computation.8 | async-start | bytes 524288 | tf_op jit(solution)/shard_map/all_to_all | solution.py:16
  262.7 5.0 %all-to-all-done.8.parts_ref = bf16[4,32,1024]{2,1,0:T(8,128)(2,1)S(1)} async-done(((bf16[4,32,1024]{2,1,0:T(8,128)(2,1)}), bf16[4,32,1024]{2,1,0:T(8,128)(2,1)S(1)}, u32[]{:S(2)}, u32[]{:S(2)}) %all-to-all-start.8) | async-done | bytes 262176 | tf_op jit(solution)/shard_map/all_to_all | solution.py:16
  267.7 2.1 shard_map.81
  270.2 34.4 %all_to_all.58 = bf16[32,12,128]{2,1,0:T(8,128)(2,1)S(1)} all-to-all(bf16[32,12,128]{2,1,0:T(8,128)(2,1)S(1)} %reshape.216), channel_id=1, replica_groups=mesh['leaf'=4,'y'=4,'core'=2,'zhi'=4,'zlo'=8] {'zhi','zlo'}, dimensions={0} | all-to-all | bytes 196608 | tf_op jit(solution)/shard_map/all_to_all | solution.py:16
  305.6 9.9 %all-to-all-start.10 = ((bf16[8,48,128]{2,1,0:T(8,128)(2,1)}), bf16[8,48,128]{2,1,0:T(8,128)(2,1)S(1)}, u32[]{:S(2)}, u32[]{:S(2)}) async-start(bf16[8,48,128]{2,1,0:T(8,128)(2,1)} %reshape.222), calls=%async_computation.10 | async-start | bytes 196608 | tf_op jit(solution)/shard_map/all_to_all | solution.py:16
  315.5 5.0 %all-to-all-done.10 = bf16[8,48,128]{2,1,0:T(8,128)(2,1)S(1)} async-done(((bf16[8,48,128]{2,1,0:T(8,128)(2,1)}), bf16[8,48,128]{2,1,0:T(8,128)(2,1)S(1)}, u32[]{:S(2)}, u32[]{:S(2)}) %all-to-all-start.10) | async-done | bytes 98336 | tf_op jit(solution)/shard_map/all_to_all | solution.py:16
  (101 shorter events, 20.7 us)
Async XLA Ops:
  7.2 3.0 copy-start
  7.2 2.3 copy-start.8
  7.2 2.9 copy-start.6
  7.2 3.0 copy-start.5
  29.1 9.5 %all-to-all-start.1 = ((bf16[4,256,128]{2,1,0:T(8,128)(2,1)}), bf16[4,256,128]{2,1,0:T(8,128)(2,1)S(1)}, u32[]{:S(2)}, u32[]{:S(2)}) async-start(bf16[4,256,128]{2,1,0:T(8,128)(2,1)} %broadcast_in_dim.16), calls=%async_computation.1 | async-start | bytes 524288 | tf_op jit(solution)/shard_map/all_to_all | solution.py:16
  32.6 74.4 %all-gather.4.cloned.1.call-start = ((), (), s32[]{:S(2)}) async-start(), calls=%async_computation.11 | async-start | bytes 1179648 | tf_op jit(solution)/shard_map/all_gather | solution.py:128
  39.7 19.1 %all-to-all-start.2 = ((bf16[8,32,640]{2,1,0:T(8,128)(2,1)}), bf16[8,32,640]{2,1,0:T(8,128)(2,1)S(1)}, u32[]{:S(2)}, u32[]{:S(2)}) async-start(bf16[8,32,640]{2,1,0:T(8,128)(2,1)} %bitcast.10), calls=%async_computation.2 | async-start | bytes 655360 | tf_op jit(solution)/shard_map/all_to_all | solution.py:16
  43.1 145.5 %all-gather.6.cloned.1.call-start = ((), (), s32[]{:S(2)}) async-start(), calls=%async_computation.12 | async-start | bytes 1769472 | tf_op jit(solution)/shard_map/all_gather | solution.py:132
  58.7 45.4 %copy-start.7 = (bf16[8,32,640]{2,1,0:T(8,128)(2,1)}, bf16[8,32,640]{2,1,0:T(8,128)(2,1)S(1)}, u32[]{:S(2)}) copy-start(bf16[8,32,640]{2,1,0:T(8,128)(2,1)S(1)} %all-to-all-done.2) | copy-start | bytes 983044
  107.0 19.6 %copy-start.2 = (bf16[512,1024]{1,0:T(8,128)(2,1)S(1)}, bf16[512,1024]{1,0:T(8,128)(2,1)}, u32[]{:S(2)}) copy-start(bf16[512,1024]{1,0:T(8,128)(2,1)} %all-gather.4.cloned.1.call-done.root_own) | copy-start | bytes 3145732
  107.0 19.6 %collective-permute-start = (bf16[512,1024]{1,0:T(8,128)(2,1)}, bf16[512,1024]{1,0:T(8,128)(2,1)S(1)}, u32[]{:S(2)}, u32[]{:S(2)}) collective-permute-start(bf16[512,1024]{1,0:T(8,128)(2,1)} %all-gather.4.cloned.1.call-done.root_own), channel_id=1, source_target_pairs={{0,32},{32,0},{1,33},{33,1},{2,34},{34,2},{3,35},{35,3},{4,36},{36... | collective-permute-start | bytes 3145736 | tf_op jit(solution)/shard_map/ppermute | solution.py:159
  115.8 9.5 %all-to-all-start.4 = ((bf16[4,48,512]{2,1,0:T(8,128)(2,1)}), bf16[4,48,512]{2,1,0:T(8,128)(2,1)S(1)}, u32[]{:S(2)}, u32[]{:S(2)}) async-start(bf16[4,48,512]{2,1,0:T(8,128)(2,1)} %broadcast_in_dim.18), calls=%async_computation.4 | async-start | bytes 393216 | tf_op jit(solution)/shard_map/all_to_all | solution.py:16
  126.6 74.8 %copy-start.3 = (bf16[512,1024]{1,0:T(8,128)(2,1)}, bf16[512,1024]{1,0:T(8,128)(2,1)S(1)}, u32[]{:S(2)}) copy-start(bf16[512,1024]{1,0:T(8,128)(2,1)S(1)} %collective-permute-done.root_oth) | copy-start | bytes 3145732
  188.7 67.7 %collective-permute-start.1 = (bf16[8,192,512]{2,1,0:T(8,128)(2,1)}, bf16[8,192,512]{2,1,0:T(8,128)(2,1)}, u32[]{:S(2)}, u32[]{:S(2)}) collective-permute-start(bf16[8,192,512]{2,1,0:T(8,128)(2,1)} %bitcast.56), channel_id=1, source_target_pairs={{0,32},{32,0},{1,33},{33,1},{2,34},{34,2},{3,35},{35,3},{4,36},{36... | collective-permute-start | bytes 4718600 | tf_op jit(solution)/shard_map/ppermute | solution.py:172
  197.8 8.4 %all-to-all-start.5 = ((bf16[4,32,512]{2,1,0:T(8,128)(2,1)}), bf16[4,32,512]{2,1,0:T(8,128)(2,1)S(1)}, u32[]{:S(2)}, u32[]{:S(2)}) async-start(bf16[4,32,512]{2,1,0:T(8,128)(2,1)} %shard_map.78), calls=%async_computation.5 | async-start | bytes 262144 | tf_op jit(solution)/shard_map/all_to_all | solution.py:16
  201.6 54.8 %copy-start.1 = (bf16[1536,512]{1,0:T(8,128)(2,1)S(1)}, bf16[1536,512]{1,0:T(8,128)(2,1)}, u32[]{:S(2)}) copy-start(bf16[1536,512]{1,0:T(8,128)(2,1)} %all-gather.6.cloned.1.call-done) | copy-start | bytes 4718596
  206.2 1.2 copy-start.4
  218.6 37.8 %all-to-all-start.7 = ((bf16[4,32,512]{2,1,0:T(8,128)(2,1)}), bf16[4,32,512]{2,1,0:T(8,128)(2,1)S(1)}, u32[]{:S(2)}, u32[]{:S(2)}) async-start(bf16[4,32,512]{2,1,0:T(8,128)(2,1)} %broadcast_in_dim.19), calls=%async_computation.7 | async-start | bytes 262144 | tf_op jit(solution)/shard_map/all_to_all | solution.py:16
  258.8 8.9 %all-to-all-start.8 = ((bf16[4,32,1024]{2,1,0:T(8,128)(2,1)}), bf16[4,32,1024]{2,1,0:T(8,128)(2,1)S(1)}, u32[]{:S(2)}, u32[]{:S(2)}) async-start(bf16[4,32,1024]{2,1,0:T(8,128)(2,1)} %shard_map.80), calls=%async_computation.8 | async-start | bytes 524288 | tf_op jit(solution)/shard_map/all_to_all | solution.py:16
  305.6 14.9 %all-to-all-start.10 = ((bf16[8,48,128]{2,1,0:T(8,128)(2,1)}), bf16[8,48,128]{2,1,0:T(8,128)(2,1)S(1)}, u32[]{:S(2)}, u32[]{:S(2)}) async-start(bf16[8,48,128]{2,1,0:T(8,128)(2,1)} %reshape.222), calls=%async_computation.10 | async-start | bytes 196608 | tf_op jit(solution)/shard_map/all_to_all | solution.py:16
Sparse Core Ops, SparseCore 0:
  36.1 70.8 all-gather.3
  109.6 78.9 all-gather.5

commit v5 on v4

--- a/solution.py
+++ b/solution.py
@@ -28,8 +28,29 @@
     return lax.dot_general(a, b, (contract, ((), ())), preferred_element_type=F32)
 
 
-def place_kernel(slot_ref, upd_ref, rhs_own, rhs_oth, root_own, root_oth, out_ref, side_ref):
+QUARTER, INV = 64, 128
+
+
+def pack_kernel(leaf_ref, root_ref, inv_ref, panel_ref, out_ref):
+    lanes = inv_ref.shape[1]
+    at = pl.ds(pl.multiple_of(leaf_ref[0] * QUARTER, QUARTER), QUARTER)
+    out_ref[:QUARTER] = root_ref[at, :lanes]
+    out_ref[QUARTER:2 * QUARTER] = root_ref[at, lanes:]
+    start = 2 * QUARTER
+    out_ref[start:start + INV] = inv_ref[...]
+    fold = lanes // TILE
+    few = panel_ref.shape[0] // fold
+    for f in range(fold):
+        out_ref[start + INV:, f * TILE:(f + 1) * TILE] = panel_ref[f * few:(f + 1) * few]
+
+
+def root_half(ref, j):
+    return ref[:, j * QUARTER:(j + 1) * QUARTER, :].reshape(ZLO * QUARTER, ref.shape[2])
+
+
+def place_kernel(slot_ref, upd_ref, rhs_own, rhs_oth, own_ref, oth_ref, out_ref, side_ref):
     half = rhs_own.shape[1]
+    lanes = own_ref.shape[2]
     side_ref[:, :half] = rhs_own[...].astype(F32)
     side_ref[:, half:] = rhs_oth[...].astype(F32)
     width = side_ref.shape[0]
@@ -37,20 +58,23 @@
         for u in range(4):
             at = pl.ds(pl.multiple_of(slot_ref[k * 4 + u] * TILE, TILE), TILE)
             side_ref[:, at] = side_ref[:, at] - upd_ref[k, :width, u * TILE:(u + 1) * TILE].astype(F32)
-    out = dot(side_ref[:, :half].astype(BF), root_own[...], ((1,), (1,)))
-    out = out + dot(side_ref[:, half:].astype(BF), root_oth[...], ((1,), (1,)))
+    out = 0.0
+    for i in range(4):
+        side = side_ref[:, i * lanes:(i + 1) * lanes].astype(BF)
+        out = out + dot(side, root_half((own_ref, oth_ref)[i // 2], i % 2), ((1,), (1,)))
     for k in range(Y):
         out_ref[k] = out.astype(BF)
 
 
-def spread_kernel(slot_ref, parts_ref, root_own, root_oth, out_ref, sol_ref):
-    half = root_own.shape[1]
+def spread_kernel(slot_ref, parts_ref, own_ref, oth_ref, out_ref, sol_ref):
+    lanes = own_ref.shape[2]
     forward = parts_ref[0].astype(F32)
     for k in range(1, Y):
         forward = forward + parts_ref[k].astype(F32)
     forward = forward.astype(BF)
-    sol_ref[:, :half] = dot(forward, root_own[...], ((1,), (0,)))
-    sol_ref[:, half:] = dot(forward, root_oth[...], ((1,), (0,)))
+    for i in range(4):
+        root = root_half((own_ref, oth_ref)[i // 2], i % 2)
+        sol_ref[:, i * lanes:(i + 1) * lanes] = dot(forward, root, ((1,), (0,)))
     width, span = forward.shape[0], 4 * TILE
     few = width // LEAF
     for k in range(LEAF):
@@ -62,15 +86,6 @@
         out_ref[k, width:, :] = mine.astype(BF)
 
 
-def pack_kernel(inv_ref, panel_ref, out_ref):
-    n, lanes = inv_ref.shape
-    out_ref[:n] = inv_ref[...]
-    fold = lanes // TILE
-    few = panel_ref.shape[0] // fold
-    for f in range(fold):
-        out_ref[n:, f * TILE:(f + 1) * TILE] = panel_ref[f * few:(f + 1) * few]
-
-
 def correct_kernel(parts_ref, own_ref, oth_ref, out_ref):
     picked = parts_ref[0].astype(F32)
     for k in range(1, ZHI):
@@ -78,10 +93,11 @@
     picked = picked.astype(BF)
     half = picked.shape[1] // 2
     n, lanes = TILE, own_ref.shape[2]
+    start = 2 * QUARTER + INV
     for z in range(ZLO):
         out = 0.0
         for i, ref in enumerate((own_ref, oth_ref)):
-            panel = jnp.concatenate([ref[z, n:, f:f + TILE] for f in range(0, lanes, TILE)], axis=0)
+            panel = jnp.concatenate([ref[z, start:, f:f + TILE] for f in range(0, lanes, TILE)], axis=0)
             out = out + dot(picked[:, i * half:(i + 1) * half], panel, ((1,), (0,)))
         for k in range(Y):
             out_ref[k, :, z * n:(z + 1) * n] = out.astype(BF)
@@ -96,7 +112,7 @@
     n = TILE
     core = core_ref[0]
     for i, ref in enumerate((own_ref, oth_ref)):
-        inv = ref[:, :n, :].reshape(ZLO * n, ref.shape[2])
+        inv = ref[:, 2 * QUARTER:2 * QUARTER + n, :].reshape(ZLO * n, ref.shape[2])
         out_ref[(core + i) % CORE] = dot(inv, residue, ((0,), (1,))).astype(BF)
 
 
@@ -123,12 +139,10 @@
     few = width // LEAF
 
     n = inv.shape[0]
-    part_rows = root_inv.shape[0] // LEAF
-    quarter = lax.dynamic_slice_in_dim(root_inv, leaf * part_rows, part_rows, axis=0)
-    root_own = lax.all_gather(quarter, "zlo", axis=0, tiled=True)
-    packed = call(
-        pack_kernel, jax.ShapeDtypeStruct((n + panel.size // inv.shape[1], inv.shape[1]), BF), [], 2, 0
-    )(inv, panel)
+    packed_rows = 2 * QUARTER + INV + panel.size // inv.shape[1]
+    packed = call(pack_kernel, jax.ShapeDtypeStruct((packed_rows, inv.shape[1]), BF), [], 3)(
+        jnp.array([leaf], jnp.int32), root_inv, inv, panel
+    )
     packed = lax.all_gather(packed, "zlo", axis=0, tiled=False)
 
     part = dot(rhs, inv, ((0,), (1,))).astype(BF).reshape(CORE, half, n)
@@ -155,8 +169,8 @@
     forward_all = jnp.transpose(both[:, :, span:], (1, 0, 2)).reshape(width, -1)
     update = total(both[:, :, :span]).astype(BF)
     update = total(share(update, "zhi", ZHI)).astype(BF)
-    root_own, update = lax.optimization_barrier((root_own, update))
-    root_oth = lax.ppermute(root_own, "core", other)
+    packed, update = lax.optimization_barrier((packed, update))
+    packed_oth = lax.ppermute(packed, "core", other)
     names = jnp.zeros((16, span), BF).at[:, :4].set(anc_y[None])
     update = share(jnp.concatenate([update, names], axis=0), "leaf", LEAF)
     slots = update[:, width, :4].reshape(-1).astype(jnp.int32)
@@ -164,12 +178,10 @@
 
     root_part = call(
         place_kernel,
-        jax.ShapeDtypeStruct((Y, width, root_own.shape[0]), BF),
+        jax.ShapeDtypeStruct((Y, width, ZLO * QUARTER), BF),
         [pltpu.VMEM((width, 2 * rows), F32)],
         5,
-    )(slots, update, side_own, side_oth, root_own, root_oth)
-    packed, root_part = lax.optimization_barrier((packed, root_part))
-    packed_oth = lax.ppermute(packed, "core", other)
+    )(slots, update, side_own, side_oth, packed, packed_oth)
     pairs = slots.reshape(LEAF, CORE, 2)
     pairs = jnp.where(core == 0, pairs, pairs[:, ::-1]).reshape(-1)
     sol = call(
@@ -177,7 +189,7 @@
         jax.ShapeDtypeStruct((LEAF, 2 * width, span), BF),
         [pltpu.VMEM((width, 2 * rows), F32)],
         3,
-    )(pairs, exchange(root_part, "y"), root_own, root_oth)
+    )(pairs, exchange(root_part, "y"), packed, packed_oth)
     sol = total(exchange(sol, "leaf")).astype(BF)
     picked, root = sol[:width], sol[width:]
     correction = call(

time: 330 us -> 282 us (0.85)
  waiting for transfers between devices: 123 us -> 35.7 us
  blocking collectives: 107 us -> 150 us
  starting transfers between devices: 59.5 us -> 41.8 us
  local copies, waits for them, and re-layouts: 11.9 us -> 26.4 us
  Pallas kernels: 8.25 us -> 4.77 us
    all_gather x1, waiting for transfers between devices: 60.1 us -> 0.01 us  [body(): packed = lax.all_gather(packed, 'zlo', axis=0, tiled=False)]
    all_to_all x4 -> x6, blocking collectives: 107 us -> 150 us  [exchange(): return lax.all_to_all(x, axis, 0, 0, tiled=True)]
    all_to_all x7 -> x5, waiting for transfers between devices: 60.2 us -> 35.7 us  [exchange(): return lax.all_to_all(x, axis, 0, 0, tiled=True)]
    unnamed x22 -> x38, local copies, waits for them, and re-layouts: 3.47 us -> 16.7 us
    all_to_all x7 -> x5, starting transfers between devices: 43.7 us -> 34.3 us  [exchange(): return lax.all_to_all(x, axis, 0, 0, tiled=True)]
    ppermute x1 -> x0, starting transfers between devices: 6.66 us -> none  [body(): root_oth = lax.ppermute(root_own, 'core', other)]
  transfers between devices with their start and end apart: 11 -> 7, of which waited for: 9 -> 5; matrix products, arithmetic and copies ran while one was open for 3% -> 5% of each run, Pallas kernels for 1% -> 0%
where the time goes in v5:
time: 282 us; the launch traced here: 281 us
  blocking collectives  150 us (53%)
  starting transfers between devices  41.8 us (15%)
  waiting for transfers between devices  35.7 us (13%)
  local copies, waits for them, and re-layouts  26.4 us (9%)
  between operations  14.5 us (5%)
  other arithmetic  6.69 us (2%)
  Pallas kernels  4.77 us (2%)
    all_to_all x6, blocking collectives, exchange(): return lax.all_to_all(x, axis, 0, 0, tiled=True)  150 us
    all_to_all x5, waiting for transfers between devices, exchange(): return lax.all_to_all(x, axis, 0, 0, tiled=True)  35.7 us
    all_to_all x5, starting transfers between devices, exchange(): return lax.all_to_all(x, axis, 0, 0, tiled=True)  34.3 us
    unnamed x38, local copies, waits for them, and re-layouts  16.7 us
    ppermute x1, starting transfers between devices, body(): packed_oth = lax.ppermute(packed, 'core', other)  7.54 us
  transfers between devices with their start and end apart: 7, of which 5 were waited for; matrix products, arithmetic and copies ran while one was open for 5% of the time, Pallas kernels for 0%

profile of v5, /device:TPU:1, one launch (start us, length us, event | category | flops | bytes accessed | tf_op | source)
XLA Modules:
  0.0 280.6 jit_solution(15303778201471533688)
XLA Ops:
  11.5 1.5 copy.42
  14.2 17.8 %all_to_all.55 = bf16[2,784,128]{2,1,0:T(8,128)(2,1)S(1)} all-to-all(bf16[2,784,128]{2,1,0:T(8,128)(2,1)S(1)} %pad_maximum_fusion), channel_id=1, replica_groups=mesh['leaf'=4,'y'=4,'core'=2,'zhi'=4,'zlo'=8] {'core'}, dimensions={0} | all-to-all | bytes 802816 | tf_op jit(solution)/shard_map/all_to_all | solution.py:16
  32.1 8.8 %all_to_all.56 = bf16[4,256,128]{2,1,0:T(8,128)(2,1)S(1)} all-to-all(bf16[4,256,128]{2,1,0:T(8,128)(2,1)S(1)} %broadcast_in_dim.18), channel_id=1, replica_groups=mesh['leaf'=4,'y'=4,'core'=2,'zhi'=4,'zlo'=8] {'y'}, dimensions={0} | all-to-all | bytes 524288 | tf_op jit(solution)/shard_map/all_to_all | solution.py:16
  41.2 26.2 %all_to_all.57 = bf16[8,32,640]{2,1,0:T(8,128)(2,1)S(1)} all-to-all(bf16[8,32,640]{2,1,0:T(8,128)(2,1)S(1)} %bitcast.67), channel_id=1, replica_groups=mesh['leaf'=4,'y'=4,'core'=2,'zhi'=4,'zlo'=8] {'zlo'}, dimensions={0} | all-to-all | bytes 655360 | tf_op jit(solution)/shard_map/all_to_all | solution.py:16
  68.3 53.1 %all_to_all.58 = bf16[4,32,512]{2,1,0:T(8,128)(2,1)S(1)} all-to-all(bf16[4,32,512]{2,1,0:T(8,128)(2,1)S(1)} %broadcast_in_dim.20), channel_id=1, replica_groups=mesh['leaf'=4,'y'=4,'core'=2,'zhi'=4,'zlo'=8] {'zhi'}, dimensions={0} | all-to-all | bytes 262144 | tf_op jit(solution)/shard_map/all_to_all | solution.py:16
  122.0 7.5 %collective-permute-start = (bf16[8,320,512]{2,1,0:T(8,128)(2,1)}, bf16[8,320,512]{2,1,0:T(8,128)(2,1)S(1)}, u32[]{:S(2)}, u32[]{:S(2)}) collective-permute-start(bf16[8,320,512]{2,1,0:T(8,128)(2,1)} %bitcast.57), channel_id=1, source_target_pairs={{0,32},{32,0},{1,33},{33,1},{2,34},{34,2},{3,35},{35,3},{4,36},{36... | collective-permute-start | bytes 7864328 | tf_op jit(solution)/shard_map/ppermute | solution.py:173
  132.5 4.2 %all-to-all-start.4 = ((bf16[4,48,512]{2,1,0:T(8,128)(2,1)}), bf16[4,48,512]{2,1,0:T(8,128)(2,1)S(1)}, u32[]{:S(2)}, u32[]{:S(2)}) async-start(bf16[4,48,512]{2,1,0:T(8,128)(2,1)} %broadcast_in_dim.21), calls=%async_computation.4 | async-start | bytes 393216 | tf_op jit(solution)/shard_map/all_to_all | solution.py:16
  137.6 4.5 %all-to-all-done.4.upd_ref = bf16[4,48,512]{2,1,0:T(8,128)(2,1)S(1)} async-done(((bf16[4,48,512]{2,1,0:T(8,128)(2,1)}), bf16[4,48,512]{2,1,0:T(8,128)(2,1)S(1)}, u32[]{:S(2)}, u32[]{:S(2)}) %all-to-all-start.4) | async-done | bytes 196640 | tf_op jit(solution)/shard_map/all_to_all | solution.py:16
  143.6 1.5 copy-done.3
  145.1 1.7 copy-done.1
  146.8 1.7 copy-done.4
  148.6 2.0 shard_map.78
  150.6 3.3 %all-to-all-start.5 = ((bf16[4,32,512]{2,1,0:T(8,128)(2,1)}), bf16[4,32,512]{2,1,0:T(8,128)(2,1)S(1)}, u32[]{:S(2)}, u32[]{:S(2)}) async-start(bf16[4,32,512]{2,1,0:T(8,128)(2,1)} %shard_map.78), calls=%async_computation.5 | async-start | bytes 262144 | tf_op jit(solution)/shard_map/all_to_all | solution.py:16
  154.1 4.6 %all-to-all-done.5.parts_ref = bf16[4,32,512]{2,1,0:T(8,128)(2,1)S(1)} async-done(((bf16[4,32,512]{2,1,0:T(8,128)(2,1)}), bf16[4,32,512]{2,1,0:T(8,128)(2,1)S(1)}, u32[]{:S(2)}, u32[]{:S(2)}) %all-to-all-start.5) | async-done | bytes 131104 | tf_op jit(solution)/shard_map/all_to_all | solution.py:16
  158.7 1.7 copy-done.5
  161.5 7.9 %all_to_all.59 = bf16[4,64,512]{2,1,0:T(8,128)(2,1)S(1)} all-to-all(bf16[4,64,512]{2,1,0:T(8,128)(2,1)S(1)} %shard_map.79), channel_id=1, replica_groups=mesh['leaf'=4,'y'=4,'core'=2,'zhi'=4,'zlo'=8] {'leaf'}, dimensions={0} | all-to-all | bytes 524288 | tf_op jit(solution)/shard_map/all_to_all | solution.py:16
  170.1 12.7 %all-to-all-start.7 = ((bf16[4,32,512]{2,1,0:T(8,128)(2,1)}), bf16[4,32,512]{2,1,0:T(8,128)(2,1)S(1)}, u32[]{:S(2)}, u32[]{:S(2)}) async-start(bf16[4,32,512]{2,1,0:T(8,128)(2,1)} %broadcast_in_dim.22), calls=%async_computation.7 | async-start | bytes 262144 | tf_op jit(solution)/shard_map/all_to_all | solution.py:16
  183.6 20.9 %all-to-all-done.7.parts_ref = bf16[4,32,512]{2,1,0:T(8,128)(2,1)S(1)} async-done(((bf16[4,32,512]{2,1,0:T(8,128)(2,1)}), bf16[4,32,512]{2,1,0:T(8,128)(2,1)S(1)}, u32[]{:S(2)}, u32[]{:S(2)}) %all-to-all-start.7) | async-done | bytes 131104 | tf_op jit(solution)/shard_map/all_to_all | solution.py:16
  204.6 1.7 copy-done.6
  207.3 3.4 %all-to-all-start.8 = ((bf16[4,32,1024]{2,1,0:T(8,128)(2,1)}), bf16[4,32,1024]{2,1,0:T(8,128)(2,1)S(1)}, u32[]{:S(2)}, u32[]{:S(2)}) async-start(bf16[4,32,1024]{2,1,0:T(8,128)(2,1)} %copy-done.8), calls=%async_computation.8 | async-start | bytes 524288 | tf_op jit(solution)/shard_map/all_to_all | solution.py:16
  216.2 1.7 copy-done.7
  219.1 36.3 %all_to_all.60 = bf16[32,12,128]{2,1,0:T(8,128)(2,1)S(1)} all-to-all(bf16[32,12,128]{2,1,0:T(8,128)(2,1)S(1)} %reshape.216), channel_id=1, replica_groups=mesh['leaf'=4,'y'=4,'core'=2,'zhi'=4,'zlo'=8] {'zhi','zlo'}, dimensions={0} | all-to-all | bytes 196608 | tf_op jit(solution)/shard_map/all_to_all | solution.py:16
  256.3 10.6 %all-to-all-start.10 = ((bf16[8,48,128]{2,1,0:T(8,128)(2,1)}), bf16[8,48,128]{2,1,0:T(8,128)(2,1)S(1)}, u32[]{:S(2)}, u32[]{:S(2)}) async-start(bf16[8,48,128]{2,1,0:T(8,128)(2,1)} %reshape.222), calls=%async_computation.10 | async-start | bytes 196608 | tf_op jit(solution)/shard_map/all_to_all | solution.py:16
  266.9 5.0 %all-to-all-done.10 = bf16[8,48,128]{2,1,0:T(8,128)(2,1)S(1)} async-done(((bf16[8,48,128]{2,1,0:T(8,128)(2,1)}), bf16[8,48,128]{2,1,0:T(8,128)(2,1)S(1)}, u32[]{:S(2)}, u32[]{:S(2)}) %all-to-all-start.10) | async-done | bytes 98336 | tf_op jit(solution)/shard_map/all_to_all | solution.py:16
  (109 shorter events, 25.4 us)
Async XLA Ops:
  7.2 6.6 %copy-start = (bf16[1,512,512]{2,1,0:T(8,128)(2,1)S(1)}, bf16[1,512,512]{2,1,0:T(8,128)(2,1)}, u32[]{:S(2)}) copy-start(bf16[1,512,512]{2,1,0:T(8,128)(2,1)} %param.12) | copy-start | bytes 1572868
  7.2 5.9 %copy-start.16 = (s32[1,2]{1,0:T(1,128)S(1)}, s32[1,2]{1,0:T(1,128)}, u32[]{:S(2)}) copy-start(s32[1,2]{1,0:T(1,128)} %param.13) | copy-start | bytes 28
  7.2 114.9 %all-gather.3.cloned.1.call-start = ((), (), s32[]{:S(2)}) async-start(), calls=%async_computation.11 | async-start | bytes 2949120 | tf_op jit(solution)/shard_map/all_gather | solution.py:146
  7.2 1.1 copy-start.9
  8.3 0.9 copy-start.10
  9.2 0.8 copy-start.12
  10.1 3.7 %copy-start.13 = (bf16[1,256,128]{2,1,0:T(8,128)(2,1)S(1)}, bf16[1,256,128]{2,1,0:T(8,128)(2,1)}, u32[]{:S(2)}) copy-start(bf16[1,256,128]{2,1,0:T(8,128)(2,1)} %param.11) | copy-start | bytes 196612
  10.1 3.7 %copy-start.11 = (bf16[1,128,512]{2,1,0:T(8,128)(2,1)S(1)}, bf16[1,128,512]{2,1,0:T(8,128)(2,1)}, u32[]{:S(2)}) copy-start(bf16[1,128,512]{2,1,0:T(8,128)(2,1)} %param.10) | copy-start | bytes 393220
  32.0 100.4 %copy-start.14 = (bf16[2,784,128]{2,1,0:T(8,128)(2,1)}, bf16[2,784,128]{2,1,0:T(8,128)(2,1)S(1)}, u32[]{:S(2)}) copy-start(bf16[2,784,128]{2,1,0:T(8,128)(2,1)S(1)} %all_to_all.55) | copy-start | bytes 1204228
  67.5 0.7 copy-start.15
  122.0 21.5 %collective-permute-start = (bf16[8,320,512]{2,1,0:T(8,128)(2,1)}, bf16[8,320,512]{2,1,0:T(8,128)(2,1)S(1)}, u32[]{:S(2)}, u32[]{:S(2)}) collective-permute-start(bf16[8,320,512]{2,1,0:T(8,128)(2,1)} %bitcast.57), channel_id=1, source_target_pairs={{0,32},{32,0},{1,33},{33,1},{2,34},{34,2},{3,35},{35,3},{4,36},{36... | collective-permute-start | bytes 7864328 | tf_op jit(solution)/shard_map/ppermute | solution.py:173
  132.5 9.7 %all-to-all-start.4 = ((bf16[4,48,512]{2,1,0:T(8,128)(2,1)}), bf16[4,48,512]{2,1,0:T(8,128)(2,1)S(1)}, u32[]{:S(2)}, u32[]{:S(2)}) async-start(bf16[4,48,512]{2,1,0:T(8,128)(2,1)} %broadcast_in_dim.21), calls=%async_computation.4 | async-start | bytes 393216 | tf_op jit(solution)/shard_map/all_to_all | solution.py:16
  143.6 1.5 copy-start.3
  145.1 1.7 copy-start.1
  146.8 1.7 copy-start.4
  148.6 10.1 %copy-start.2 = (bf16[2560,512]{1,0:T(8,128)(2,1)S(1)}, bf16[2560,512]{1,0:T(8,128)(2,1)}, u32[]{:S(2)}) copy-start(bf16[2560,512]{1,0:T(8,128)(2,1)} %all-gather.3.cloned.1.call-done) | copy-start | bytes 7864324
  150.6 8.1 %all-to-all-start.5 = ((bf16[4,32,512]{2,1,0:T(8,128)(2,1)}), bf16[4,32,512]{2,1,0:T(8,128)(2,1)S(1)}, u32[]{:S(2)}, u32[]{:S(2)}) async-start(bf16[4,32,512]{2,1,0:T(8,128)(2,1)} %shard_map.78), calls=%async_computation.5 | async-start | bytes 262144 | tf_op jit(solution)/shard_map/all_to_all | solution.py:16
  158.7 1.7 copy-start.5
  170.1 34.5 %all-to-all-start.7 = ((bf16[4,32,512]{2,1,0:T(8,128)(2,1)}), bf16[4,32,512]{2,1,0:T(8,128)(2,1)S(1)}, u32[]{:S(2)}, u32[]{:S(2)}) async-start(bf16[4,32,512]{2,1,0:T(8,128)(2,1)} %broadcast_in_dim.22), calls=%async_computation.7 | async-start | bytes 262144 | tf_op jit(solution)/shard_map/all_to_all | solution.py:16
  204.6 1.7 copy-start.6
  206.6 0.7 copy-start.8
  207.3 8.9 %all-to-all-start.8 = ((bf16[4,32,1024]{2,1,0:T(8,128)(2,1)}), bf16[4,32,1024]{2,1,0:T(8,128)(2,1)S(1)}, u32[]{:S(2)}, u32[]{:S(2)}) async-start(bf16[4,32,1024]{2,1,0:T(8,128)(2,1)} %copy-done.8), calls=%async_computation.8 | async-start | bytes 524288 | tf_op jit(solution)/shard_map/all_to_all | solution.py:16
  216.2 1.7 copy-start.7
  256.3 15.6 %all-to-all-start.10 = ((bf16[8,48,128]{2,1,0:T(8,128)(2,1)}), bf16[8,48,128]{2,1,0:T(8,128)(2,1)S(1)}, u32[]{:S(2)}, u32[]{:S(2)}) async-start(bf16[8,48,128]{2,1,0:T(8,128)(2,1)} %reshape.222), calls=%async_computation.10 | async-start | bytes 196608 | tf_op jit(solution)/shard_map/all_to_all | solution.py:16
Sparse Core Ops, SparseCore 0:
  11.0 109.8 all-gather.2

commit v6 on v5

--- a/solution.py
+++ b/solution.py
@@ -28,20 +28,19 @@
     return lax.dot_general(a, b, (contract, ((), ())), preferred_element_type=F32)
 
 
-QUARTER, INV = 64, 128
-
-
-def pack_kernel(leaf_ref, root_ref, inv_ref, panel_ref, out_ref):
-    lanes = inv_ref.shape[1]
+QUARTER = 64
+
+
+def pack_kernel(leaf_ref, root_ref, panel_ref, out_ref):
+    lanes = out_ref.shape[1]
     at = pl.ds(pl.multiple_of(leaf_ref[0] * QUARTER, QUARTER), QUARTER)
     out_ref[:QUARTER] = root_ref[at, :lanes]
     out_ref[QUARTER:2 * QUARTER] = root_ref[at, lanes:]
     start = 2 * QUARTER
-    out_ref[start:start + INV] = inv_ref[...]
     fold = lanes // TILE
     few = panel_ref.shape[0] // fold
     for f in range(fold):
-        out_ref[start + INV:, f * TILE:(f + 1) * TILE] = panel_ref[f * few:(f + 1) * few]
+        out_ref[start:, f * TILE:(f + 1) * TILE] = panel_ref[f * few:(f + 1) * few]
 
 
 def root_half(ref, j):
@@ -93,11 +92,10 @@
     picked = picked.astype(BF)
     half = picked.shape[1] // 2
     n, lanes = TILE, own_ref.shape[2]
-    start = 2 * QUARTER + INV
     for z in range(ZLO):
         out = 0.0
         for i, ref in enumerate((own_ref, oth_ref)):
-            panel = jnp.concatenate([ref[z, start:, f:f + TILE] for f in range(0, lanes, TILE)], axis=0)
+            panel = jnp.concatenate([ref[z, :, f:f + TILE] for f in range(0, lanes, TILE)], axis=0)
             out = out + dot(picked[:, i * half:(i + 1) * half], panel, ((1,), (0,)))
         for k in range(Y):
             out_ref[k, :, z * n:(z + 1) * n] = out.astype(BF)
@@ -112,20 +110,25 @@
     n = TILE
     core = core_ref[0]
     for i, ref in enumerate((own_ref, oth_ref)):
-        inv = ref[:, 2 * QUARTER:2 * QUARTER + n, :].reshape(ZLO * n, ref.shape[2])
+        inv = ref[...].reshape(ZLO * n, ref.shape[2])
         out_ref[(core + i) % CORE] = dot(inv, residue, ((0,), (1,))).astype(BF)
 
 
-def call(kernel, out_shape, scratch, n_in, n_scalar=1):
+def call(kernel, out_shape, scratch, inputs, scalars=(), blocks=()):
+    def whole(x):
+        return pl.BlockSpec(x.shape, lambda i: (0,) * len(x.shape))
+
     return pl.pallas_call(
         kernel,
+        grid=(1,),
         out_shape=out_shape,
-        in_specs=[pl.BlockSpec(memory_space=pltpu.SMEM)] * n_scalar
-        + [pl.BlockSpec(memory_space=pltpu.VMEM)] * n_in,
-        out_specs=jax.tree.map(lambda _: pl.BlockSpec(memory_space=pltpu.VMEM), out_shape),
+        in_specs=[pl.BlockSpec(memory_space=pltpu.SMEM)] * len(scalars)
+        + [whole(x) for x in inputs[:len(inputs) - len(blocks)]]
+        + list(blocks),
+        out_specs=whole(out_shape),
         scratch_shapes=scratch,
-        compiler_params=pltpu.CompilerParams(vmem_limit_bytes=32 * 1024 * 1024),
-    )
+        compiler_params=pltpu.CompilerParams(vmem_limit_bytes=40 * 1024 * 1024),
+    )(*scalars, *inputs)
 
 
 def body(child_inv, child_panel, child_rhs, anc_tiles, root_inv, root_rhs):
@@ -139,11 +142,19 @@
     few = width // LEAF
 
     n = inv.shape[0]
-    packed_rows = 2 * QUARTER + INV + panel.size // inv.shape[1]
-    packed = call(pack_kernel, jax.ShapeDtypeStruct((packed_rows, inv.shape[1]), BF), [], 3)(
-        jnp.array([leaf], jnp.int32), root_inv, inv, panel
+    lanes = inv.shape[1]
+    packed_rows = 2 * QUARTER + panel.size // lanes
+    packed = call(
+        pack_kernel,
+        jax.ShapeDtypeStruct((packed_rows, lanes), BF),
+        [],
+        (root_inv, panel),
+        (jnp.array([leaf], jnp.int32),),
     )
     packed = lax.all_gather(packed, "zlo", axis=0, tiled=False)
+    inv_own = lax.all_gather(inv, "zlo", axis=0, tiled=False)
+    root_block = pl.BlockSpec((ZLO, 2 * QUARTER, lanes), lambda i: (0, 0, 0))
+    panel_block = pl.BlockSpec((ZLO, QUARTER, lanes), lambda i: (0, 2, 0))
 
     part = dot(rhs, inv, ((0,), (1,))).astype(BF).reshape(CORE, half, n)
     chunk = lax.dynamic_slice_in_dim(
@@ -180,31 +191,49 @@
         place_kernel,
         jax.ShapeDtypeStruct((Y, width, ZLO * QUARTER), BF),
         [pltpu.VMEM((width, 2 * rows), F32)],
-        5,
-    )(slots, update, side_own, side_oth, packed, packed_oth)
+        (update, side_own, side_oth, packed, packed_oth),
+        (slots,),
+        (root_block, root_block),
+    )
     pairs = slots.reshape(LEAF, CORE, 2)
     pairs = jnp.where(core == 0, pairs, pairs[:, ::-1]).reshape(-1)
     sol = call(
         spread_kernel,
         jax.ShapeDtypeStruct((LEAF, 2 * width, span), BF),
         [pltpu.VMEM((width, 2 * rows), F32)],
-        3,
-    )(pairs, exchange(root_part, "y"), packed, packed_oth)
+        (exchange(root_part, "y"), packed, packed_oth),
+        (pairs,),
+        (root_block, root_block),
+    )
     sol = total(exchange(sol, "leaf")).astype(BF)
-    picked, root = sol[:width], sol[width:]
-    correction = call(
-        correct_kernel, jax.ShapeDtypeStruct((Y, width, ZLO * n), BF), [], 3, 0
-    )(share(picked, "zhi", ZHI), packed, packed_oth)
-    child = call(
-        solve_kernel, jax.ShapeDtypeStruct((CORE, inv.shape[1], width), BF), [], 4
-    )(jnp.array([core], jnp.int32), forward_all, exchange(correction, "y"), packed, packed_oth)
+    picked, root = share(sol[:width], "zhi", ZHI), sol[width:]
 
     cols = ZHI * ZLO
-    child = jnp.transpose(child.reshape(CORE, cols, -1, width), (1, 0, 2, 3)).reshape(cols, -1)
-    n_child = child.shape[1]
     root = jnp.transpose(root.reshape(CORE, 2, few, span), (0, 2, 1, 3)).reshape(CORE, few, rows)
     root = jnp.stack([jnp.where(core == 0, root[0], root[1]), jnp.where(core == 0, root[1], root[0])])
     root = jnp.transpose(root.reshape(CORE, few, cols, -1), (2, 0, 1, 3)).reshape(cols, -1)
+    root, picked = lax.optimization_barrier((root, picked))
+
+    correction = call(
+        correct_kernel,
+        jax.ShapeDtypeStruct((Y, width, ZLO * n), BF),
+        [],
+        (picked, packed, packed_oth),
+        (),
+        (panel_block, panel_block),
+    )
+    inv_own, correction = lax.optimization_barrier((inv_own, correction))
+    inv_oth = lax.ppermute(inv_own, "core", other)
+    child = call(
+        solve_kernel,
+        jax.ShapeDtypeStruct((CORE, lanes, width), BF),
+        [],
+        (forward_all, exchange(correction, "y"), inv_own, inv_oth),
+        (jnp.array([core], jnp.int32),),
+    )
+
+    child = jnp.transpose(child.reshape(CORE, cols, -1, width), (1, 0, 2, 3)).reshape(cols, -1)
+    n_child = child.shape[1]
     out = exchange(jnp.concatenate([child, root], axis=1).reshape(cols, -1, TILE), Z)
     out = total(out.reshape(ZHI, ZLO, -1)).astype(BF)
     child = jnp.transpose(out[:, :n_child].reshape(ZLO, CORE, -1), (1, 0, 2)).reshape(CORE, -1)

time: 282 us -> 300 us (1.064)
  waiting for transfers between devices: 35.7 us -> 82.3 us
  blocking collectives: 150 us -> 120 us
  starting transfers between devices: 41.8 us -> 56.3 us
  local copies, waits for them, and re-layouts: 26.4 us -> 15.6 us
    all_to_all x6 -> x5, blocking collectives: 150 us -> 120 us  [exchange(): return lax.all_to_all(x, axis, 0, 0, tiled=True)]
    all_to_all x5 -> x6, waiting for transfers between devices: 35.7 us -> 61 us  [exchange(): return lax.all_to_all(x, axis, 0, 0, tiled=True)]
    all_gather x1, waiting for transfers between devices: 0.01 us -> 21.2 us  [body(): packed = lax.all_gather(packed, 'zlo', axis=0, tiled=False)]
    all_to_all x5 -> x6, starting transfers between devices: 34.3 us -> 45.5 us  [exchange(): return lax.all_to_all(x, axis, 0, 0, tiled=True)]
    unnamed x38 -> x28, local copies, waits for them, and re-layouts: 16.7 us -> 10.2 us
    ppermute x0 -> x1, starting transfers between devices: none -> 5.36 us  [body(): inv_oth = lax.ppermute(inv_own, 'core', other)]
  transfers between devices with their start and end apart: 7 -> 10, of which waited for: 5 -> 7; matrix products, arithmetic and copies ran while one was open for 5% -> 2% of each run, Pallas kernels for 0% -> 2%
where the time goes in v6:
time: 300 us; the launch traced here: 299 us
  blocking collectives  120 us (40%)
  waiting for transfers between devices  82.3 us (27%)
  starting transfers between devices  56.3 us (19%)
  local copies, waits for them, and re-layouts  15.6 us (5%)
  between operations  14.5 us (5%)
  Pallas kernels  5.44 us (2%)
  other arithmetic  4.33 us (1%)
    all_to_all x5, blocking collectives, exchange(): return lax.all_to_all(x, axis, 0, 0, tiled=True)  120 us
    all_to_all x6, waiting for transfers between devices, exchange(): return lax.all_to_all(x, axis, 0, 0, tiled=True)  61 us
    all_to_all x6, starting transfers between devices, exchange(): return lax.all_to_all(x, axis, 0, 0, tiled=True)  45.5 us
    all_gather x1, waiting for transfers between devices, body(): packed = lax.all_gather(packed, 'zlo', axis=0, tiled=False)  21.2 us
    unnamed x28, local copies, waits for them, and re-layouts  10.2 us
  transfers between devices with their start and end apart: 10, of which 7 were waited for; matrix products, arithmetic and copies ran while one was open for 2% of the time, Pallas kernels for 2%

profile of v6, /device:TPU:1, one launch (start us, length us, event | category | flops | bytes accessed | tf_op | source)
XLA Modules:
  0.0 299.1 jit_solution(17046546278873180467)
XLA Ops:
  7.9 1.5 copy.42
  10.6 17.8 %all_to_all.55 = bf16[2,784,128]{2,1,0:T(8,128)(2,1)S(1)} all-to-all(bf16[2,784,128]{2,1,0:T(8,128)(2,1)S(1)} %pad_maximum_fusion), channel_id=1, replica_groups=mesh['leaf'=4,'y'=4,'core'=2,'zhi'=4,'zlo'=8] {'core'}, dimensions={0} | all-to-all | bytes 802816 | tf_op jit(solution)/shard_map/all_to_all | solution.py:16
  28.5 8.9 %all_to_all.56 = bf16[4,256,128]{2,1,0:T(8,128)(2,1)S(1)} all-to-all(bf16[4,256,128]{2,1,0:T(8,128)(2,1)S(1)} %broadcast_in_dim.18), channel_id=1, replica_groups=mesh['leaf'=4,'y'=4,'core'=2,'zhi'=4,'zlo'=8] {'y'}, dimensions={0} | all-to-all | bytes 524288 | tf_op jit(solution)/shard_map/all_to_all | solution.py:16
  38.4 3.4 %all-to-all-start.2 = ((bf16[8,32,640]{2,1,0:T(8,128)(2,1)}), bf16[8,32,640]{2,1,0:T(8,128)(2,1)S(1)}, u32[]{:S(2)}, u32[]{:S(2)}) async-start(bf16[8,32,640]{2,1,0:T(8,128)(2,1)} %bitcast.10), calls=%async_computation.2 | async-start | bytes 655360 | tf_op jit(solution)/shard_map/all_to_all | solution.py:16
  42.7 14.8 %all-to-all-done.2 = bf16[8,32,640]{2,1,0:T(8,128)(2,1)S(1)} async-done(((bf16[8,32,640]{2,1,0:T(8,128)(2,1)}), bf16[8,32,640]{2,1,0:T(8,128)(2,1)S(1)}, u32[]{:S(2)}, u32[]{:S(2)}) %all-to-all-start.2) | async-done | bytes 327712 | tf_op jit(solution)/shard_map/all_to_all | solution.py:16
  57.5 45.6 %all_to_all.57 = bf16[4,32,512]{2,1,0:T(8,128)(2,1)S(1)} all-to-all(bf16[4,32,512]{2,1,0:T(8,128)(2,1)S(1)} %broadcast_in_dim.20), channel_id=1, replica_groups=mesh['leaf'=4,'y'=4,'core'=2,'zhi'=4,'zlo'=8] {'zhi'}, dimensions={0} | all-to-all | bytes 262144 | tf_op jit(solution)/shard_map/all_to_all | solution.py:16
  103.2 21.2 %all-gather.6.cloned.1.call-done = bf16[1536,512]{1,0:T(8,128)(2,1)} async-done(((bf16[192,512]{1,0:T(8,128)(2,1)}), bf16[1536,512]{1,0:T(8,128)(2,1)}) %all-gather.6.cloned.1.call-update) | async-done | bytes 1572880 | tf_op jit(solution)/shard_map/all_gather | solution.py:154
  124.4 5.4 %collective-permute-start = (bf16[8,192,512]{2,1,0:T(8,128)(2,1)}, bf16[8,192,512]{2,1,0:T(8,128)(2,1)S(1)}, u32[]{:S(2)}, u32[]{:S(2)}) collective-permute-start(bf16[8,192,512]{2,1,0:T(8,128)(2,1)} %bitcast.57), channel_id=1, source_target_pairs={{0,32},{32,0},{1,33},{33,1},{2,34},{34,2},{3,35},{35,3},{4,36},{36... | collective-permute-start | bytes 4718600 | tf_op jit(solution)/shard_map/ppermute | solution.py:184
  132.0 4.9 %all-to-all-start.4 = ((bf16[4,48,512]{2,1,0:T(8,128)(2,1)}), bf16[4,48,512]{2,1,0:T(8,128)(2,1)S(1)}, u32[]{:S(2)}, u32[]{:S(2)}) async-start(bf16[4,48,512]{2,1,0:T(8,128)(2,1)} %broadcast_in_dim.21), calls=%async_computation.4 | async-start | bytes 393216 | tf_op jit(solution)/shard_map/all_to_all | solution.py:16
  136.9 5.4 %all-to-all-done.4.upd_ref = bf16[4,48,512]{2,1,0:T(8,128)(2,1)S(1)} async-done(((bf16[4,48,512]{2,1,0:T(8,128)(2,1)}), bf16[4,48,512]{2,1,0:T(8,128)(2,1)S(1)}, u32[]{:S(2)}, u32[]{:S(2)}) %all-to-all-start.4) | async-done | bytes 196640 | tf_op jit(solution)/shard_map/all_to_all | solution.py:16
  147.7 1.9 shard_map.78
  149.6 4.7 %all-to-all-start.5 = ((bf16[4,32,512]{2,1,0:T(8,128)(2,1)}), bf16[4,32,512]{2,1,0:T(8,128)(2,1)S(1)}, u32[]{:S(2)}, u32[]{:S(2)}) async-start(bf16[4,32,512]{2,1,0:T(8,128)(2,1)} %shard_map.78), calls=%async_computation.5 | async-start | bytes 262144 | tf_op jit(solution)/shard_map/all_to_all | solution.py:16
  154.5 4.6 %all-to-all-done.5.parts_ref = bf16[4,32,512]{2,1,0:T(8,128)(2,1)S(1)} async-done(((bf16[4,32,512]{2,1,0:T(8,128)(2,1)}), bf16[4,32,512]{2,1,0:T(8,128)(2,1)S(1)}, u32[]{:S(2)}, u32[]{:S(2)}) %all-to-all-start.5) | async-done | bytes 131104 | tf_op jit(solution)/shard_map/all_to_all | solution.py:16
  159.2 1.4 copy-done.5
  161.6 8.3 %all_to_all.58 = bf16[4,64,512]{2,1,0:T(8,128)(2,1)S(1)} all-to-all(bf16[4,64,512]{2,1,0:T(8,128)(2,1)S(1)} %shard_map.79), channel_id=1, replica_groups=mesh['leaf'=4,'y'=4,'core'=2,'zhi'=4,'zlo'=8] {'leaf'}, dimensions={0} | all-to-all | bytes 524288 | tf_op jit(solution)/shard_map/all_to_all | solution.py:16
  170.7 20.8 %all-to-all-start.7 = ((bf16[4,32,512]{2,1,0:T(8,128)(2,1)}), bf16[4,32,512]{2,1,0:T(8,128)(2,1)S(1)}, u32[]{:S(2)}, u32[]{:S(2)}) async-start(bf16[4,32,512]{2,1,0:T(8,128)(2,1)} %broadcast_in_dim.22), calls=%async_computation.7 | async-start | bytes 262144 | tf_op jit(solution)/shard_map/all_to_all | solution.py:16
  192.0 24.5 %all-to-all-done.7.parts_ref = bf16[4,32,512]{2,1,0:T(8,128)(2,1)S(1)} async-done(((bf16[4,32,512]{2,1,0:T(8,128)(2,1)}), bf16[4,32,512]{2,1,0:T(8,128)(2,1)S(1)}, u32[]{:S(2)}, u32[]{:S(2)}) %all-to-all-start.7) | async-done | bytes 131104 | tf_op jit(solution)/shard_map/all_to_all | solution.py:16
  216.5 1.4 copy-done.6
  218.9 5.4 %collective-permute-start.1 = (bf16[8,128,512]{2,1,0:T(8,128)(2,1)}, bf16[8,128,512]{2,1,0:T(8,128)(2,1)S(1)}, u32[]{:S(2)}, u32[]{:S(2)}) collective-permute-start(bf16[8,128,512]{2,1,0:T(8,128)(2,1)} %all-gather.4.cloned.1.call-done.own_ref), channel_id=1, source_target_pairs={{0,32},{32,0},{1,33},{33,1},{2,34},{34,2},{3,35},{35,3},{4,36},{36... | collective-permute-start | bytes 3145736 | tf_op jit(solution)/shard_map/ppermute | solution.py:226
  224.3 3.4 %all-to-all-start.8 = ((bf16[4,32,1024]{2,1,0:T(8,128)(2,1)}), bf16[4,32,1024]{2,1,0:T(8,128)(2,1)S(1)}, u32[]{:S(2)}, u32[]{:S(2)}) async-start(bf16[4,32,1024]{2,1,0:T(8,128)(2,1)} %shard_map.80), calls=%async_computation.8 | async-start | bytes 524288 | tf_op jit(solution)/shard_map/all_to_all | solution.py:16
  227.7 6.8 %all-to-all-done.8.parts_ref = bf16[4,32,1024]{2,1,0:T(8,128)(2,1)S(1)} async-done(((bf16[4,32,1024]{2,1,0:T(8,128)(2,1)}), bf16[4,32,1024]{2,1,0:T(8,128)(2,1)S(1)}, u32[]{:S(2)}, u32[]{:S(2)}) %all-to-all-start.8) | async-done | bytes 262176 | tf_op jit(solution)/shard_map/all_to_all | solution.py:16
  236.9 39.4 %all_to_all.59 = bf16[32,12,128]{2,1,0:T(8,128)(2,1)S(1)} all-to-all(bf16[32,12,128]{2,1,0:T(8,128)(2,1)S(1)} %reshape.216), channel_id=1, replica_groups=mesh['leaf'=4,'y'=4,'core'=2,'zhi'=4,'zlo'=8] {'zhi','zlo'}, dimensions={0} | all-to-all | bytes 196608 | tf_op jit(solution)/shard_map/all_to_all | solution.py:16
  277.2 8.2 %all-to-all-start.10 = ((bf16[8,48,128]{2,1,0:T(8,128)(2,1)}), bf16[8,48,128]{2,1,0:T(8,128)(2,1)S(1)}, u32[]{:S(2)}, u32[]{:S(2)}) async-start(bf16[8,48,128]{2,1,0:T(8,128)(2,1)} %reshape.222), calls=%async_computation.10 | async-start | bytes 196608 | tf_op jit(solution)/shard_map/all_to_all | solution.py:16
  285.5 5.0 %all-to-all-done.10 = bf16[8,48,128]{2,1,0:T(8,128)(2,1)S(1)} async-done(((bf16[8,48,128]{2,1,0:T(8,128)(2,1)}), bf16[8,48,128]{2,1,0:T(8,128)(2,1)S(1)}, u32[]{:S(2)}, u32[]{:S(2)}) %all-to-all-start.10) | async-done | bytes 98336 | tf_op jit(solution)/shard_map/all_to_all | solution.py:16
  (105 shorter events, 19.8 us)
Async XLA Ops:
  7.2 3.0 %copy-start = (bf16[1,512,512]{2,1,0:T(8,128)(2,1)S(1)}, bf16[1,512,512]{2,1,0:T(8,128)(2,1)}, u32[]{:S(2)}) copy-start(bf16[1,512,512]{2,1,0:T(8,128)(2,1)} %param.12) | copy-start | bytes 1572868
  7.2 2.3 copy-start.11
  7.2 2.9 copy-start.9
  7.2 3.0 copy-start.10
  28.4 13.5 %copy-start.8 = (bf16[256,1024]{1,0:T(8,128)(2,1)S(1)}, bf16[256,1024]{1,0:T(8,128)(2,1)}, u32[]{:S(2)}) copy-start(bf16[256,1024]{1,0:T(8,128)(2,1)} %root_ref.1) | copy-start | bytes 1572868
  38.4 19.1 %all-to-all-start.2 = ((bf16[8,32,640]{2,1,0:T(8,128)(2,1)}), bf16[8,32,640]{2,1,0:T(8,128)(2,1)S(1)}, u32[]{:S(2)}, u32[]{:S(2)}) async-start(bf16[8,32,640]{2,1,0:T(8,128)(2,1)} %bitcast.10), calls=%async_computation.2 | async-start | bytes 655360 | tf_op jit(solution)/shard_map/all_to_all | solution.py:16
  41.9 82.5 %all-gather.6.cloned.1.call-start = ((), (), s32[]{:S(2)}) async-start(), calls=%async_computation.12 | async-start | bytes 1769472 | tf_op jit(solution)/shard_map/all_gather | solution.py:154
  42.7 176.2 %all-gather.4.cloned.1.call-start = ((), (), s32[]{:S(2)}) async-start(), calls=%async_computation.11 | async-start | bytes 1179648 | tf_op jit(solution)/shard_map/all_gather | solution.py:155
  124.4 19.3 %collective-permute-start = (bf16[8,192,512]{2,1,0:T(8,128)(2,1)}, bf16[8,192,512]{2,1,0:T(8,128)(2,1)S(1)}, u32[]{:S(2)}, u32[]{:S(2)}) collective-permute-start(bf16[8,192,512]{2,1,0:T(8,128)(2,1)} %bitcast.57), channel_id=1, source_target_pairs={{0,32},{32,0},{1,33},{33,1},{2,34},{34,2},{3,35},{35,3},{4,36},{36... | collective-permute-start | bytes 4718600 | tf_op jit(solution)/shard_map/ppermute | solution.py:184
  132.0 10.4 %all-to-all-start.4 = ((bf16[4,48,512]{2,1,0:T(8,128)(2,1)}), bf16[4,48,512]{2,1,0:T(8,128)(2,1)S(1)}, u32[]{:S(2)}, u32[]{:S(2)}) async-start(bf16[4,48,512]{2,1,0:T(8,128)(2,1)} %broadcast_in_dim.21), calls=%async_computation.4 | async-start | bytes 393216 | tf_op jit(solution)/shard_map/all_to_all | solution.py:16
  143.7 1.2 copy-start.3
  144.9 1.4 copy-start.1
  146.3 1.4 copy-start.4
  147.7 11.5 %copy-start.2 = (bf16[1536,512]{1,0:T(8,128)(2,1)S(1)}, bf16[1536,512]{1,0:T(8,128)(2,1)}, u32[]{:S(2)}) copy-start(bf16[1536,512]{1,0:T(8,128)(2,1)} %all-gather.6.cloned.1.call-done) | copy-start | bytes 4718596
  149.6 9.5 %all-to-all-start.5 = ((bf16[4,32,512]{2,1,0:T(8,128)(2,1)}), bf16[4,32,512]{2,1,0:T(8,128)(2,1)S(1)}, u32[]{:S(2)}, u32[]{:S(2)}) async-start(bf16[4,32,512]{2,1,0:T(8,128)(2,1)} %shard_map.78), calls=%async_computation.5 | async-start | bytes 262144 | tf_op jit(solution)/shard_map/all_to_all | solution.py:16
  159.2 1.4 copy-start.5
  170.7 45.8 %all-to-all-start.7 = ((bf16[4,32,512]{2,1,0:T(8,128)(2,1)}), bf16[4,32,512]{2,1,0:T(8,128)(2,1)S(1)}, u32[]{:S(2)}, u32[]{:S(2)}) async-start(bf16[4,32,512]{2,1,0:T(8,128)(2,1)} %broadcast_in_dim.22), calls=%async_computation.7 | async-start | bytes 262144 | tf_op jit(solution)/shard_map/all_to_all | solution.py:16
  216.5 1.4 copy-start.6
  218.9 15.6 %collective-permute-start.1 = (bf16[8,128,512]{2,1,0:T(8,128)(2,1)}, bf16[8,128,512]{2,1,0:T(8,128)(2,1)S(1)}, u32[]{:S(2)}, u32[]{:S(2)}) collective-permute-start(bf16[8,128,512]{2,1,0:T(8,128)(2,1)} %all-gather.4.cloned.1.call-done.own_ref), channel_id=1, source_target_pairs={{0,32},{32,0},{1,33},{33,1},{2,34},{34,2},{3,35},{35,3},{4,36},{36... | collective-permute-start | bytes 3145736 | tf_op jit(solution)/shard_map/ppermute | solution.py:226
  224.3 10.2 %all-to-all-start.8 = ((bf16[4,32,1024]{2,1,0:T(8,128)(2,1)}), bf16[4,32,1024]{2,1,0:T(8,128)(2,1)S(1)}, u32[]{:S(2)}, u32[]{:S(2)}) async-start(bf16[4,32,1024]{2,1,0:T(8,128)(2,1)} %shard_map.80), calls=%async_computation.8 | async-start | bytes 524288 | tf_op jit(solution)/shard_map/all_to_all | solution.py:16
  234.5 1.2 copy-start.7
  277.2 13.2 %all-to-all-start.10 = ((bf16[8,48,128]{2,1,0:T(8,128)(2,1)}), bf16[8,48,128]{2,1,0:T(8,128)(2,1)S(1)}, u32[]{:S(2)}, u32[]{:S(2)}) async-start(bf16[8,48,128]{2,1,0:T(8,128)(2,1)} %reshape.222), calls=%async_computation.10 | async-start | bytes 196608 | tf_op jit(solution)/shard_map/all_to_all | solution.py:16
Sparse Core Ops, SparseCore 0:
  45.4 78.9 all-gather.5
  130.0 77.3 all-gather.3

commit v7 on v6

--- a/solution.py
+++ b/solution.py
@@ -28,28 +28,41 @@
     return lax.dot_general(a, b, (contract, ((), ())), preferred_element_type=F32)
 
 
-QUARTER = 64
-
-
-def pack_kernel(leaf_ref, root_ref, panel_ref, out_ref):
+QUARTER, INV = 64, 128
+ROOT_ROWS, INV_ROWS, PANEL_ROWS = (0, 128), (128, 128), (256, 64)
+
+
+def pack_kernel(leaf_ref, root_ref, inv_ref, panel_ref, out_ref):
     lanes = out_ref.shape[1]
     at = pl.ds(pl.multiple_of(leaf_ref[0] * QUARTER, QUARTER), QUARTER)
     out_ref[:QUARTER] = root_ref[at, :lanes]
     out_ref[QUARTER:2 * QUARTER] = root_ref[at, lanes:]
-    start = 2 * QUARTER
+    out_ref[INV_ROWS[0]:PANEL_ROWS[0]] = inv_ref[...]
     fold = lanes // TILE
     few = panel_ref.shape[0] // fold
     for f in range(fold):
-        out_ref[start:, f * TILE:(f + 1) * TILE] = panel_ref[f * few:(f + 1) * few]
-
-
-def root_half(ref, j):
-    return ref[:, j * QUARTER:(j + 1) * QUARTER, :].reshape(ZLO * QUARTER, ref.shape[2])
-
-
-def place_kernel(slot_ref, upd_ref, rhs_own, rhs_oth, own_ref, oth_ref, out_ref, side_ref):
+        out_ref[PANEL_ROWS[0]:, f * TILE:(f + 1) * TILE] = panel_ref[f * few:(f + 1) * few]
+
+
+def fetch(refs, span, buf_ref, sems):
+    copies = [
+        pltpu.make_async_copy(ref.at[:, pl.ds(*span)], buf_ref.at[i], sems.at[i])
+        for i, ref in enumerate(refs)
+    ]
+    for copy in copies:
+        copy.start()
+    return copies
+
+
+def root_half(buf_ref, i):
+    j = i % 2
+    return buf_ref[i // 2, :, j * QUARTER:(j + 1) * QUARTER, :].reshape(ZLO * QUARTER, buf_ref.shape[3])
+
+
+def place_kernel(slot_ref, upd_ref, rhs_own, rhs_oth, own_ref, oth_ref, out_ref, buf_ref, sems, side_ref):
+    copies = fetch((own_ref, oth_ref), ROOT_ROWS, buf_ref, sems)
     half = rhs_own.shape[1]
-    lanes = own_ref.shape[2]
+    lanes = buf_ref.shape[3]
     side_ref[:, :half] = rhs_own[...].astype(F32)
     side_ref[:, half:] = rhs_oth[...].astype(F32)
     width = side_ref.shape[0]
@@ -57,23 +70,27 @@
         for u in range(4):
             at = pl.ds(pl.multiple_of(slot_ref[k * 4 + u] * TILE, TILE), TILE)
             side_ref[:, at] = side_ref[:, at] - upd_ref[k, :width, u * TILE:(u + 1) * TILE].astype(F32)
+    for copy in copies:
+        copy.wait()
     out = 0.0
     for i in range(4):
         side = side_ref[:, i * lanes:(i + 1) * lanes].astype(BF)
-        out = out + dot(side, root_half((own_ref, oth_ref)[i // 2], i % 2), ((1,), (1,)))
+        out = out + dot(side, root_half(buf_ref, i), ((1,), (1,)))
     for k in range(Y):
         out_ref[k] = out.astype(BF)
 
 
-def spread_kernel(slot_ref, parts_ref, own_ref, oth_ref, out_ref, sol_ref):
-    lanes = own_ref.shape[2]
+def spread_kernel(slot_ref, parts_ref, own_ref, oth_ref, out_ref, buf_ref, sems, sol_ref):
+    copies = fetch((own_ref, oth_ref), ROOT_ROWS, buf_ref, sems)
+    lanes = buf_ref.shape[3]
     forward = parts_ref[0].astype(F32)
     for k in range(1, Y):
         forward = forward + parts_ref[k].astype(F32)
     forward = forward.astype(BF)
+    for copy in copies:
+        copy.wait()
     for i in range(4):
-        root = root_half((own_ref, oth_ref)[i // 2], i % 2)
-        sol_ref[:, i * lanes:(i + 1) * lanes] = dot(forward, root, ((1,), (0,)))
+        sol_ref[:, i * lanes:(i + 1) * lanes] = dot(forward, root_half(buf_ref, i), ((1,), (0,)))
     width, span = forward.shape[0], 4 * TILE
     few = width // LEAF
     for k in range(LEAF):
@@ -85,50 +102,55 @@
         out_ref[k, width:, :] = mine.astype(BF)
 
 
-def correct_kernel(parts_ref, own_ref, oth_ref, out_ref):
+def correct_kernel(parts_ref, own_ref, oth_ref, out_ref, buf_ref, sems):
+    copies = fetch((own_ref, oth_ref), PANEL_ROWS, buf_ref, sems)
     picked = parts_ref[0].astype(F32)
     for k in range(1, ZHI):
         picked = picked + parts_ref[k].astype(F32)
     picked = picked.astype(BF)
     half = picked.shape[1] // 2
-    n, lanes = TILE, own_ref.shape[2]
+    n, lanes = TILE, buf_ref.shape[3]
+    for copy in copies:
+        copy.wait()
     for z in range(ZLO):
         out = 0.0
-        for i, ref in enumerate((own_ref, oth_ref)):
-            panel = jnp.concatenate([ref[z, :, f:f + TILE] for f in range(0, lanes, TILE)], axis=0)
+        for i in range(CORE):
+            panel = jnp.concatenate([buf_ref[i, z, :, f:f + TILE] for f in range(0, lanes, TILE)], axis=0)
             out = out + dot(picked[:, i * half:(i + 1) * half], panel, ((1,), (0,)))
         for k in range(Y):
             out_ref[k, :, z * n:(z + 1) * n] = out.astype(BF)
 
 
-def solve_kernel(core_ref, forward_ref, parts_ref, own_ref, oth_ref, out_ref):
+def solve_kernel(core_ref, forward_ref, parts_ref, own_ref, oth_ref, out_ref, buf_ref, sems):
+    copies = fetch((own_ref, oth_ref), INV_ROWS, buf_ref, sems)
     correction = parts_ref[0].astype(F32)
     for k in range(1, Y):
         correction = correction + parts_ref[k].astype(F32)
     residue = forward_ref[...].astype(F32) - correction.astype(BF).astype(F32)
     residue = residue.astype(BF)
-    n = TILE
     core = core_ref[0]
-    for i, ref in enumerate((own_ref, oth_ref)):
-        inv = ref[...].reshape(ZLO * n, ref.shape[2])
+    for copy in copies:
+        copy.wait()
+    for i in range(CORE):
+        inv = buf_ref[i].reshape(ZLO * INV, buf_ref.shape[3])
         out_ref[(core + i) % CORE] = dot(inv, residue, ((0,), (1,))).astype(BF)
 
 
-def call(kernel, out_shape, scratch, inputs, scalars=(), blocks=()):
-    def whole(x):
-        return pl.BlockSpec(x.shape, lambda i: (0,) * len(x.shape))
-
+def call(kernel, out_shape, inputs, scalars=(), gathered=(), span=None, scratch=()):
+    vmem = pl.BlockSpec(memory_space=pltpu.VMEM)
+    buffers = []
+    if gathered:
+        blocks, _, lanes = gathered[0].shape
+        buffers = [pltpu.VMEM((len(gathered), blocks, span[1], lanes), BF), pltpu.SemaphoreType.DMA((len(gathered),))]
     return pl.pallas_call(
         kernel,
-        grid=(1,),
         out_shape=out_shape,
         in_specs=[pl.BlockSpec(memory_space=pltpu.SMEM)] * len(scalars)
-        + [whole(x) for x in inputs[:len(inputs) - len(blocks)]]
-        + list(blocks),
-        out_specs=whole(out_shape),
-        scratch_shapes=scratch,
-        compiler_params=pltpu.CompilerParams(vmem_limit_bytes=40 * 1024 * 1024),
-    )(*scalars, *inputs)
+        + [vmem] * len(inputs)
+        + [pl.BlockSpec(memory_space=pl.ANY)] * len(gathered),
+        out_specs=vmem,
+        scratch_shapes=buffers + list(scratch),
+    )(*scalars, *inputs, *gathered)
 
 
 def body(child_inv, child_panel, child_rhs, anc_tiles, root_inv, root_rhs):
@@ -143,18 +165,13 @@
 
     n = inv.shape[0]
     lanes = inv.shape[1]
-    packed_rows = 2 * QUARTER + panel.size // lanes
     packed = call(
         pack_kernel,
-        jax.ShapeDtypeStruct((packed_rows, lanes), BF),
-        [],
-        (root_inv, panel),
+        jax.ShapeDtypeStruct((sum(PANEL_ROWS), lanes), BF),
+        (root_inv, inv, panel),
         (jnp.array([leaf], jnp.int32),),
     )
     packed = lax.all_gather(packed, "zlo", axis=0, tiled=False)
-    inv_own = lax.all_gather(inv, "zlo", axis=0, tiled=False)
-    root_block = pl.BlockSpec((ZLO, 2 * QUARTER, lanes), lambda i: (0, 0, 0))
-    panel_block = pl.BlockSpec((ZLO, QUARTER, lanes), lambda i: (0, 2, 0))
 
     part = dot(rhs, inv, ((0,), (1,))).astype(BF).reshape(CORE, half, n)
     chunk = lax.dynamic_slice_in_dim(
@@ -180,30 +197,33 @@
     forward_all = jnp.transpose(both[:, :, span:], (1, 0, 2)).reshape(width, -1)
     update = total(both[:, :, :span]).astype(BF)
     update = total(share(update, "zhi", ZHI)).astype(BF)
-    packed, update = lax.optimization_barrier((packed, update))
-    packed_oth = lax.ppermute(packed, "core", other)
     names = jnp.zeros((16, span), BF).at[:, :4].set(anc_y[None])
     update = share(jnp.concatenate([update, names], axis=0), "leaf", LEAF)
+    packed, update = lax.optimization_barrier((packed, update))
+    both = (packed, lax.ppermute(packed, "core", other))
     slots = update[:, width, :4].reshape(-1).astype(jnp.int32)
     slots = lax.rem(slots - y * 16 + core * 8, 16)
 
+    wide = [pltpu.VMEM((width, 2 * rows), F32)]
     root_part = call(
         place_kernel,
         jax.ShapeDtypeStruct((Y, width, ZLO * QUARTER), BF),
-        [pltpu.VMEM((width, 2 * rows), F32)],
-        (update, side_own, side_oth, packed, packed_oth),
+        (update, side_own, side_oth),
         (slots,),
-        (root_block, root_block),
+        both,
+        ROOT_ROWS,
+        wide,
     )
     pairs = slots.reshape(LEAF, CORE, 2)
     pairs = jnp.where(core == 0, pairs, pairs[:, ::-1]).reshape(-1)
     sol = call(
         spread_kernel,
         jax.ShapeDtypeStruct((LEAF, 2 * width, span), BF),
-        [pltpu.VMEM((width, 2 * rows), F32)],
-        (exchange(root_part, "y"), packed, packed_oth),
+        (exchange(root_part, "y"),),
         (pairs,),
-        (root_block, root_block),
+        both,
+        ROOT_ROWS,
+        wide,
     )
     sol = total(exchange(sol, "leaf")).astype(BF)
     picked, root = share(sol[:width], "zhi", ZHI), sol[width:]
@@ -217,19 +237,18 @@
     correction = call(
         correct_kernel,
         jax.ShapeDtypeStruct((Y, width, ZLO * n), BF),
-        [],
-        (picked, packed, packed_oth),
+        (picked,),
         (),
-        (panel_block, panel_block),
-    )
-    inv_own, correction = lax.optimization_barrier((inv_own, correction))
-    inv_oth = lax.ppermute(inv_own, "core", other)
+        both,
+        PANEL_ROWS,
+    )
     child = call(
         solve_kernel,
         jax.ShapeDtypeStruct((CORE, lanes, width), BF),
-        [],
-        (forward_all, exchange(correction, "y"), inv_own, inv_oth),
+        (forward_all, exchange(correction, "y")),
         (jnp.array([core], jnp.int32),),
+        both,
+        INV_ROWS,
     )
 
     child = jnp.transpose(child.reshape(CORE, cols, -1, width), (1, 0, 2, 3)).reshape(cols, -1)

time: 300 us -> 285 us (0.950)
  waiting for transfers between devices: 82.3 us -> 59.2 us
  Pallas kernels: 5.44 us -> 16.6 us
  blocking collectives: 120 us -> 114 us
    all_gather x1, waiting for transfers between devices: 21.2 us -> 0.01 us  [body(): packed = lax.all_gather(packed, 'zlo', axis=0, tiled=False)]
    pallas_call x5, Pallas kernels: 5.44 us -> 16.6 us  [call(): pl.pallas_call(kernel, out_shape=out_shape, in_specs=[pl.BlockSpec(memory...]
    all_to_all x5 -> x6, blocking collectives: 120 us -> 114 us  [exchange(): return lax.all_to_all(x, axis, 0, 0, tiled=True)]
    unnamed x28 -> x18, local copies, waits for them, and re-layouts: 10.2 us -> 5.77 us
    all_to_all x6 -> x5, waiting for transfers between devices: 61 us -> 59.2 us  [exchange(): return lax.all_to_all(x, axis, 0, 0, tiled=True)]
    ppermute x2 -> x1, starting transfers between devices: 10.8 us -> 9.45 us  [body(): both = (packed, lax.ppermute(packed, 'core', other))]
    all_to_all x6 -> x5, starting transfers between devices: 45.5 us -> 44.6 us  [exchange(): return lax.all_to_all(x, axis, 0, 0, tiled=True)]
  transfers between devices with their start and end apart: 10 -> 7, of which waited for: 7 -> 5; matrix products, arithmetic and copies ran while one was open for 2% -> 6% of each run, Pallas kernels for 2% -> 0%
where the time goes in v7:
time: 285 us; the launch traced here: 283 us
  blocking collectives  114 us (40%)
  waiting for transfers between devices  59.2 us (21%)
  starting transfers between devices  54.1 us (19%)
  local copies, waits for them, and re-layouts  16.9 us (6%)
  Pallas kernels  16.6 us (6%)
  between operations  14.5 us (5%)
  other arithmetic  6.96 us (2%)
    all_to_all x6, blocking collectives, exchange(): return lax.all_to_all(x, axis, 0, 0, tiled=True)  114 us
    all_to_all x5, waiting for transfers between devices, exchange(): return lax.all_to_all(x, axis, 0, 0, tiled=True)  59.2 us
    all_to_all x5, starting transfers between devices, exchange(): return lax.all_to_all(x, axis, 0, 0, tiled=True)  44.6 us
    pallas_call x5, Pallas kernels, call(): pl.pallas_call(kernel, out_shape=out_shape, in_specs=[pl.BlockSpec(memory...  16.6 us
    ppermute x1, starting transfers between devices, body(): both = (packed, lax.ppermute(packed, 'core', other))  9.45 us
    unnamed x18, local copies, waits for them, and re-layouts  5.77 us
  transfers between devices with their start and end apart: 7, of which 5 were waited for; matrix products, arithmetic and copies ran while one was open for 6% of the time, Pallas kernels for 0%

profile of v7, /device:TPU:1, one launch (start us, length us, event | category | flops | bytes accessed | tf_op | source)
XLA Modules:
  0.0 283.2 jit_solution(6502860394649349285)
XLA Ops:
  7.2 1.9 shard_map.77
  14.0 17.8 %all_to_all.55 = bf16[2,784,128]{2,1,0:T(8,128)(2,1)S(1)} all-to-all(bf16[2,784,128]{2,1,0:T(8,128)(2,1)S(1)} %pad_maximum_fusion), channel_id=1, replica_groups=mesh['leaf'=4,'y'=4,'core'=2,'zhi'=4,'zlo'=8] {'core'}, dimensions={0} | all-to-all | bytes 802816 | tf_op jit(solution)/shard_map/all_to_all | solution.py:16
  31.9 8.8 %all_to_all.56 = bf16[4,256,128]{2,1,0:T(8,128)(2,1)S(1)} all-to-all(bf16[4,256,128]{2,1,0:T(8,128)(2,1)S(1)} %broadcast_in_dim.18), channel_id=1, replica_groups=mesh['leaf'=4,'y'=4,'core'=2,'zhi'=4,'zlo'=8] {'y'}, dimensions={0} | all-to-all | bytes 524288 | tf_op jit(solution)/shard_map/all_to_all | solution.py:16
  41.0 26.2 %all_to_all.57 = bf16[8,32,640]{2,1,0:T(8,128)(2,1)S(1)} all-to-all(bf16[8,32,640]{2,1,0:T(8,128)(2,1)S(1)} %bitcast.63), channel_id=1, replica_groups=mesh['leaf'=4,'y'=4,'core'=2,'zhi'=4,'zlo'=8] {'zlo'}, dimensions={0} | all-to-all | bytes 655360 | tf_op jit(solution)/shard_map/all_to_all | solution.py:16
  68.0 27.4 %all-to-all-start.3 = ((bf16[4,32,512]{2,1,0:T(8,128)(2,1)}), bf16[4,32,512]{2,1,0:T(8,128)(2,1)S(1)}, u32[]{:S(2)}, u32[]{:S(2)}) async-start(bf16[4,32,512]{2,1,0:T(8,128)(2,1)} %broadcast_in_dim.20), calls=%async_computation.3 | async-start | bytes 262144 | tf_op jit(solution)/shard_map/all_to_all | solution.py:16
  96.8 24.5 %all-to-all-done.3 = bf16[4,32,512]{2,1,0:T(8,128)(2,1)S(1)} async-done(((bf16[4,32,512]{2,1,0:T(8,128)(2,1)}), bf16[4,32,512]{2,1,0:T(8,128)(2,1)S(1)}, u32[]{:S(2)}, u32[]{:S(2)}) %all-to-all-start.3) | async-done | bytes 131104 | tf_op jit(solution)/shard_map/all_to_all | solution.py:16
  121.4 8.8 %all_to_all.58.upd_ref = bf16[4,48,512]{2,1,0:T(8,128)(2,1)} all-to-all(bf16[4,48,512]{2,1,0:T(8,128)(2,1)S(1)} %broadcast_in_dim.21), channel_id=1, replica_groups=mesh['leaf'=4,'y'=4,'core'=2,'zhi'=4,'zlo'=8] {'leaf'}, dimensions={0} | all-to-all | bytes 393216 | tf_op jit(solution)/shard_map/all_to_all | solution.py:16
  130.2 9.4 %collective-permute-start = (bf16[8,320,512]{2,1,0:T(8,128)(2,1)}, bf16[8,320,512]{2,1,0:T(8,128)(2,1)S(1)}, u32[]{:S(2)}, u32[]{:S(2)}) collective-permute-start(bf16[8,320,512]{2,1,0:T(8,128)(2,1)} %bitcast.57), channel_id=1, source_target_pairs={{0,32},{32,0},{1,33},{33,1},{2,34},{34,2},{3,35},{35,3},{4,36},{36... | collective-permute-start | bytes 7864328 | tf_op jit(solution)/shard_map/ppermute | solution.py:203
  141.8 1.5 select_n.71.rhs_own
  145.9 1.5 copy-done.1
  147.4 3.9 %shard_map.78 = bf16[4,32,512]{2,1,0:T(8,128)(2,1)} custom-call(s32[16]{0:T(128)} %compare_select_fusion.2.slot_ref, bf16[4,48,512]{2,1,0:T(8,128)(2,1)} %all_to_all.58.upd_ref, bf16[32,1024]{1,0:T(8,128)(2,1)} %select_n.71.rhs_own, bf16[32,1024]{1,0:T(8,128)(2,1)} %select_n.73.rhs_oth, bf16[8,320,512]{2,1,0:T(8,128)(2,1)} %bitcast.58, ...), custom_call_target="tpu_custom_call" | custom-call | tf_op jit(solution)/shard_map/pallas_call | solution.py:145
  151.3 3.3 %all-to-all-start.5 = ((bf16[4,32,512]{2,1,0:T(8,128)(2,1)}), bf16[4,32,512]{2,1,0:T(8,128)(2,1)S(1)}, u32[]{:S(2)}, u32[]{:S(2)}) async-start(bf16[4,32,512]{2,1,0:T(8,128)(2,1)} %shard_map.78), calls=%async_computation.5 | async-start | bytes 262144 | tf_op jit(solution)/shard_map/all_to_all | solution.py:16
  155.4 4.4 %all-to-all-done.5.parts_ref = bf16[4,32,512]{2,1,0:T(8,128)(2,1)S(1)} async-done(((bf16[4,32,512]{2,1,0:T(8,128)(2,1)}), bf16[4,32,512]{2,1,0:T(8,128)(2,1)S(1)}, u32[]{:S(2)}, u32[]{:S(2)}) %all-to-all-start.5) | async-done | bytes 131104 | tf_op jit(solution)/shard_map/all_to_all | solution.py:16
  160.4 3.7 %shard_map.79 = bf16[4,64,512]{2,1,0:T(8,128)(2,1)} custom-call(s32[16]{0:T(128)} %reshape.211.slot_ref, bf16[4,32,512]{2,1,0:T(8,128)(2,1)} %copy-done.5, bf16[8,320,512]{2,1,0:T(8,128)(2,1)} %bitcast.59, bf16[8,320,512]{2,1,0:T(8,128)(2,1)} %copy-done.1), custom_call_target="tpu_custom_call" | custom-call | tf_op jit(solution)/shard_map/pallas_call | solution.py:145
  164.1 8.9 %all_to_all.59 = bf16[4,64,512]{2,1,0:T(8,128)(2,1)S(1)} all-to-all(bf16[4,64,512]{2,1,0:T(8,128)(2,1)} %shard_map.79), channel_id=1, replica_groups=mesh['leaf'=4,'y'=4,'core'=2,'zhi'=4,'zlo'=8] {'leaf'}, dimensions={0} | all-to-all | bytes 524288 | tf_op jit(solution)/shard_map/all_to_all | solution.py:16
  173.8 3.3 %all-to-all-start.7 = ((bf16[4,32,512]{2,1,0:T(8,128)(2,1)}), bf16[4,32,512]{2,1,0:T(8,128)(2,1)S(1)}, u32[]{:S(2)}, u32[]{:S(2)}) async-start(bf16[4,32,512]{2,1,0:T(8,128)(2,1)} %broadcast_in_dim.22), calls=%async_computation.7 | async-start | bytes 262144 | tf_op jit(solution)/shard_map/all_to_all | solution.py:16
  177.6 21.3 %all-to-all-done.7.parts_ref = bf16[4,32,512]{2,1,0:T(8,128)(2,1)S(1)} async-done(((bf16[4,32,512]{2,1,0:T(8,128)(2,1)}), bf16[4,32,512]{2,1,0:T(8,128)(2,1)S(1)}, u32[]{:S(2)}, u32[]{:S(2)}) %all-to-all-start.7) | async-done | bytes 131104 | tf_op jit(solution)/shard_map/all_to_all | solution.py:16
  199.5 3.1 %shard_map.80 = bf16[4,32,1024]{2,1,0:T(8,128)(2,1)} custom-call(bf16[4,32,512]{2,1,0:T(8,128)(2,1)} %copy-done.4, bf16[8,320,512]{2,1,0:T(8,128)(2,1)} %bitcast.60, bf16[8,320,512]{2,1,0:T(8,128)(2,1)} %copy-done.1), custom_call_target="tpu_custom_call" | custom-call | tf_op jit(solution)/shard_map/pallas_call | solution.py:145
  202.7 3.4 %all-to-all-start.8 = ((bf16[4,32,1024]{2,1,0:T(8,128)(2,1)}), bf16[4,32,1024]{2,1,0:T(8,128)(2,1)S(1)}, u32[]{:S(2)}, u32[]{:S(2)}) async-start(bf16[4,32,1024]{2,1,0:T(8,128)(2,1)} %shard_map.80), calls=%async_computation.8 | async-start | bytes 524288 | tf_op jit(solution)/shard_map/all_to_all | solution.py:16
  207.5 4.0 %all-to-all-done.8.parts_ref = bf16[4,32,1024]{2,1,0:T(8,128)(2,1)S(1)} async-done(((bf16[4,32,1024]{2,1,0:T(8,128)(2,1)}), bf16[4,32,1024]{2,1,0:T(8,128)(2,1)S(1)}, u32[]{:S(2)}, u32[]{:S(2)}) %all-to-all-start.8) | async-done | bytes 262176 | tf_op jit(solution)/shard_map/all_to_all | solution.py:16
  212.3 4.0 %shard_map.81 = bf16[2,512,32]{2,1,0:T(8,128)(2,1)} custom-call(s32[1]{0:T(128)} %bitcast.core_ref, bf16[32,1024]{1,0:T(8,128)(2,1)} %copy_bitcast_fusion.1.forward_ref, bf16[4,32,1024]{2,1,0:T(8,128)(2,1)} %copy-done.3, bf16[8,320,512]{2,1,0:T(8,128)(2,1)} %bitcast.61, bf16[8,320,512]{2,1,0:T(8,128)(2,1)} %copy-done.1), custom_call_target="tpu_custom_call" | custom-call | tf_op jit(solution)/shard_map/pallas_call | solution.py:145
  217.7 43.8 %all_to_all.60 = bf16[32,12,128]{2,1,0:T(8,128)(2,1)S(1)} all-to-all(bf16[32,12,128]{2,1,0:T(8,128)(2,1)S(1)} %reshape.216), channel_id=1, replica_groups=mesh['leaf'=4,'y'=4,'core'=2,'zhi'=4,'zlo'=8] {'zhi','zlo'}, dimensions={0} | all-to-all | bytes 196608 | tf_op jit(solution)/shard_map/all_to_all | solution.py:16
  262.4 7.1 %all-to-all-start.10 = ((bf16[8,48,128]{2,1,0:T(8,128)(2,1)}), bf16[8,48,128]{2,1,0:T(8,128)(2,1)S(1)}, u32[]{:S(2)}, u32[]{:S(2)}) async-start(bf16[8,48,128]{2,1,0:T(8,128)(2,1)} %reshape.222), calls=%async_computation.10 | async-start | bytes 196608 | tf_op jit(solution)/shard_map/all_to_all | solution.py:16
  269.5 5.0 %all-to-all-done.10 = bf16[8,48,128]{2,1,0:T(8,128)(2,1)S(1)} async-done(((bf16[8,48,128]{2,1,0:T(8,128)(2,1)}), bf16[8,48,128]{2,1,0:T(8,128)(2,1)S(1)}, u32[]{:S(2)}, u32[]{:S(2)}) %all-to-all-start.10) | async-done | bytes 98336 | tf_op jit(solution)/shard_map/all_to_all | solution.py:16
  (89 shorter events, 21.5 us)
Async XLA Ops:
  7.2 6.4 %copy-start = (bf16[1,512,512]{2,1,0:T(8,128)(2,1)S(1)}, bf16[1,512,512]{2,1,0:T(8,128)(2,1)}, u32[]{:S(2)}) copy-start(bf16[1,512,512]{2,1,0:T(8,128)(2,1)} %param.12) | copy-start | bytes 1572868
  7.2 6.4 %copy-start.6 = (bf16[1,128,512]{2,1,0:T(8,128)(2,1)S(1)}, bf16[1,128,512]{2,1,0:T(8,128)(2,1)}, u32[]{:S(2)}) copy-start(bf16[1,128,512]{2,1,0:T(8,128)(2,1)} %param.10) | copy-start | bytes 393220
  7.2 123.0 %all-gather.3.cloned.1.call-start = ((), (), s32[]{:S(2)}) async-start(), calls=%async_computation.11 | async-start | bytes 2949120 | tf_op jit(solution)/shard_map/all_gather | solution.py:174
  67.2 62.9 %copy-start.2 = (bf16[8,32,640]{2,1,0:T(8,128)(2,1)}, bf16[8,32,640]{2,1,0:T(8,128)(2,1)S(1)}, u32[]{:S(2)}) copy-start(bf16[8,32,640]{2,1,0:T(8,128)(2,1)S(1)} %all_to_all.57) | copy-start | bytes 983044
  68.0 53.3 %all-to-all-start.3 = ((bf16[4,32,512]{2,1,0:T(8,128)(2,1)}), bf16[4,32,512]{2,1,0:T(8,128)(2,1)S(1)}, u32[]{:S(2)}, u32[]{:S(2)}) async-start(bf16[4,32,512]{2,1,0:T(8,128)(2,1)} %broadcast_in_dim.20), calls=%async_computation.3 | async-start | bytes 262144 | tf_op jit(solution)/shard_map/all_to_all | solution.py:16
  130.2 15.7 %collective-permute-start = (bf16[8,320,512]{2,1,0:T(8,128)(2,1)}, bf16[8,320,512]{2,1,0:T(8,128)(2,1)S(1)}, u32[]{:S(2)}, u32[]{:S(2)}) collective-permute-start(bf16[8,320,512]{2,1,0:T(8,128)(2,1)} %bitcast.57), channel_id=1, source_target_pairs={{0,32},{32,0},{1,33},{33,1},{2,34},{34,2},{3,35},{35,3},{4,36},{36... | collective-permute-start | bytes 7864328 | tf_op jit(solution)/shard_map/ppermute | solution.py:203
  145.9 1.5 copy-start.1
  151.3 8.4 %all-to-all-start.5 = ((bf16[4,32,512]{2,1,0:T(8,128)(2,1)}), bf16[4,32,512]{2,1,0:T(8,128)(2,1)S(1)}, u32[]{:S(2)}, u32[]{:S(2)}) async-start(bf16[4,32,512]{2,1,0:T(8,128)(2,1)} %shard_map.78), calls=%async_computation.5 | async-start | bytes 262144 | tf_op jit(solution)/shard_map/all_to_all | solution.py:16
  159.7 0.7 copy-start.5
  173.8 25.1 %all-to-all-start.7 = ((bf16[4,32,512]{2,1,0:T(8,128)(2,1)}), bf16[4,32,512]{2,1,0:T(8,128)(2,1)S(1)}, u32[]{:S(2)}, u32[]{:S(2)}) async-start(bf16[4,32,512]{2,1,0:T(8,128)(2,1)} %broadcast_in_dim.22), calls=%async_computation.7 | async-start | bytes 262144 | tf_op jit(solution)/shard_map/all_to_all | solution.py:16
  198.9 0.7 copy-start.4
  202.7 8.9 %all-to-all-start.8 = ((bf16[4,32,1024]{2,1,0:T(8,128)(2,1)}), bf16[4,32,1024]{2,1,0:T(8,128)(2,1)S(1)}, u32[]{:S(2)}, u32[]{:S(2)}) async-start(bf16[4,32,1024]{2,1,0:T(8,128)(2,1)} %shard_map.80), calls=%async_computation.8 | async-start | bytes 524288 | tf_op jit(solution)/shard_map/all_to_all | solution.py:16
  211.6 0.7 copy-start.3
  262.4 12.1 %all-to-all-start.10 = ((bf16[8,48,128]{2,1,0:T(8,128)(2,1)}), bf16[8,48,128]{2,1,0:T(8,128)(2,1)S(1)}, u32[]{:S(2)}, u32[]{:S(2)}) async-start(bf16[8,48,128]{2,1,0:T(8,128)(2,1)} %reshape.222), calls=%async_computation.10 | async-start | bytes 196608 | tf_op jit(solution)/shard_map/all_to_all | solution.py:16
Sparse Core Ops, SparseCore 0:
  10.7 109.5 all-gather.2

commit v8 on v7

--- a/solution.py
+++ b/solution.py
@@ -44,25 +44,14 @@
         out_ref[PANEL_ROWS[0]:, f * TILE:(f + 1) * TILE] = panel_ref[f * few:(f + 1) * few]
 
 
-def fetch(refs, span, buf_ref, sems):
-    copies = [
-        pltpu.make_async_copy(ref.at[:, pl.ds(*span)], buf_ref.at[i], sems.at[i])
-        for i, ref in enumerate(refs)
-    ]
-    for copy in copies:
-        copy.start()
-    return copies
-
-
-def root_half(buf_ref, i):
-    j = i % 2
-    return buf_ref[i // 2, :, j * QUARTER:(j + 1) * QUARTER, :].reshape(ZLO * QUARTER, buf_ref.shape[3])
-
-
-def place_kernel(slot_ref, upd_ref, rhs_own, rhs_oth, own_ref, oth_ref, out_ref, buf_ref, sems, side_ref):
-    copies = fetch((own_ref, oth_ref), ROOT_ROWS, buf_ref, sems)
+def root_half(refs, i):
+    ref, j = refs[i // 2], i % 2
+    return ref[:, j * QUARTER:(j + 1) * QUARTER, :].reshape(ZLO * QUARTER, ref.shape[2])
+
+
+def place_kernel(slot_ref, upd_ref, rhs_own, rhs_oth, own_ref, oth_ref, out_ref, side_ref):
     half = rhs_own.shape[1]
-    lanes = buf_ref.shape[3]
+    lanes = own_ref.shape[2]
     side_ref[:, :half] = rhs_own[...].astype(F32)
     side_ref[:, half:] = rhs_oth[...].astype(F32)
     width = side_ref.shape[0]
@@ -70,27 +59,22 @@
         for u in range(4):
             at = pl.ds(pl.multiple_of(slot_ref[k * 4 + u] * TILE, TILE), TILE)
             side_ref[:, at] = side_ref[:, at] - upd_ref[k, :width, u * TILE:(u + 1) * TILE].astype(F32)
-    for copy in copies:
-        copy.wait()
     out = 0.0
     for i in range(4):
         side = side_ref[:, i * lanes:(i + 1) * lanes].astype(BF)
-        out = out + dot(side, root_half(buf_ref, i), ((1,), (1,)))
+        out = out + dot(side, root_half((own_ref, oth_ref), i), ((1,), (1,)))
     for k in range(Y):
         out_ref[k] = out.astype(BF)
 
 
-def spread_kernel(slot_ref, parts_ref, own_ref, oth_ref, out_ref, buf_ref, sems, sol_ref):
-    copies = fetch((own_ref, oth_ref), ROOT_ROWS, buf_ref, sems)
-    lanes = buf_ref.shape[3]
+def spread_kernel(slot_ref, parts_ref, own_ref, oth_ref, out_ref, sol_ref):
+    lanes = own_ref.shape[2]
     forward = parts_ref[0].astype(F32)
     for k in range(1, Y):
         forward = forward + parts_ref[k].astype(F32)
     forward = forward.astype(BF)
-    for copy in copies:
-        copy.wait()
     for i in range(4):
-        sol_ref[:, i * lanes:(i + 1) * lanes] = dot(forward, root_half(buf_ref, i), ((1,), (0,)))
+        sol_ref[:, i * lanes:(i + 1) * lanes] = dot(forward, root_half((own_ref, oth_ref), i), ((1,), (0,)))
     width, span = forward.shape[0], 4 * TILE
     few = width // LEAF
     for k in range(LEAF):
@@ -102,55 +86,45 @@
         out_ref[k, width:, :] = mine.astype(BF)
 
 
-def correct_kernel(parts_ref, own_ref, oth_ref, out_ref, buf_ref, sems):
-    copies = fetch((own_ref, oth_ref), PANEL_ROWS, buf_ref, sems)
+def correct_kernel(parts_ref, own_ref, oth_ref, out_ref):
     picked = parts_ref[0].astype(F32)
     for k in range(1, ZHI):
         picked = picked + parts_ref[k].astype(F32)
     picked = picked.astype(BF)
     half = picked.shape[1] // 2
-    n, lanes = TILE, buf_ref.shape[3]
-    for copy in copies:
-        copy.wait()
+    n, lanes = TILE, own_ref.shape[2]
     for z in range(ZLO):
         out = 0.0
-        for i in range(CORE):
-            panel = jnp.concatenate([buf_ref[i, z, :, f:f + TILE] for f in range(0, lanes, TILE)], axis=0)
+        for i, ref in enumerate((own_ref, oth_ref)):
+            panel = jnp.concatenate([ref[z, :, f:f + TILE] for f in range(0, lanes, TILE)], axis=0)
             out = out + dot(picked[:, i * half:(i + 1) * half], panel, ((1,), (0,)))
         for k in range(Y):
             out_ref[k, :, z * n:(z + 1) * n] = out.astype(BF)
 
 
-def solve_kernel(core_ref, forward_ref, parts_ref, own_ref, oth_ref, out_ref, buf_ref, sems):
-    copies = fetch((own_ref, oth_ref), INV_ROWS, buf_ref, sems)
+def solve_kernel(core_ref, forward_ref, parts_ref, own_ref, oth_ref, out_ref):
     correction = parts_ref[0].astype(F32)
     for k in range(1, Y):
         correction = correction + parts_ref[k].astype(F32)
     residue = forward_ref[...].astype(F32) - correction.astype(BF).astype(F32)
     residue = residue.astype(BF)
     core = core_ref[0]
-    for copy in copies:
-        copy.wait()
-    for i in range(CORE):
-        inv = buf_ref[i].reshape(ZLO * INV, buf_ref.shape[3])
+    for i, ref in enumerate((own_ref, oth_ref)):
+        inv = ref[...].reshape(ZLO * INV, ref.shape[2])
         out_ref[(core + i) % CORE] = dot(inv, residue, ((0,), (1,))).astype(BF)
 
 
 def call(kernel, out_shape, inputs, scalars=(), gathered=(), span=None, scratch=()):
     vmem = pl.BlockSpec(memory_space=pltpu.VMEM)
-    buffers = []
-    if gathered:
-        blocks, _, lanes = gathered[0].shape
-        buffers = [pltpu.VMEM((len(gathered), blocks, span[1], lanes), BF), pltpu.SemaphoreType.DMA((len(gathered),))]
+    inputs = tuple(inputs) + tuple(g[:, span[0]:span[0] + span[1]] for g in gathered)
     return pl.pallas_call(
         kernel,
         out_shape=out_shape,
-        in_specs=[pl.BlockSpec(memory_space=pltpu.SMEM)] * len(scalars)
-        + [vmem] * len(inputs)
-        + [pl.BlockSpec(memory_space=pl.ANY)] * len(gathered),
+        in_specs=[pl.BlockSpec(memory_space=pltpu.SMEM)] * len(scalars) + [vmem] * len(inputs),
         out_specs=vmem,
-        scratch_shapes=buffers + list(scratch),
-    )(*scalars, *inputs, *gathered)
+        scratch_shapes=list(scratch),
+        compiler_params=pltpu.CompilerParams(vmem_limit_bytes=16 * 1024 * 1024),
+    )(*scalars, *inputs)
 
 
 def body(child_inv, child_panel, child_rhs, anc_tiles, root_inv, root_rhs):

time: 285 us -> 274 us (0.961)
  Pallas kernels: 16.6 us -> 5.42 us
  local copies, waits for them, and re-layouts: 16.9 us -> 21.5 us
    pallas_call x5, Pallas kernels: 16.6 us -> 5.42 us  [call(): pl.pallas_call(kernel, out_shape=out_shape, in_specs=[pl.BlockSpec(memory...]
    slice x0 -> x4, local copies, waits for them, and re-layouts: none -> 8.6 us  [call(): g[:, span[0]:span[0] + span[1]]]
    unnamed x18 -> x22, local copies, waits for them, and re-layouts: 5.77 us -> 6.83 us
  transfers between devices with their start and end apart: 7 -> 7, of which waited for: 5 -> 6; matrix products, arithmetic and copies ran while one was open for 6% -> 6% of each run, Pallas kernels for 0% -> 0%
where the time goes in v8:
time: 274 us; the launch traced here: 273 us
  blocking collectives  116 us (42%)
  waiting for transfers between devices  58.3 us (21%)
  starting transfers between devices  51.6 us (19%)
  local copies, waits for them, and re-layouts  21.5 us (8%)
  between operations  14.4 us (5%)
  Pallas kernels  5.42 us (2%)
  other arithmetic  5.11 us (2%)
    all_to_all x6, blocking collectives, exchange(): return lax.all_to_all(x, axis, 0, 0, tiled=True)  116 us
    all_to_all x5, waiting for transfers between devices, exchange(): return lax.all_to_all(x, axis, 0, 0, tiled=True)  57.6 us
    all_to_all x5, starting transfers between devices, exchange(): return lax.all_to_all(x, axis, 0, 0, tiled=True)  42.5 us
    ppermute x1, starting transfers between devices, body(): both = (packed, lax.ppermute(packed, 'core', other))  9.03 us
    slice x4, local copies, waits for them, and re-layouts, call(): g[:, span[0]:span[0] + span[1]]  8.6 us
    unnamed x22, local copies, waits for them, and re-layouts  6.83 us
  transfers between devices with their start and end apart: 7, of which 6 were waited for; matrix products, arithmetic and copies ran while one was open for 6% of the time, Pallas kernels for 0%

profile of v8, /device:TPU:1, one launch (start us, length us, event | category | flops | bytes accessed | tf_op | source)
XLA Modules:
  0.0 272.9 jit_solution(8218208978944801762)
XLA Ops:
  11.5 1.3 fusion.3
  13.6 1.5 copy.42
  15.7 17.8 %all_to_all.55 = bf16[2,784,128]{2,1,0:T(8,128)(2,1)S(1)} all-to-all(bf16[2,784,128]{2,1,0:T(8,128)(2,1)S(1)} %pad_maximum_fusion), channel_id=1, replica_groups=mesh['leaf'=4,'y'=4,'core'=2,'zhi'=4,'zlo'=8] {'core'}, dimensions={0} | all-to-all | bytes 802816 | tf_op jit(solution)/shard_map/all_to_all | solution.py:16
  33.5 8.8 %all_to_all.56 = bf16[4,256,128]{2,1,0:T(8,128)(2,1)S(1)} all-to-all(bf16[4,256,128]{2,1,0:T(8,128)(2,1)S(1)} %broadcast_in_dim.18), channel_id=1, replica_groups=mesh['leaf'=4,'y'=4,'core'=2,'zhi'=4,'zlo'=8] {'y'}, dimensions={0} | all-to-all | bytes 524288 | tf_op jit(solution)/shard_map/all_to_all | solution.py:16
  42.7 31.5 %all_to_all.57 = bf16[8,32,640]{2,1,0:T(8,128)(2,1)S(1)} all-to-all(bf16[8,32,640]{2,1,0:T(8,128)(2,1)S(1)} %bitcast.65), channel_id=1, replica_groups=mesh['leaf'=4,'y'=4,'core'=2,'zhi'=4,'zlo'=8] {'zlo'}, dimensions={0} | all-to-all | bytes 655360 | tf_op jit(solution)/shard_map/all_to_all | solution.py:16
  75.6 20.8 %all-to-all-start.3 = ((bf16[4,32,512]{2,1,0:T(8,128)(2,1)}), bf16[4,32,512]{2,1,0:T(8,128)(2,1)S(1)}, u32[]{:S(2)}, u32[]{:S(2)}) async-start(bf16[4,32,512]{2,1,0:T(8,128)(2,1)} %broadcast_in_dim.20), calls=%async_computation.3 | async-start | bytes 262144 | tf_op jit(solution)/shard_map/all_to_all | solution.py:16
  97.8 25.2 %all-to-all-done.3 = bf16[4,32,512]{2,1,0:T(8,128)(2,1)S(1)} async-done(((bf16[4,32,512]{2,1,0:T(8,128)(2,1)}), bf16[4,32,512]{2,1,0:T(8,128)(2,1)S(1)}, u32[]{:S(2)}, u32[]{:S(2)}) %all-to-all-start.3) | async-done | bytes 131104 | tf_op jit(solution)/shard_map/all_to_all | solution.py:16
  123.0 9.7 %all_to_all.58.upd_ref = bf16[4,48,512]{2,1,0:T(8,128)(2,1)S(1)} all-to-all(bf16[4,48,512]{2,1,0:T(8,128)(2,1)S(1)} %broadcast_in_dim.21), channel_id=1, replica_groups=mesh['leaf'=4,'y'=4,'core'=2,'zhi'=4,'zlo'=8] {'leaf'}, dimensions={0} | all-to-all | bytes 393216 | tf_op jit(solution)/shard_map/all_to_all | solution.py:16
  132.8 9.0 %collective-permute-start = (bf16[8,320,512]{2,1,0:T(8,128)(2,1)}, bf16[8,320,512]{2,1,0:T(8,128)(2,1)}, u32[]{:S(2)}, u32[]{:S(2)}) collective-permute-start(bf16[8,320,512]{2,1,0:T(8,128)(2,1)} %bitcast.61), channel_id=1, source_target_pairs={{0,32},{32,0},{1,33},{33,1},{2,34},{34,2},{3,35},{35,3},{4,36},{36... | collective-permute-start | bytes 7864328 | tf_op jit(solution)/shard_map/ppermute | solution.py:177
  143.3 2.8 %fusion.8 = (bf16[8,128,512]{2,1,0:T(8,128)(2,1)}, bf16[8,128,512]{2,1,0:T(8,128)(2,1)S(1)}) fusion(bf16[8,320,512]{2,1,0:T(8,128)(2,1)} %bitcast.62), kind=kLoop, calls=%fused_computation.38 | loop fusion | bytes 4194304 | tf_op jit(solution)/shard_map/slice | solution.py:119
  146.6 2.7 %fusion.7 = (bf16[8,128,512]{2,1,0:T(8,128)(2,1)}, bf16[8,128,512]{2,1,0:T(8,128)(2,1)S(1)}) fusion(bf16[8,320,512]{2,1,0:T(8,128)(2,1)} %collective-permute-done), kind=kLoop, calls=%fused_computation.37 | loop fusion | bytes 4194304 | tf_op jit(solution)/shard_map/slice | solution.py:119
  149.4 1.9 shard_map.78
  151.3 3.3 %all-to-all-start.5 = ((bf16[4,32,512]{2,1,0:T(8,128)(2,1)}), bf16[4,32,512]{2,1,0:T(8,128)(2,1)S(1)}, u32[]{:S(2)}, u32[]{:S(2)}) async-start(bf16[4,32,512]{2,1,0:T(8,128)(2,1)} %shard_map.78), calls=%async_computation.5 | async-start | bytes 262144 | tf_op jit(solution)/shard_map/all_to_all | solution.py:16
  154.9 4.6 %all-to-all-done.5.parts_ref = bf16[4,32,512]{2,1,0:T(8,128)(2,1)S(1)} async-done(((bf16[4,32,512]{2,1,0:T(8,128)(2,1)}), bf16[4,32,512]{2,1,0:T(8,128)(2,1)S(1)}, u32[]{:S(2)}, u32[]{:S(2)}) %all-to-all-start.5) | async-done | bytes 131104 | tf_op jit(solution)/shard_map/all_to_all | solution.py:16
  160.5 7.9 %all_to_all.59 = bf16[4,64,512]{2,1,0:T(8,128)(2,1)S(1)} all-to-all(bf16[4,64,512]{2,1,0:T(8,128)(2,1)S(1)} %shard_map.79), channel_id=1, replica_groups=mesh['leaf'=4,'y'=4,'core'=2,'zhi'=4,'zlo'=8] {'leaf'}, dimensions={0} | all-to-all | bytes 524288 | tf_op jit(solution)/shard_map/all_to_all | solution.py:16
  169.1 4.2 %all-to-all-start.7 = ((bf16[4,32,512]{2,1,0:T(8,128)(2,1)}), bf16[4,32,512]{2,1,0:T(8,128)(2,1)S(1)}, u32[]{:S(2)}, u32[]{:S(2)}) async-start(bf16[4,32,512]{2,1,0:T(8,128)(2,1)} %broadcast_in_dim.22), calls=%async_computation.7 | async-start | bytes 262144 | tf_op jit(solution)/shard_map/all_to_all | solution.py:16
  173.4 1.2 slice.125.own_ref
  174.6 1.9 slice.145.oth_ref
  177.0 18.1 %all-to-all-done.7.parts_ref = bf16[4,32,512]{2,1,0:T(8,128)(2,1)S(1)} async-done(((bf16[4,32,512]{2,1,0:T(8,128)(2,1)}), bf16[4,32,512]{2,1,0:T(8,128)(2,1)S(1)}, u32[]{:S(2)}, u32[]{:S(2)}) %all-to-all-start.7) | async-done | bytes 131104 | tf_op jit(solution)/shard_map/all_to_all | solution.py:16
  197.1 4.9 %all-to-all-start.8 = ((bf16[4,32,1024]{2,1,0:T(8,128)(2,1)}), bf16[4,32,1024]{2,1,0:T(8,128)(2,1)S(1)}, u32[]{:S(2)}, u32[]{:S(2)}) async-start(bf16[4,32,1024]{2,1,0:T(8,128)(2,1)} %shard_map.80), calls=%async_computation.8 | async-start | bytes 524288 | tf_op jit(solution)/shard_map/all_to_all | solution.py:16
  202.9 4.7 %all-to-all-done.8.parts_ref = bf16[4,32,1024]{2,1,0:T(8,128)(2,1)S(1)} async-done(((bf16[4,32,1024]{2,1,0:T(8,128)(2,1)}), bf16[4,32,1024]{2,1,0:T(8,128)(2,1)S(1)}, u32[]{:S(2)}, u32[]{:S(2)}) %all-to-all-start.8) | async-done | bytes 262176 | tf_op jit(solution)/shard_map/all_to_all | solution.py:16
  208.7 40.3 %all_to_all.60 = bf16[32,12,128]{2,1,0:T(8,128)(2,1)S(1)} all-to-all(bf16[32,12,128]{2,1,0:T(8,128)(2,1)S(1)} %reshape.216), channel_id=1, replica_groups=mesh['leaf'=4,'y'=4,'core'=2,'zhi'=4,'zlo'=8] {'zhi','zlo'}, dimensions={0} | all-to-all | bytes 196608 | tf_op jit(solution)/shard_map/all_to_all | solution.py:16
  250.0 9.2 %all-to-all-start.10 = ((bf16[8,48,128]{2,1,0:T(8,128)(2,1)}), bf16[8,48,128]{2,1,0:T(8,128)(2,1)S(1)}, u32[]{:S(2)}, u32[]{:S(2)}) async-start(bf16[8,48,128]{2,1,0:T(8,128)(2,1)} %reshape.222), calls=%async_computation.10 | async-start | bytes 196608 | tf_op jit(solution)/shard_map/all_to_all | solution.py:16
  259.2 5.0 %all-to-all-done.10 = bf16[8,48,128]{2,1,0:T(8,128)(2,1)S(1)} async-done(((bf16[8,48,128]{2,1,0:T(8,128)(2,1)}), bf16[8,48,128]{2,1,0:T(8,128)(2,1)S(1)}, u32[]{:S(2)}, u32[]{:S(2)}) %all-to-all-start.10) | async-done | bytes 98336 | tf_op jit(solution)/shard_map/all_to_all | solution.py:16
  (97 shorter events, 20.0 us)
Async XLA Ops:
  7.2 8.1 %copy-start = (bf16[1,512,512]{2,1,0:T(8,128)(2,1)S(1)}, bf16[1,512,512]{2,1,0:T(8,128)(2,1)}, u32[]{:S(2)}) copy-start(bf16[1,512,512]{2,1,0:T(8,128)(2,1)} %param.12) | copy-start | bytes 1572868
  7.2 125.6 %all-gather.3.cloned.1.call-start = ((), (), s32[]{:S(2)}) async-start(), calls=%async_computation.11 | async-start | bytes 2949120 | tf_op jit(solution)/shard_map/all_gather | solution.py:148
  7.2 1.1 copy-start.4
  8.3 0.9 copy-start.5
  9.2 0.8 copy-start.7
  10.1 5.2 %copy-start.6 = (bf16[1,128,512]{2,1,0:T(8,128)(2,1)S(1)}, bf16[1,128,512]{2,1,0:T(8,128)(2,1)}, u32[]{:S(2)}) copy-start(bf16[1,128,512]{2,1,0:T(8,128)(2,1)} %param.10) | copy-start | bytes 393220
  74.1 0.7 copy-start.8
  75.6 47.4 %all-to-all-start.3 = ((bf16[4,32,512]{2,1,0:T(8,128)(2,1)}), bf16[4,32,512]{2,1,0:T(8,128)(2,1)S(1)}, u32[]{:S(2)}, u32[]{:S(2)}) async-start(bf16[4,32,512]{2,1,0:T(8,128)(2,1)} %broadcast_in_dim.20), calls=%async_computation.3 | async-start | bytes 262144 | tf_op jit(solution)/shard_map/all_to_all | solution.py:16
  132.8 13.9 %collective-permute-start = (bf16[8,320,512]{2,1,0:T(8,128)(2,1)}, bf16[8,320,512]{2,1,0:T(8,128)(2,1)}, u32[]{:S(2)}, u32[]{:S(2)}) collective-permute-start(bf16[8,320,512]{2,1,0:T(8,128)(2,1)} %bitcast.61), channel_id=1, source_target_pairs={{0,32},{32,0},{1,33},{33,1},{2,34},{34,2},{3,35},{35,3},{4,36},{36... | collective-permute-start | bytes 7864328 | tf_op jit(solution)/shard_map/ppermute | solution.py:177
  151.3 8.1 %all-to-all-start.5 = ((bf16[4,32,512]{2,1,0:T(8,128)(2,1)}), bf16[4,32,512]{2,1,0:T(8,128)(2,1)S(1)}, u32[]{:S(2)}, u32[]{:S(2)}) async-start(bf16[4,32,512]{2,1,0:T(8,128)(2,1)} %shard_map.78), calls=%async_computation.5 | async-start | bytes 262144 | tf_op jit(solution)/shard_map/all_to_all | solution.py:16
  169.1 26.0 %all-to-all-start.7 = ((bf16[4,32,512]{2,1,0:T(8,128)(2,1)}), bf16[4,32,512]{2,1,0:T(8,128)(2,1)S(1)}, u32[]{:S(2)}, u32[]{:S(2)}) async-start(bf16[4,32,512]{2,1,0:T(8,128)(2,1)} %broadcast_in_dim.22), calls=%async_computation.7 | async-start | bytes 262144 | tf_op jit(solution)/shard_map/all_to_all | solution.py:16
  173.4 34.2 %copy-start.1 = (bf16[8,128,512]{2,1,0:T(8,128)(2,1)S(1)}, bf16[8,128,512]{2,1,0:T(8,128)(2,1)}, u32[]{:S(2)}) copy-start(bf16[8,128,512]{2,1,0:T(8,128)(2,1)} %get-tuple-element.46.own_ref) | copy-start | bytes 3145732
  173.4 34.2 %copy-start.2 = (bf16[8,128,512]{2,1,0:T(8,128)(2,1)S(1)}, bf16[8,128,512]{2,1,0:T(8,128)(2,1)}, u32[]{:S(2)}) copy-start(bf16[8,128,512]{2,1,0:T(8,128)(2,1)} %get-tuple-element.44.oth_ref) | copy-start | bytes 3145732
  195.1 1.0 copy-start.3
  197.1 10.5 %all-to-all-start.8 = ((bf16[4,32,1024]{2,1,0:T(8,128)(2,1)}), bf16[4,32,1024]{2,1,0:T(8,128)(2,1)S(1)}, u32[]{:S(2)}, u32[]{:S(2)}) async-start(bf16[4,32,1024]{2,1,0:T(8,128)(2,1)} %shard_map.80), calls=%async_computation.8 | async-start | bytes 524288 | tf_op jit(solution)/shard_map/all_to_all | solution.py:16
  250.0 14.2 %all-to-all-start.10 = ((bf16[8,48,128]{2,1,0:T(8,128)(2,1)}), bf16[8,48,128]{2,1,0:T(8,128)(2,1)S(1)}, u32[]{:S(2)}, u32[]{:S(2)}) async-start(bf16[8,48,128]{2,1,0:T(8,128)(2,1)} %reshape.222), calls=%async_computation.10 | async-start | bytes 196608 | tf_op jit(solution)/shard_map/all_to_all | solution.py:16
Sparse Core Ops, SparseCore 0:
  11.0 112.3 all-gather.2

commit v9 on v8

--- a/solution.py
+++ b/solution.py
@@ -200,6 +200,7 @@
         wide,
     )
     sol = total(exchange(sol, "leaf")).astype(BF)
+    both, sol = lax.optimization_barrier((both, sol))
     picked, root = share(sol[:width], "zhi", ZHI), sol[width:]
 
     cols = ZHI * ZLO

time: 274 us -> 271 us (0.989)
  local copies, waits for them, and re-layouts: 21.5 us -> 17.8 us
  waiting for transfers between devices: 58.3 us -> 61.7 us
    unnamed x22 -> x14, local copies, waits for them, and re-layouts: 6.83 us -> 5.05 us
    slice x4 -> x6, local copies, waits for them, and re-layouts: 8.6 us -> 7.5 us  [call(): g[:, span[0]:span[0] + span[1]]]
where the time goes in v9:
time: 271 us; the launch traced here: 270 us
  blocking collectives  114 us (42%)
  waiting for transfers between devices  61.7 us (23%)
  starting transfers between devices  51.3 us (19%)
  local copies, waits for them, and re-layouts  17.8 us (7%)
  between operations  14.5 us (5%)
  Pallas kernels  5.45 us (2%)
  other arithmetic  5.11 us (2%)
    all_to_all x6, blocking collectives, exchange(): return lax.all_to_all(x, axis, 0, 0, tiled=True)  114 us
    all_to_all x5, waiting for transfers between devices, exchange(): return lax.all_to_all(x, axis, 0, 0, tiled=True)  59.7 us
    all_to_all x5, starting transfers between devices, exchange(): return lax.all_to_all(x, axis, 0, 0, tiled=True)  41.6 us
    ppermute x1, starting transfers between devices, body(): both = (packed, lax.ppermute(packed, 'core', other))  9.6 us
    slice x6, local copies, waits for them, and re-layouts, call(): g[:, span[0]:span[0] + span[1]]  7.5 us
    pallas_call x5, Pallas kernels, call(): pl.pallas_call(kernel, out_shape=out_shape, in_specs=[pl.BlockSpec(memory...  5.45 us
  transfers between devices with their start and end apart: 7, of which 6 were waited for; matrix products, arithmetic and copies ran while one was open for 6% of the time, Pallas kernels for 0%

profile of v9, /device:TPU:1, one launch (start us, length us, event | category | flops | bytes accessed | tf_op | source)
XLA Modules:
  0.0 270.1 jit_solution(9727566265942427632)
XLA Ops:
  13.6 1.5 copy.42
  15.7 17.8 %all_to_all.55 = bf16[2,784,128]{2,1,0:T(8,128)(2,1)S(1)} all-to-all(bf16[2,784,128]{2,1,0:T(8,128)(2,1)S(1)} %pad_maximum_fusion), channel_id=1, replica_groups=mesh['leaf'=4,'y'=4,'core'=2,'zhi'=4,'zlo'=8] {'core'}, dimensions={0} | all-to-all | bytes 802816 | tf_op jit(solution)/shard_map/all_to_all | solution.py:16
  33.5 8.8 %all_to_all.56 = bf16[4,256,128]{2,1,0:T(8,128)(2,1)S(1)} all-to-all(bf16[4,256,128]{2,1,0:T(8,128)(2,1)S(1)} %broadcast_in_dim.18), channel_id=1, replica_groups=mesh['leaf'=4,'y'=4,'core'=2,'zhi'=4,'zlo'=8] {'y'}, dimensions={0} | all-to-all | bytes 524288 | tf_op jit(solution)/shard_map/all_to_all | solution.py:16
  42.7 31.5 %all_to_all.57 = bf16[8,32,640]{2,1,0:T(8,128)(2,1)S(1)} all-to-all(bf16[8,32,640]{2,1,0:T(8,128)(2,1)S(1)} %bitcast.66), channel_id=1, replica_groups=mesh['leaf'=4,'y'=4,'core'=2,'zhi'=4,'zlo'=8] {'zlo'}, dimensions={0} | all-to-all | bytes 655360 | tf_op jit(solution)/shard_map/all_to_all | solution.py:16
  74.9 20.8 %all-to-all-start.3 = ((bf16[4,32,512]{2,1,0:T(8,128)(2,1)}), bf16[4,32,512]{2,1,0:T(8,128)(2,1)S(1)}, u32[]{:S(2)}, u32[]{:S(2)}) async-start(bf16[4,32,512]{2,1,0:T(8,128)(2,1)} %broadcast_in_dim.20), calls=%async_computation.3 | async-start | bytes 262144 | tf_op jit(solution)/shard_map/all_to_all | solution.py:16
  97.0 25.5 %all-to-all-done.3 = bf16[4,32,512]{2,1,0:T(8,128)(2,1)S(1)} async-done(((bf16[4,32,512]{2,1,0:T(8,128)(2,1)}), bf16[4,32,512]{2,1,0:T(8,128)(2,1)S(1)}, u32[]{:S(2)}, u32[]{:S(2)}) %all-to-all-start.3) | async-done | bytes 131104 | tf_op jit(solution)/shard_map/all_to_all | solution.py:16
  122.6 9.1 %all_to_all.58.upd_ref = bf16[4,48,512]{2,1,0:T(8,128)(2,1)S(1)} all-to-all(bf16[4,48,512]{2,1,0:T(8,128)(2,1)S(1)} %broadcast_in_dim.21), channel_id=1, replica_groups=mesh['leaf'=4,'y'=4,'core'=2,'zhi'=4,'zlo'=8] {'leaf'}, dimensions={0} | all-to-all | bytes 393216 | tf_op jit(solution)/shard_map/all_to_all | solution.py:16
  131.7 9.6 %collective-permute-start = (bf16[8,320,512]{2,1,0:T(8,128)(2,1)}, bf16[8,320,512]{2,1,0:T(8,128)(2,1)}, u32[]{:S(2)}, u32[]{:S(2)}) collective-permute-start(bf16[8,320,512]{2,1,0:T(8,128)(2,1)} %bitcast.61), channel_id=1, source_target_pairs={{0,32},{32,0},{1,33},{33,1},{2,34},{34,2},{3,35},{35,3},{4,36},{36... | collective-permute-start | bytes 7864328 | tf_op jit(solution)/shard_map/ppermute | solution.py:177
  141.4 1.3 slice.119.own_ref
  144.2 2.0 collective-permute-done
  146.2 1.3 slice.140.oth_ref
  147.5 1.9 shard_map.78
  149.5 3.3 %all-to-all-start.5 = ((bf16[4,32,512]{2,1,0:T(8,128)(2,1)}), bf16[4,32,512]{2,1,0:T(8,128)(2,1)S(1)}, u32[]{:S(2)}, u32[]{:S(2)}) async-start(bf16[4,32,512]{2,1,0:T(8,128)(2,1)} %shard_map.78), calls=%async_computation.5 | async-start | bytes 262144 | tf_op jit(solution)/shard_map/all_to_all | solution.py:16
  153.0 4.6 %all-to-all-done.5.parts_ref = bf16[4,32,512]{2,1,0:T(8,128)(2,1)S(1)} async-done(((bf16[4,32,512]{2,1,0:T(8,128)(2,1)}), bf16[4,32,512]{2,1,0:T(8,128)(2,1)S(1)}, u32[]{:S(2)}, u32[]{:S(2)}) %all-to-all-start.5) | async-done | bytes 131104 | tf_op jit(solution)/shard_map/all_to_all | solution.py:16
  158.6 7.9 %all_to_all.59 = bf16[4,64,512]{2,1,0:T(8,128)(2,1)S(1)} all-to-all(bf16[4,64,512]{2,1,0:T(8,128)(2,1)S(1)} %shard_map.79), channel_id=1, replica_groups=mesh['leaf'=4,'y'=4,'core'=2,'zhi'=4,'zlo'=8] {'leaf'}, dimensions={0} | all-to-all | bytes 524288 | tf_op jit(solution)/shard_map/all_to_all | solution.py:16
  167.3 4.7 %all-to-all-start.7 = ((bf16[4,32,512]{2,1,0:T(8,128)(2,1)}), bf16[4,32,512]{2,1,0:T(8,128)(2,1)S(1)}, u32[]{:S(2)}, u32[]{:S(2)}) async-start(bf16[4,32,512]{2,1,0:T(8,128)(2,1)} %broadcast_in_dim.22), calls=%async_computation.7 | async-start | bytes 262144 | tf_op jit(solution)/shard_map/all_to_all | solution.py:16
  174.6 21.7 %all-to-all-done.7.parts_ref = bf16[4,32,512]{2,1,0:T(8,128)(2,1)S(1)} async-done(((bf16[4,32,512]{2,1,0:T(8,128)(2,1)}), bf16[4,32,512]{2,1,0:T(8,128)(2,1)S(1)}, u32[]{:S(2)}, u32[]{:S(2)}) %all-to-all-start.7) | async-done | bytes 131104 | tf_op jit(solution)/shard_map/all_to_all | solution.py:16
  197.3 3.4 %all-to-all-start.8 = ((bf16[4,32,1024]{2,1,0:T(8,128)(2,1)}), bf16[4,32,1024]{2,1,0:T(8,128)(2,1)S(1)}, u32[]{:S(2)}, u32[]{:S(2)}) async-start(bf16[4,32,1024]{2,1,0:T(8,128)(2,1)} %shard_map.80), calls=%async_computation.8 | async-start | bytes 524288 | tf_op jit(solution)/shard_map/all_to_all | solution.py:16
  200.8 1.3 slice.127.own_ref
  202.1 1.3 slice.128.oth_ref
  203.4 2.8 %all-to-all-done.8.parts_ref = bf16[4,32,1024]{2,1,0:T(8,128)(2,1)S(1)} async-done(((bf16[4,32,1024]{2,1,0:T(8,128)(2,1)}), bf16[4,32,1024]{2,1,0:T(8,128)(2,1)S(1)}, u32[]{:S(2)}, u32[]{:S(2)}) %all-to-all-start.8) | async-done | bytes 262176 | tf_op jit(solution)/shard_map/all_to_all | solution.py:16
  207.4 38.6 %all_to_all.60 = bf16[32,12,128]{2,1,0:T(8,128)(2,1)S(1)} all-to-all(bf16[32,12,128]{2,1,0:T(8,128)(2,1)S(1)} %reshape.216), channel_id=1, replica_groups=mesh['leaf'=4,'y'=4,'core'=2,'zhi'=4,'zlo'=8] {'zhi','zlo'}, dimensions={0} | all-to-all | bytes 196608 | tf_op jit(solution)/shard_map/all_to_all | solution.py:16
  246.9 9.5 %all-to-all-start.10 = ((bf16[8,48,128]{2,1,0:T(8,128)(2,1)}), bf16[8,48,128]{2,1,0:T(8,128)(2,1)S(1)}, u32[]{:S(2)}, u32[]{:S(2)}) async-start(bf16[8,48,128]{2,1,0:T(8,128)(2,1)} %reshape.222), calls=%async_computation.10 | async-start | bytes 196608 | tf_op jit(solution)/shard_map/all_to_all | solution.py:16
  256.4 5.0 %all-to-all-done.10 = bf16[8,48,128]{2,1,0:T(8,128)(2,1)S(1)} async-done(((bf16[8,48,128]{2,1,0:T(8,128)(2,1)}), bf16[8,48,128]{2,1,0:T(8,128)(2,1)S(1)}, u32[]{:S(2)}, u32[]{:S(2)}) %all-to-all-start.10) | async-done | bytes 98336 | tf_op jit(solution)/shard_map/all_to_all | solution.py:16
  (91 shorter events, 20.2 us)
Async XLA Ops:
  7.2 8.1 %copy-start = (bf16[1,512,512]{2,1,0:T(8,128)(2,1)S(1)}, bf16[1,512,512]{2,1,0:T(8,128)(2,1)}, u32[]{:S(2)}) copy-start(bf16[1,512,512]{2,1,0:T(8,128)(2,1)} %param.12) | copy-start | bytes 1572868
  7.2 124.5 %all-gather.3.cloned.1.call-start = ((), (), s32[]{:S(2)}) async-start(), calls=%async_computation.11 | async-start | bytes 2949120 | tf_op jit(solution)/shard_map/all_gather | solution.py:148
  7.2 1.1 copy-start.1
  8.3 0.9 copy-start.2
  9.2 0.8 copy-start.4
  10.1 5.2 %copy-start.3 = (bf16[1,128,512]{2,1,0:T(8,128)(2,1)S(1)}, bf16[1,128,512]{2,1,0:T(8,128)(2,1)}, u32[]{:S(2)}) copy-start(bf16[1,128,512]{2,1,0:T(8,128)(2,1)} %param.10) | copy-start | bytes 393220
  74.9 47.7 %all-to-all-start.3 = ((bf16[4,32,512]{2,1,0:T(8,128)(2,1)}), bf16[4,32,512]{2,1,0:T(8,128)(2,1)S(1)}, u32[]{:S(2)}, u32[]{:S(2)}) async-start(bf16[4,32,512]{2,1,0:T(8,128)(2,1)} %broadcast_in_dim.20), calls=%async_computation.3 | async-start | bytes 262144 | tf_op jit(solution)/shard_map/all_to_all | solution.py:16
  131.7 14.5 %collective-permute-start = (bf16[8,320,512]{2,1,0:T(8,128)(2,1)}, bf16[8,320,512]{2,1,0:T(8,128)(2,1)}, u32[]{:S(2)}, u32[]{:S(2)}) collective-permute-start(bf16[8,320,512]{2,1,0:T(8,128)(2,1)} %bitcast.61), channel_id=1, source_target_pairs={{0,32},{32,0},{1,33},{33,1},{2,34},{34,2},{3,35},{35,3},{4,36},{36... | collective-permute-start | bytes 7864328 | tf_op jit(solution)/shard_map/ppermute | solution.py:177
  149.5 8.1 %all-to-all-start.5 = ((bf16[4,32,512]{2,1,0:T(8,128)(2,1)}), bf16[4,32,512]{2,1,0:T(8,128)(2,1)S(1)}, u32[]{:S(2)}, u32[]{:S(2)}) async-start(bf16[4,32,512]{2,1,0:T(8,128)(2,1)} %shard_map.78), calls=%async_computation.5 | async-start | bytes 262144 | tf_op jit(solution)/shard_map/all_to_all | solution.py:16
  167.3 29.1 %all-to-all-start.7 = ((bf16[4,32,512]{2,1,0:T(8,128)(2,1)}), bf16[4,32,512]{2,1,0:T(8,128)(2,1)S(1)}, u32[]{:S(2)}, u32[]{:S(2)}) async-start(bf16[4,32,512]{2,1,0:T(8,128)(2,1)} %broadcast_in_dim.22), calls=%async_computation.7 | async-start | bytes 262144 | tf_op jit(solution)/shard_map/all_to_all | solution.py:16
  197.3 8.9 %all-to-all-start.8 = ((bf16[4,32,1024]{2,1,0:T(8,128)(2,1)}), bf16[4,32,1024]{2,1,0:T(8,128)(2,1)S(1)}, u32[]{:S(2)}, u32[]{:S(2)}) async-start(bf16[4,32,1024]{2,1,0:T(8,128)(2,1)} %shard_map.80), calls=%async_computation.8 | async-start | bytes 524288 | tf_op jit(solution)/shard_map/all_to_all | solution.py:16
  246.9 14.5 %all-to-all-start.10 = ((bf16[8,48,128]{2,1,0:T(8,128)(2,1)}), bf16[8,48,128]{2,1,0:T(8,128)(2,1)S(1)}, u32[]{:S(2)}, u32[]{:S(2)}) async-start(bf16[8,48,128]{2,1,0:T(8,128)(2,1)} %reshape.222), calls=%async_computation.10 | async-start | bytes 196608 | tf_op jit(solution)/shard_map/all_to_all | solution.py:16
Sparse Core Ops, SparseCore 0:
  11.0 111.7 all-gather.2
